TPU v7x, 32 devices: a whole 2x2x4 slice. The times are simulated.
32 devices in a mesh: dp: 16 (over z, x, core), tensor: 2 (over y).
Axes of the slice: x: 2, y: 2, z: 4, core: 2. Of those that a mesh axis runs over, the one named last changes fastest.
Arguments:
- hidden: bfloat16 [8192, 14336], P('dp', 'tensor'), may hold values from -76 to 76
- base_weight: bfloat16 [14336, 4096], P('tensor', 'dp'), may hold values from -0.046875 to 0.046875
- adapter_in: bfloat16 [256, 14336], P(None, 'tensor'), may hold values from -0.046875 to 0.046875
- adapter_out: bfloat16 [256, 4096], P(None, 'tensor'), may hold values from -0.375 to 0.375
- cotangent: bfloat16 [8192, 4096], P('dp', 'tensor'), may hold values from -0.06591797 to 0.06591797
Outputs:
- output: bfloat16 [8192, 4096], P('dp', 'tensor')
- grad_in: float32 [256, 14336], P('dp', 'tensor')
- grad_out: float32 [256, 4096], P('dp', 'tensor')
All inputs are finite; a program needn't handle non-finite values.
Results may differ from a plain program's by a relative error of at most 0.0031.
Values may be sent and summed in bfloat16 or wider, within the bound.
No kernel may reach another device: no remote copies, remote signals or barrier semaphores. Data moves between devices by JAX's collectives and lax.ppermute only.
A program may use at most 128 MiB of HBM per device.

v0:
```python
import jax
import jax.numpy as jnp
from jax import lax
from jax.sharding import PartitionSpec as P

adapter_scale = 4.0
exp_rate = 0.25
tiny_eps = 1e-06


def inverse_sinh(value):
    return jnp.log(value + jnp.sqrt(1.0 + value * value))


def shards(hidden, base_weight, adapter_in, adapter_out, cotangent):
    feature_count = hidden.shape[1] * lax.axis_size("tensor")
    contract_last = (((1,), (1,)), ((), ()))
    contract_first = (((0,), (0,)), ((), ()))
    square_part = jnp.sum(jnp.square(hidden.astype(jnp.float32)), axis=1)
    rank_part = lax.dot_general(
        hidden, adapter_in, contract_last, preferred_element_type=jnp.float32
    )
    square_sum, lorentz_raw = lax.psum((square_part, rank_part), "tensor")
    level = jnp.sqrt(square_sum / feature_count + tiny_eps)
    radius = exp_rate * level
    lift_factor = jnp.sinh(radius) / radius
    lorentz = lift_factor[:, None] * lorentz_raw
    norm_value = jnp.sqrt(jnp.sum(lorentz * lorentz, axis=1) + tiny_eps)
    phi_value = inverse_sinh(norm_value) / norm_value
    tangent = (phi_value[:, None] * lorentz).astype(jnp.bfloat16)
    partial_cols = jnp.dot(
        hidden,
        lax.all_gather(base_weight, "dp", axis=1, tiled=True),
        preferred_element_type=jnp.float32,
    )
    base_sum = lax.psum_scatter(partial_cols, "tensor", scatter_dimension=1, tiled=True)
    adapter_term = jnp.dot(tangent, adapter_out, preferred_element_type=jnp.float32)
    output = (base_sum + adapter_scale * adapter_term).astype(jnp.bfloat16)
    out_part = adapter_scale * lax.dot_general(
        tangent, cotangent, contract_first, preferred_element_type=jnp.float32
    )
    cotan_later = adapter_scale * lax.dot_general(
        cotangent, adapter_out, contract_last, preferred_element_type=jnp.float32
    )
    tangent_grad = lax.psum(cotan_later, "tensor")
    inner_value = jnp.sum(lorentz * tangent_grad, axis=1)
    coefficient = (1.0 / jnp.sqrt(1.0 + norm_value * norm_value) - phi_value) / (
        norm_value * norm_value
    )
    lorentz_grad = (
        phi_value[:, None] * tangent_grad + (coefficient * inner_value)[:, None] * lorentz
    )
    raw_grad = (lift_factor[:, None] * lorentz_grad).astype(jnp.bfloat16)
    in_part = lax.dot_general(raw_grad, hidden, contract_first, preferred_element_type=jnp.float32)
    grad_in, grad_out = (
        lax.psum_scatter(in_part, "dp", scatter_dimension=0, tiled=True),
        lax.psum_scatter(out_part, "dp", scatter_dimension=0, tiled=True),
    )
    return (output, grad_in, grad_out)


def solution(mesh):
    return jax.shard_map(
        shards,
        mesh=mesh,
        in_specs=(
            P("dp", "tensor"),
            P("tensor", "dp"),
            P(None, "tensor"),
            P(None, "tensor"),
            P("dp", "tensor"),
        ),
        out_specs=(P("dp", "tensor"), P("dp", "tensor"), P("dp", "tensor")),
        check_vma=False,
    )
```

profile of v0, /device:TPU:1, one launch (start us, length us, event | category | flops | bytes accessed | tf_op | source)
XLA Modules:
  0.0 616.1 jit_solution(16781562704618691420)
XLA Ops:
  8.0 0.0 copy-start
  8.0 0.0 all-gather.2.cloned.1.call-start
  8.1 0.7 all-gather.2.cloned.1.call-update
  8.7 0.0 all-reduce.3.cloned.1.call-start
  8.8 0.8 copy-done
  9.6 0.0 copy-start.3
  9.6 2.9 convolution_multiply_fusion.1
  12.5 0.0 copy-done.3
  12.5 6.1 fusion.10
  18.6 0.0 all-reduce.3.cloned.1.call-update
  18.6 0.0 reduce-scatter.4.cloned.1.call-start
  18.7 291.5 %all-gather.2.cloned.1.call-done = bf16[7168,4096]{1,0:T(8,128)(2,1)} async-done(((bf16[7168,256]{1,0:T(8,128)(2,1)}), bf16[7168,4096]{1,0:T(8,128)(2,1)}) %all-gather.2.cloned.1.call-update) | async-done | bytes 58720272 | tf_op jit(solution)/shard_map/all_gather | solution.py:33
  310.2 39.5 %fusion.9 = f32[512,4096]{1,0:T(8,128)} fusion(bf16[512,7168]{1,0:T(8,128)(2,1)} %param.5, bf16[7168,4096]{1,0:T(8,128)(2,1)} %all-gather.2.cloned.1.call-done), kind=kOutput, calls=%fused_computation.23 | convolution fusion | flops 30064771072 | bytes 74448896 | tf_op jit(solution)/shard_map/dot_general | solution.py:31
  349.7 0.0 reduce-scatter.4.cloned.1.call-update
  349.7 0.0 reduce-scatter.8.cloned.1.call-start
  349.8 4.6 multiply_reduce_fusion
  354.4 4.2 psum.21
  358.6 0.0 all-reduce.3.cloned.1.call-done
  358.6 0.0 copy-start.1
  358.6 0.0 copy-start.2
  358.6 1.6 multiply_reduce_fusion.1
  360.3 3.3 convolution_multiply_fusion
  363.6 0.0 reduce-scatter.8.cloned.1.call-update
  363.6 0.2 reduce-scatter.6.cloned.1.call-start
  363.9 0.0 copy-done.1
  363.9 0.0 copy-done.2
  363.9 8.3 %fusion = f32[256,7168]{1,0:T(8,128)} fusion(bf16[512,7168]{1,0:T(8,128)(2,1)} %param.5, f32[512,256]{1,0:T(8,128)S(1)} %copy-done.2, f32[512,256]{1,0:T(8,128)S(1)} %copy-done.1, f32[512]{0:T(512)S(1)} %get-tuple-element.7, f32[512]{0:T(512)S(1)} %get-tuple-element.8, f32[512]{0:T(512)S(1)} %fusion.8), kind=kOutput, calls=%fused_computation.8 | convolution fusion | flops 1879834624 | bytes 15734784 | tf_op jit(solution)/shard_map/dot_general | solution.py:54
  372.2 0.0 reduce-scatter.6.cloned.1.call-update
  372.2 75.2 %reduce-scatter.4.cloned.1.call-done = f32[512,2048]{1,0:T(8,128)} async-done(((f32[512,4096]{1,0:T(8,128)}), f32[512,2048]{1,0:T(8,128)}) %reduce-scatter.4.cloned.1.call-update) | async-done | bytes 4194320 | tf_op jit(solution)/shard_map/reduce_scatter | solution.py:36
  447.4 4.6 add_convert_fusion
  452.0 59.4 %reduce-scatter.8.cloned.1.call-done = f32[16,2048]{1,0:T(8,128)} async-done(((f32[256,2048]{1,0:T(8,128)}), f32[16,2048]{1,0:T(8,128)}) %reduce-scatter.8.cloned.1.call-update) | async-done | bytes 131088 | tf_op jit(solution)/shard_map/reduce_scatter | solution.py:57
  511.4 97.1 %reduce-scatter.6.cloned.1.call-done = f32[16,7168]{1,0:T(8,128)} async-done(((f32[256,7168]{1,0:T(8,128)}), f32[16,7168]{1,0:T(8,128)}) %reduce-scatter.6.cloned.1.call-update) | async-done | bytes 458768 | tf_op jit(solution)/shard_map/reduce_scatter | solution.py:56
  (2 shorter events, 0.1 us)
Async XLA Ops:
  8.0 1.6 copy-start
  8.0 302.1 %all-gather.2.cloned.1.call-start = ((), (), s32[]{:S(2)}) async-start(), calls=%async_computation.3 | async-start | bytes 62390272 | tf_op jit(solution)/shard_map/all_gather | solution.py:33
  8.7 349.9 %all-reduce.3.cloned.1.call-start = ((), (), s32[]{:S(2)}) async-start(), calls=%async_computation.7 | async-start | bytes 2097152 | tf_op jit(solution)/shard_map/psum | solution.py:23
  9.6 2.9 copy-start.3
  18.6 428.8 %reduce-scatter.4.cloned.1.call-start = ((), (), s32[]{:S(2)}) async-start(), calls=%async_computation.4 | async-start | bytes 12582912 | tf_op jit(solution)/shard_map/reduce_scatter | solution.py:36
  349.7 161.7 %reduce-scatter.8.cloned.1.call-start = ((), (), s32[]{:S(2)}) async-start(), calls=%async_computation.6 | async-start | bytes 2228224 | tf_op jit(solution)/shard_map/reduce_scatter | solution.py:57
  358.6 5.2 copy-start.1
  358.6 5.2 copy-start.2
  363.6 244.9 %reduce-scatter.6.cloned.1.call-start = ((), (), s32[]{:S(2)}) async-start(), calls=%async_computation.5 | async-start | bytes 7798784 | tf_op jit(solution)/shard_map/reduce_scatter | solution.py:56
Sparse Core Ops, SparseCore 0:
  10.4 299.6 all-gather.1
Sparse Core Ops, SparseCore 1:
  18.7 42.0 all-reduce.2
  349.8 97.6 reduce-scatter.3
  451.6 59.8 reduce-scatter.7
  516.5 91.9 reduce-scatter.5
where the time goes:
time: 617 us; the launch traced here: 616 us
  waiting for transfers between devices  524 us (85%)
  matrix products  64.8 us (11%)
  between operations  15.7 us (3%)
  other arithmetic  6.24 us (1%)
    all_gather x1, waiting for transfers between devices, shards(): lax.all_gather(base_weight, 'dp', axis=1, tiled=True)  291 us
    reduce_scatter x1, waiting for transfers between devices, shards(): lax.psum_scatter(in_part, 'dp', scatter_dimension=0, tiled=True)  97.1 us
    reduce_scatter x1, waiting for transfers between devices, shards(): lax.psum_scatter(partial_cols, 'tensor', scatter_dimension=1, tiled=True)  75.2 us
    reduce_scatter x1, waiting for transfers between devices, shards(): lax.psum_scatter(out_part, 'dp', scatter_dimension=0, tiled=True)  59.4 us
    dot_general x1, matrix products, shards(): jnp.dot(hidden, lax.all_gather(base_weight, 'dp', axis=1, tiled=True), pr...  39.5 us
  transfers between devices with their start and end apart: 5, of which 4 were waited for; matrix products, arithmetic and copies ran while one was open for 12% of the time, Pallas kernels for 0%

commit v1 on v0

--- a/solution.py
+++ b/solution.py
@@ -12,7 +12,7 @@
     return jnp.log(value + jnp.sqrt(1.0 + value * value))
 
 
-def shards(hidden, base_weight, adapter_in, adapter_out, cotangent):
+def plain_shards(hidden, base_weight, adapter_in, adapter_out, cotangent):
     feature_count = hidden.shape[1] * lax.axis_size("tensor")
     contract_last = (((1,), (1,)), ((), ()))
     contract_first = (((0,), (0,)), ((), ()))
@@ -59,9 +59,217 @@
     return (output, grad_in, grad_out)
 
 
+GROUP = 4
+LINE = 4
+QUARTERS = 4
+AHEAD = 2
+core_swap = [(d, d ^ 1) for d in range(LINE * GROUP)]
+x_swap = [(d, d ^ 2) for d in range(LINE * GROUP)]
+both_swap = [(d, d ^ 3) for d in range(LINE * GROUP)]
+pair_swap = [(0, 1), (1, 0)]
+
+
+def line_pairs(sources, step):
+    return [(z * GROUP + r, (z + step) * GROUP + r) for z in sources for r in range(GROUP)]
+
+
+def after(value, *others):
+    return lax.optimization_barrier((value, *others))[0]
+
+
+def pick(cases, default):
+    out = default
+    for condition, value in cases:
+        out = jnp.where(condition, value, out)
+    return out
+
+
+def dot32(a, b):
+    return jnp.dot(a, b, preferred_element_type=jnp.float32)
+
+
+def weight_streams(base_weight, z, early):
+    rows = base_weight.shape[0] // QUARTERS
+    own = [base_weight[i * rows : (i + 1) * rows] for i in range(QUARTERS)]
+    left, right = [], []
+    for s in range(3 * QUARTERS):
+        for got, sign, inner in ((left, -1, 1), (right, 1, 2)):
+            sent = own[s] if s < QUARTERS else got[s - QUARTERS]
+            if AHEAD <= s:
+                other = got[s - AHEAD] if s < 2 * QUARTERS + AHEAD else own[s - 2 * QUARTERS]
+                sent = jnp.where(jnp.logical_and(early, z == inner), other, sent)
+            hop = s // QUARTERS
+            sources = [q for q in range(LINE) if 0 <= q + sign < LINE and 0 <= q - sign * hop < LINE]
+            got.append(lax.ppermute(sent, "dp", line_pairs(sources, sign)))
+    return left, right
+
+
+def group_sum(part, x, core):
+    rows, width = part.shape
+    view = part.reshape(LINE, 2, 2, rows // (4 * LINE), width)
+    got = lax.ppermute(jnp.where(core == 0, view[:, :, 1], view[:, :, 0]), "dp", core_swap)
+    mine = jnp.where(core == 0, view[:, :, 0], view[:, :, 1]) + got
+    sent = jnp.where(x == 0, mine[:, 1], mine[:, 0]).astype(jnp.bfloat16)
+    kept = jnp.where(x == 0, mine[:, 0], mine[:, 1])
+    return kept, lax.ppermute(sent, "dp", x_swap)
+
+
+def line_sum(mine, z, holds):
+    got_left = got_right = None
+    for k in range(1, LINE):
+        send_left = lax.dynamic_index_in_dim(mine, jnp.maximum(z + k - LINE, 0), 0, False)
+        send_right = lax.dynamic_index_in_dim(mine, jnp.minimum(z + LINE - k, LINE - 1), 0, False)
+        if k > 1:
+            send_left = send_left + after(got_left, *holds[k - 1])
+            send_right = send_right + after(got_right, *holds[k - 1])
+        got_left = lax.ppermute(send_left, "dp", line_pairs(range(LINE - k, LINE), -1))
+        got_right = lax.ppermute(send_right, "dp", line_pairs(range(0, k), 1))
+    own = lax.dynamic_index_in_dim(mine, z, 0, False)
+    return own + after(got_left, *holds[LINE - 1]) + after(got_right, *holds[LINE - 1])
+
+
+def fast_shards(hidden, base_weight, adapter_in, adapter_out, cotangent):
+    feature_count = hidden.shape[1] * 2
+    tokens, depth = hidden.shape
+    columns = base_weight.shape[1]
+    contract_last = (((1,), (1,)), ((), ()))
+    contract_first = (((0,), (0,)), ((), ()))
+    place = lax.axis_index("dp")
+    z, member = place // GROUP, place % GROUP
+    x, core = member // 2, member % 2
+    y = lax.axis_index("tensor")
+    outer = jnp.logical_or(z == 0, z == LINE - 1)
+    low = z < 2
+    early = (z // 2) == y
+    late = jnp.logical_not(early)
+
+    left, right = weight_streams(base_weight, z, early)
+
+    half = tokens // 2
+    other_x0 = lax.ppermute(hidden[:half], "dp", x_swap)
+    other_core = lax.ppermute(hidden, "dp", core_swap)
+    rank_part = lax.dot_general(
+        hidden, adapter_in, contract_last, preferred_element_type=jnp.float32
+    )
+    square_part = jnp.sum(jnp.square(hidden.astype(jnp.float32)), axis=1)
+    rank_other = lax.ppermute(rank_part, "tensor", pair_swap)
+    square_other = lax.ppermute(square_part, "tensor", pair_swap)
+    cotan_part = adapter_scale * lax.dot_general(
+        cotangent, adapter_out, contract_last, preferred_element_type=jnp.float32
+    )
+    cotan_other = lax.ppermute(cotan_part, "tensor", pair_swap)
+
+    level = jnp.sqrt((square_part + square_other) / feature_count + tiny_eps)
+    radius = exp_rate * level
+    lift_factor = jnp.sinh(radius) / radius
+    lorentz = lift_factor[:, None] * (rank_part + rank_other)
+    norm_value = jnp.sqrt(jnp.sum(lorentz * lorentz, axis=1) + tiny_eps)
+    phi_value = inverse_sinh(norm_value) / norm_value
+    tangent = (phi_value[:, None] * lorentz).astype(jnp.bfloat16)
+    tangent_grad = cotan_part + cotan_other
+    inner_value = jnp.sum(lorentz * tangent_grad, axis=1)
+    coefficient = (1.0 / jnp.sqrt(1.0 + norm_value * norm_value) - phi_value) / (
+        norm_value * norm_value
+    )
+    lorentz_grad = (
+        phi_value[:, None] * tangent_grad + (coefficient * inner_value)[:, None] * lorentz
+    )
+    raw_grad = (lift_factor[:, None] * lorentz_grad).astype(jnp.bfloat16)
+    out_part = adapter_scale * lax.dot_general(
+        tangent, cotangent, contract_first, preferred_element_type=jnp.float32
+    )
+    in_part = lax.dot_general(raw_grad, hidden, contract_first, preferred_element_type=jnp.float32)
+    tangents = [tangent] + [
+        lax.ppermute(tangent, "dp", swap) for swap in (core_swap, x_swap, both_swap)
+    ]
+    in_kept, in_got = group_sum(in_part, x, core)
+    out_kept, out_got = group_sum(out_part, x, core)
+
+    other_x1 = lax.ppermute(after(hidden, other_x0, left[3], right[3])[half:], "dp", x_swap)
+    far0 = lax.ppermute(after(other_x0, left[3], right[3]), "dp", core_swap)
+    far1 = lax.ppermute(after(other_x1, left[8], right[8]), "dp", core_swap)
+
+    holds = [None] + [(left[s], right[s]) for s in (7, 8, 9)]
+    in_mine = in_kept + after(in_got, left[6], right[6]).astype(jnp.float32)
+    out_mine = out_kept + after(out_got, left[6], right[6]).astype(jnp.float32)
+    grad_in = line_sum(in_mine, z, holds)
+    grad_out = line_sum(out_mine, z, holds)
+
+    far = [jnp.where(low, a, b) for a, b in zip(left, right)]
+    near = [jnp.where(low, b, a) for a, b in zip(left[:QUARTERS], right[:QUARTERS])]
+    end_early = jnp.logical_and(outer, early)
+    end_late = jnp.logical_and(outer, late)
+    mid_late = jnp.logical_and(jnp.logical_not(outer), late)
+    first = jnp.concatenate(
+        [
+            pick([(end_early, far[2 + q]), (mid_late, near[q])], far[q])
+            for q in range(QUARTERS)
+        ]
+    )
+    second = jnp.concatenate(
+        [
+            pick([(end_early, far[6 + q]), (mid_late, far[q])], far[4 + q])
+            for q in range(QUARTERS)
+        ]
+    )
+    third = [
+        pick(
+            [
+                (end_early, far[q if q < AHEAD else 8 + q]),
+                (end_late, far[8 + q]),
+                (mid_late, far[4 + q]),
+            ],
+            near[q],
+        )
+        for q in range(QUARTERS)
+    ]
+    third_head, third_tail = jnp.concatenate(third[:3]), third[3]
+
+    pieces = [[hidden], [other_core], [other_x0, other_x1], [far0, far1]]
+    cut = third_head.shape[0]
+
+    def products(block):
+        return [jnp.concatenate([dot32(p, block) for p in ps]) for ps in pieces]
+
+    sum_own = products(base_weight)
+    sum_first = products(first)
+    sum_second = products(second)
+    sum_third = [
+        jnp.concatenate(
+            [dot32(p[:, :cut], third_head) + dot32(p[:, cut:], third_tail) for p in ps]
+        )
+        for ps in pieces
+    ]
+    flip = jnp.logical_and(late, jnp.logical_not(outer)).astype(jnp.int32)
+    parity = (z % 2) ^ flip
+
+    scale = jnp.float32(adapter_scale)
+    output = jnp.zeros((tokens, adapter_out.shape[1]), jnp.bfloat16)
+    swaps = (None, core_swap, x_swap, both_swap)
+    for turn in range(2):
+        offset = (parity ^ turn) * (GROUP * columns)
+        factor = lax.dynamic_slice_in_dim(adapter_out, offset + member * columns, columns, 1)
+        for m in (3, 2, 1, 0):
+            if turn == 0:
+                sent = jnp.where(early, sum_first[m], sum_own[m])
+                kept = jnp.where(early, sum_own[m], sum_second[m])
+            else:
+                sent = jnp.where(early, sum_second[m], sum_first[m]).astype(jnp.bfloat16)
+                kept = sum_third[m]
+            total = kept + lax.ppermute(sent, "tensor", pair_swap).astype(jnp.float32)
+            done = (total + scale * dot32(tangents[m], factor)).astype(jnp.bfloat16)
+            if m:
+                done = lax.ppermute(done, "dp", swaps[m])
+            output = lax.dynamic_update_slice(
+                output, done, (0, offset + (member ^ m) * columns)
+            )
+    return (output, grad_in, grad_out)
+
+
 def solution(mesh):
+    fits = mesh.shape["dp"] == LINE * GROUP and mesh.shape["tensor"] == 2
     return jax.shard_map(
-        shards,
+        fast_shards if fits else plain_shards,
         mesh=mesh,
         in_specs=(
             P("dp", "tensor"),

time: 617 us -> 528 us (0.86); the launches traced: 616 us -> 517 us
  waiting for transfers between devices: 524 us -> 220 us
  starting transfers between devices: 0.39 us -> 138 us
  matrix products: 64.8 us -> 106 us
  other arithmetic: 6.24 us -> 35.6 us
  local copies, waits for them, and re-layouts: 0.82 us -> 15.3 us
  between operations: 15.7 us -> 2.43 us
    all_gather x1 -> x0, waiting for transfers between devices: 291 us -> none  [shards(): lax.all_gather(base_weight, 'dp', axis=1, tiled=True)]
    reduce_scatter x3 -> x0, waiting for transfers between devices: 232 us -> none  [the longest x1 97.1 us: shards(): lax.psum_scatter(in_part, 'dp', scatter_dimension=0, tiled=True)]
    ppermute x0 -> x65, waiting for transfers between devices: none -> 220 us  [the longest x24 126 us: weight_streams(): got.append(lax.ppermute(sent, 'dp', line_pairs(sources, sign)))]
    ppermute x0 -> x65, starting transfers between devices: none -> 138 us  [the longest x6 41.9 us: line_sum(): got_right = lax.ppermute(send_right, 'dp', line_pairs(range(0, k), 1))]
    dot_general x6 -> x42, matrix products: 64.8 us -> 106 us  [the longest x38 96.3 us: dot32(): return jnp.dot(a, b, preferred_element_type=jnp.float32)]
    select_n x0 -> x20, other arithmetic: none -> 23.1 us  [the longest x6 12.6 us: pick(): out = jnp.where(condition, value, out)]
    slice x0 -> x3, local copies, waits for them, and re-layouts: none -> 9.11 us  [the longest x1 4.09 us: fast_shards(): other_x0 = lax.ppermute(hidden[:half], 'dp', x_swap)]
    add x0 -> x12, other arithmetic: none -> 8.82 us  [the longest x4 4.12 us: line_sum(): send_left = send_left + after(got_left, *holds[k - 1])]
  transfers between devices with their start and end apart: 5 -> 65, of which waited for: 4 -> 19; matrix products, arithmetic and copies ran while one was open for 12% -> 29% of each run, Pallas kernels for 0% -> 0%
where the time goes in v1:
time: 528 us; the launch traced here: 517 us
  waiting for transfers between devices  220 us (42%)
  starting transfers between devices  138 us (26%)
  matrix products  106 us (20%)
  other arithmetic  35.6 us (7%)
  local copies, waits for them, and re-layouts  15.3 us (3%)
    ppermute x24, waiting for transfers between devices, weight_streams(): got.append(lax.ppermute(sent, 'dp', line_pairs(sources, sign)))  126 us
    dot_general x38, matrix products, dot32(): return jnp.dot(a, b, preferred_element_type=jnp.float32)  96.3 us
    ppermute x1, waiting for transfers between devices, fast_shards(): lax.ppermute(after(hidden, other_x0, left[3], right[3])[half:], 'dp', x_s...  45.4 us
    ppermute x6, starting transfers between devices, line_sum(): got_right = lax.ppermute(send_right, 'dp', line_pairs(range(0, k), 1))  41.9 us
    ppermute x24, starting transfers between devices, weight_streams(): got.append(lax.ppermute(sent, 'dp', line_pairs(sources, sign)))  38.8 us
    ppermute x6, waiting for transfers between devices, fast_shards(): done = lax.ppermute(done, 'dp', swaps[m])  19.1 us
    ppermute x8, waiting for transfers between devices, fast_shards(): total = kept + lax.ppermute(sent, 'tensor', pair_swap).astype(jnp.float32)  17.2 us
    select_n x6, other arithmetic, pick(): out = jnp.where(condition, value, out)  12.6 us
  transfers between devices with their start and end apart: 65, of which 19 were waited for; matrix products, arithmetic and copies ran while one was open for 29% of the time, Pallas kernels for 0%

profile of v1, /device:TPU:1, one launch (start us, length us, event | category | flops | bytes accessed | tf_op | source)
XLA Modules:
  0.0 517.5 jit_solution(13952141486273105323)
XLA Ops:
  0.7 3.0 fusion.125
  5.2 5.6 %collective-permute-start.3 = (bf16[1792,256]{1,0:T(8,128)(2,1)}, bf16[1792,256]{1,0:T(8,128)(2,1)}, u32[]{:S(2)}, u32[]{:S(2)}) collective-permute-start(bf16[1792,256]{1,0:T(8,128)(2,1)} %get-tuple-element.63), channel_id=1, source_target_pairs={{0,8},{2,10},{4,12},{6,14},{8,16},{10,18},{12,20},{14,22},{16,24},... | collective-permute-start | bytes 2752520 | tf_op jit(solution)/shard_map/ppermute | solution.py:103
  14.7 2.9 fusion.128
  19.0 2.9 fusion.132
  21.9 4.1 slice.86
  26.0 2.3 collective-permute-start.12
  29.7 5.8 %collective-permute-done.26 = f32[512,256]{1,0:T(8,128)} collective-permute-done((f32[512,256]{1,0:T(8,128)}, f32[512,256]{1,0:T(8,128)}, u32[]{:S(2)}, u32[]{:S(2)}) %collective-permute-start.26) | collective-permute-done | bytes 524320 | tf_op jit(solution)/shard_map/ppermute | solution.py:155
  40.2 5.5 %fusion.91 = f32[256,7168]{1,0:T(8,128)S(1)} fusion(bf16[512,7168]{1,0:T(8,128)(2,1)} %param.5, f32[512,256]{1,0:T(8,128)S(1)} %get-tuple-element.49, f32[512]{0:T(512)S(1)} %get-tuple-element.88, f32[512]{0:T(512)S(1)} %get-tuple-element.89, f32[512]{0:T(512)S(1)} %fusion.118, f32[512,256]{1,0:T(8,128)S(1)} %copy-done.26, ...), kind=kOutput, calls=%fused_computation.161 | convolution fusion | flops 1879834624 | bytes 16259072 | tf_op jit(solution)/shard_map/dot_general | solution.py:181
  45.7 2.2 select_bitcast_fusion
  53.6 4.5 collective-permute-start.13
  58.4 16.4 %collective-permute-done.8 = bf16[1792,256]{1,0:T(8,128)(2,1)S(1)} collective-permute-done((bf16[1792,256]{1,0:T(8,128)(2,1)S(1)}, bf16[1792,256]{1,0:T(8,128)(2,1)S(1)}, u32[]{:S(2)}, u32[]{:S(2)}) %collective-permute-start.8) | collective-permute-done | bytes 917536 | tf_op jit(solution)/shard_map/ppermute | solution.py:103
  78.1 16.6 %collective-permute-done.4 = bf16[1792,256]{1,0:T(8,128)(2,1)S(1)} collective-permute-done((bf16[1792,256]{1,0:T(8,128)(2,1)S(1)}, bf16[1792,256]{1,0:T(8,128)(2,1)S(1)}, u32[]{:S(2)}, u32[]{:S(2)}) %collective-permute-start.4) | collective-permute-done | bytes 917536 | tf_op jit(solution)/shard_map/ppermute | solution.py:103
  97.3 3.0 collective-permute-done.2
  101.1 19.6 %collective-permute-done.9 = bf16[1792,256]{1,0:T(8,128)(2,1)S(1)} collective-permute-done((bf16[1792,256]{1,0:T(8,128)(2,1)S(1)}, bf16[1792,256]{1,0:T(8,128)(2,1)S(1)}, u32[]{:S(2)}, u32[]{:S(2)}) %collective-permute-start.9) | collective-permute-done | bytes 917536 | tf_op jit(solution)/shard_map/ppermute | solution.py:103
  125.7 19.2 %collective-permute-done.18 = bf16[1792,256]{1,0:T(8,128)(2,1)S(1)} collective-permute-done((bf16[1792,256]{1,0:T(8,128)(2,1)S(1)}, bf16[1792,256]{1,0:T(8,128)(2,1)S(1)}, u32[]{:S(2)}, u32[]{:S(2)}) %collective-permute-start.18) | collective-permute-done | bytes 917536 | tf_op jit(solution)/shard_map/ppermute | solution.py:103
  146.3 4.2 collective-permute-done.58
  151.2 13.4 %collective-permute-done.10 = bf16[1792,256]{1,0:T(8,128)(2,1)S(1)} collective-permute-done((bf16[1792,256]{1,0:T(8,128)(2,1)S(1)}, bf16[1792,256]{1,0:T(8,128)(2,1)S(1)}, u32[]{:S(2)}, u32[]{:S(2)}) %collective-permute-start.10) | collective-permute-done | bytes 917536 | tf_op jit(solution)/shard_map/ppermute | solution.py:103
  167.9 2.5 collective-permute-start.32
  171.3 15.4 %collective-permute-start.62 = (f32[16,2048]{1,0:T(8,128)}, f32[16,2048]{1,0:T(8,128)S(1)}, u32[]{:S(2)}, u32[]{:S(2)}) collective-permute-start(f32[16,2048]{1,0:T(8,128)} %get-tuple-element.87), channel_id=1, source_target_pairs={{0,8},{2,10},{4,12},{6,14},{1,9},{3,11},{5,13},{7,15}} | collective-permute-start | bytes 393224 | tf_op jit(solution)/shard_map/ppermute | solution.py:126
  188.3 5.6 %broadcast_select_fusion.15 = (bf16[1792,256]{1,0:T(8,128)(2,1)}, bf16[1792,256]{1,0:T(8,128)(2,1)}, bf16[1792,256]{1,0:T(8,128)(2,1)}, bf16[1792,256]{1,0:T(8,1...) fusion(bf16[1792,256]{1,0:T(8,128)(2,1)} %copy-done.19, pred[]{:T(512)S(6)} %and.65, ...), kind=kLoop, calls=%fused_computation.102 | loop fusion | flops 3211264 | bytes 14680066 | tf_op jit(solution)/shard_map/jit(_where)/select_n | solution.py:100
  195.2 3.1 fusion.129
  205.9 2.5 fusion.5
  208.6 26.0 %collective-permute-done.39 = bf16[1792,256]{1,0:T(8,128)(2,1)} collective-permute-done((bf16[1792,256]{1,0:T(8,128)(2,1)}, bf16[1792,256]{1,0:T(8,128)(2,1)}, u32[]{:S(2)}, u32[]{:S(2)}) %collective-permute-start.39) | collective-permute-done | bytes 917536 | tf_op jit(solution)/shard_map/ppermute | solution.py:103
  242.7 2.6 fusion.70
  245.3 9.4 %collective-permute-done.22 = bf16[1792,256]{1,0:T(8,128)(2,1)S(1)} collective-permute-done((bf16[1792,256]{1,0:T(8,128)(2,1)}, bf16[1792,256]{1,0:T(8,128)(2,1)S(1)}, u32[]{:S(2)}, u32[]{:S(2)}) %collective-permute-start.22) | collective-permute-done | bytes 917536 | tf_op jit(solution)/shard_map/ppermute | solution.py:103
  257.6 3.4 select_select_fusion.8
  261.0 2.6 fusion.75
  263.6 2.8 select_select_fusion.10
  272.3 2.2 collective-permute-done.11
  276.7 4.2 collective-permute-start.63
  284.2 2.9 broadcast_select_fusion.34
  289.2 3.2 convolution_bitcast_fusion.5
  294.3 3.1 convolution_bitcast_fusion.4
  298.7 13.9 %collective-permute-start.55 = (f32[16,7168]{1,0:T(8,128)S(1)}, f32[16,7168]{1,0:T(8,128)S(1)}, u32[]{:S(2)}, u32[]{:S(2)}) collective-permute-start(f32[16,7168]{1,0:T(8,128)S(1)} %get-tuple-element.65), channel_id=1, source_target_pairs={{0,8},{2,10},{4,12},{6,14},{8,16},{10,18},{12,20},{14,22},{1,9},{3... | collective-permute-start | bytes 1376264 | tf_op jit(solution)/shard_map/ppermute | solution.py:126
  312.6 2.8 fusion.62
  315.4 2.2 collective-permute-start.64
  319.0 4.2 collective-permute-start.56
  326.8 8.6 %collective-permute-start.5 = (bf16[256,7168]{1,0:T(8,128)(2,1)}, bf16[256,7168]{1,0:T(8,128)(2,1)}, u32[]{:S(2)}, u32[]{:S(2)}) collective-permute-start(bf16[256,7168]{1,0:T(8,128)(2,1)} %collective-permute-done), channel_id=1, source_target_pairs={{0,2},{2,0},{4,6},{6,4},{8,10},{10,8},{12,14},{14,12},{16,18},{18,... | collective-permute-start | bytes 11010056 | tf_op jit(solution)/shard_map/ppermute | solution.py:189
  336.3 5.2 %fusion.131 = f32[512,256]{1,0:T(8,128)S(1)} fusion(bf16[512,7168]{1,0:T(8,128)(2,1)} %collective-permute-done.32, bf16[7168,256]{1,0:T(8,128)(2,1)S(1)} %copy-done.5), kind=kOutput, calls=%fused_computation.222 | convolution fusion | flops 1879048192 | bytes 11534336 | tf_op jit(solution)/shard_map/dot_general | solution.py:88
  341.5 5.9 %broadcast_select_fusion.35 = (f32[512,256]{1,0:T(8,128)}, bf16[512,256]{1,0:T(8,128)(2,1)S(1)}) fusion(f32[512,256]{1,0:T(8,128)S(1)} %fusion.131, pred[]{:T(512)S(6)} %eq.18, bf16[512,7168]{1,0:T(8,128)(2,1)} %collective-permute-done.32, bf16[1792,256]{1,0:T(8,128)(2,1)S(1)} %copy-done.34, bf16[1792,256]{1,0:T(8,128)(2,1)S(1)} %get-tuple-element.78, ...), kind=kOutput, calls=%fused_computation.167 | convolution fusion | flops 1893990400 | bytes 12320769 | tf_op jit(solution)/shard_map/dot_general | solution.py:88
  347.4 5.9 %select_convert_fusion.3 = (bf16[512,256]{1,0:T(8,128)(2,1)}, f32[512,256]{1,0:T(8,128)S(1)}) fusion(bf16[512,256]{1,0:T(8,128)(2,1)S(1)} %get-tuple-element.91, pred[]{:T(512)S(6)} %eq.18, bf16[512,7168]{1,0:T(8,128)(2,1)} %collective-permute-done.32, bf16[1792,256]{1,0:T(8,128)(2,1)S(1)} %copy-done.32, bf16[1792,256]{1,0:T(8,128)(2,1)S(1)} %get-tuple-element.50, ...), kind=kOutput, calls=%fused_computation.140 | convolution fusion | flops 1893859328 | bytes 12058625 | tf_op jit(solution)/shard_map/dot_general | solution.py:88
  355.1 45.4 %collective-permute-done.6 = bf16[256,7168]{1,0:T(8,128)(2,1)} collective-permute-done((bf16[256,7168]{1,0:T(8,128)(2,1)S(1)}, bf16[256,7168]{1,0:T(8,128)(2,1)}, u32[]{:S(2)}, u32[]{:S(2)}) %collective-permute-start.6) | collective-permute-done | bytes 3670048 | tf_op jit(solution)/shard_map/ppermute | solution.py:188
  400.5 3.2 fusion.122
  403.7 3.2 fusion.119
  407.7 11.2 %collective-permute-start.17 = (bf16[256,7168]{1,0:T(8,128)(2,1)}, bf16[256,7168]{1,0:T(8,128)(2,1)}, u32[]{:S(2)}, u32[]{:S(2)}) collective-permute-start(bf16[256,7168]{1,0:T(8,128)(2,1)} %collective-permute-done.6), channel_id=1, source_target_pairs={{0,2},{2,0},{4,6},{6,4},{8,10},{10,8},{12,14},{14,12},{16,18},{18,... | collective-permute-start | bytes 11010056 | tf_op jit(solution)/shard_map/ppermute | solution.py:190
  420.4 3.2 fusion.130
  423.7 2.7 fusion.65
  428.2 2.7 fusion.53
  430.9 3.2 fusion.126
  434.2 3.4 fusion.124
  437.6 3.1 fusion.121
  440.8 2.2 fusion.14
  444.3 4.2 fusion.44
  452.3 4.1 collective-permute-done.29
  458.4 3.1 fusion.120
  461.6 3.2 fusion.127
  466.2 3.2 fusion.123
  471.3 13.1 %collective-permute-done.24 = f32[512,256]{1,0:T(8,128)S(1)} collective-permute-done((f32[512,256]{1,0:T(8,128)S(1)}, f32[512,256]{1,0:T(8,128)S(1)}, u32[]{:S(2)}, u32[]{:S(2)}) %collective-permute-start.24) | collective-permute-done | bytes 524320 | tf_op jit(solution)/shard_map/ppermute | solution.py:259
  484.7 3.0 collective-permute-start.28
  487.7 2.7 fusion.56
  491.6 3.1 collective-permute-done.28
  495.3 4.9 collective-permute-done.31
  500.3 2.2 collective-permute-start.42
  502.8 11.1 %collective-permute-done.42 = bf16[512,256]{1,0:T(8,128)(2,1)S(1)} collective-permute-done((bf16[512,256]{1,0:T(8,128)(2,1)S(1)}, bf16[512,256]{1,0:T(8,128)(2,1)S(1)}, u32[]{:S(2)}, u32[]{:S(2)}) %collective-permute-start.42) | collective-permute-done | bytes 262176 | tf_op jit(solution)/shard_map/ppermute | solution.py:262
  (256 shorter events, 102.4 us)
Async XLA Ops:
  3.6 46.4 %collective-permute-start.1 = (bf16[1792,256]{1,0:T(8,128)(2,1)}, bf16[1792,256]{1,0:T(8,128)(2,1)S(1)}, u32[]{:S(2)}, u32[]{:S(2)}) collective-permute-start(bf16[1792,256]{1,0:T(8,128)(2,1)} %get-tuple-element.63), channel_id=1, source_target_pairs={{8,0},{10,2},{12,4},{14,6},{16,8},{18,10},{20,12},{22,14},{24,16},... | collective-permute-start | bytes 2752520 | tf_op jit(solution)/shard_map/ppermute | solution.py:103
  5.2 46.6 %collective-permute-start.3 = (bf16[1792,256]{1,0:T(8,128)(2,1)}, bf16[1792,256]{1,0:T(8,128)(2,1)}, u32[]{:S(2)}, u32[]{:S(2)}) collective-permute-start(bf16[1792,256]{1,0:T(8,128)(2,1)} %get-tuple-element.63), channel_id=1, source_target_pairs={{0,8},{2,10},{4,12},{6,14},{8,16},{10,18},{12,20},{14,22},{16,24},... | collective-permute-start | bytes 2752520 | tf_op jit(solution)/shard_map/ppermute | solution.py:103
  11.6 16.8 %collective-permute-start.48 = (f32[512,256]{1,0:T(8,128)S(1)}, f32[512,256]{1,0:T(8,128)}, u32[]{:S(2)}, u32[]{:S(2)}) collective-permute-start(f32[512,256]{1,0:T(8,128)S(1)} %convolution_multiply_fusion.1), channel_id=1, source_target_pairs={{0,1},{1,0},{2,3},{3,2},{4,5},{5,4},{6,7},{7,6},{8,9},{9,8},{10,11... | collective-permute-start | bytes 1572872 | tf_op jit(solution)/shard_map/ppermute | solution.py:160
  14.5 11.4 %collective-permute-start.25 = (f32[512]{0:T(512)S(1)}, f32[512]{0:T(512)S(1)}, u32[]{:S(2)}, u32[]{:S(2)}) collective-permute-start(f32[512]{0:T(512)S(1)} %multiply_reduce_fusion), channel_id=1, source_target_pairs={{0,1},{1,0},{2,3},{3,2},{4,5},{5,4},{6,7},{7,6},{8,9},{9,8},{10,11... | collective-permute-start | bytes 6152 | tf_op jit(solution)/shard_map/ppermute | solution.py:156
  17.6 17.9 %collective-permute-start.26 = (f32[512,256]{1,0:T(8,128)}, f32[512,256]{1,0:T(8,128)}, u32[]{:S(2)}, u32[]{:S(2)}) collective-permute-start(f32[512,256]{1,0:T(8,128)} %fusion.128), channel_id=1, source_target_pairs={{0,1},{1,0},{2,3},{3,2},{4,5},{5,4},{6,7},{7,6},{8,9},{9,8},{10,11... | collective-permute-start | bytes 1572872 | tf_op jit(solution)/shard_map/ppermute | solution.py:155
  26.0 25.5 %collective-permute-start.12 = (bf16[1792,256]{1,0:T(8,128)(2,1)}, bf16[1792,256]{1,0:T(8,128)(2,1)S(1)}, u32[]{:S(2)}, u32[]{:S(2)}) collective-permute-start(bf16[1792,256]{1,0:T(8,128)(2,1)} %get-tuple-element.62), channel_id=1, source_target_pairs={{0,8},{2,10},{4,12},{6,14},{8,16},{10,18},{12,20},{14,22},{16,24},... | collective-permute-start | bytes 2752520 | tf_op jit(solution)/shard_map/ppermute | solution.py:103
  28.4 23.6 %collective-permute-start.7 = (bf16[1792,256]{1,0:T(8,128)(2,1)}, bf16[1792,256]{1,0:T(8,128)(2,1)S(1)}, u32[]{:S(2)}, u32[]{:S(2)}) collective-permute-start(bf16[1792,256]{1,0:T(8,128)(2,1)} %get-tuple-element.62), channel_id=1, source_target_pairs={{8,0},{10,2},{12,4},{14,6},{16,8},{18,10},{20,12},{22,14},{24,16},... | collective-permute-start | bytes 2752520 | tf_op jit(solution)/shard_map/ppermute | solution.py:103
  38.2 15.4 %collective-permute-start.57 = (f32[4,2,16,2048]{3,2,1,0:T(8,128)S(1)}, f32[4,2,16,2048]{3,2,1,0:T(8,128)S(1)}, u32[]{:S(2)}, u32[]{:S(2)}) collective-permute-start(f32[4,2,16,2048]{3,2,1,0:T(8,128)S(1)} %select_bitcast_fusion.1), channel_id=1, source_target_pairs={{0,2},{2,0},{4,6},{6,4},{8,10},{10,8},{12,14},{14,12},{16,18},{18,... | collective-permute-start | bytes 3145736 | tf_op jit(solution)/shard_map/ppermute | solution.py:110
  50.1 143.8 %collective-permute-start = (bf16[256,7168]{1,0:T(8,128)(2,1)}, bf16[256,7168]{1,0:T(8,128)(2,1)}, u32[]{:S(2)}, u32[]{:S(2)}) collective-permute-start(bf16[256,7168]{1,0:T(8,128)(2,1)} %slice.86), channel_id=1, source_target_pairs={{0,4},{2,6},{4,0},{6,2},{8,12},{10,14},{12,8},{14,10},{16,20},{18,... | collective-permute-start | bytes 11010056 | tf_op jit(solution)/shard_map/ppermute | solution.py:149
  51.5 72.1 %collective-permute-start.34 = (bf16[512,256]{1,0:T(8,128)(2,1)S(1)}, bf16[512,256]{1,0:T(8,128)(2,1)S(1)}, u32[]{:S(2)}, u32[]{:S(2)}) collective-permute-start(bf16[512,256]{1,0:T(8,128)(2,1)S(1)} %multiply_convert_fusion.1), channel_id=1, source_target_pairs={{0,2},{2,0},{4,6},{6,4},{8,10},{10,8},{12,14},{14,12},{16,18},{18,... | collective-permute-start | bytes 786440 | tf_op jit(solution)/shard_map/ppermute | solution.py:183
  51.8 152.4 %collective-permute-start.49 = (f32[4,2,16,7168]{3,2,1,0:T(8,128)}, f32[4,2,16,7168]{3,2,1,0:T(8,128)}, u32[]{:S(2)}, u32[]{:S(2)}) collective-permute-start(f32[4,2,16,7168]{3,2,1,0:T(8,128)} %select_bitcast_fusion), channel_id=1, source_target_pairs={{0,2},{2,0},{4,6},{6,4},{8,10},{10,8},{12,14},{14,12},{16,18},{18,... | collective-permute-start | bytes 11010056 | tf_op jit(solution)/shard_map/ppermute | solution.py:110
  52.3 22.6 %collective-permute-start.8 = (bf16[1792,256]{1,0:T(8,128)(2,1)S(1)}, bf16[1792,256]{1,0:T(8,128)(2,1)S(1)}, u32[]{:S(2)}, u32[]{:S(2)}) collective-permute-start(bf16[1792,256]{1,0:T(8,128)(2,1)S(1)} %get-tuple-element.59), channel_id=1, source_target_pairs={{8,0},{10,2},{12,4},{14,6},{16,8},{18,10},{20,12},{22,14},{24,16},... | collective-permute-start | bytes 2752520 | tf_op jit(solution)/shard_map/ppermute | solution.py:103
  53.6 23.1 %collective-permute-start.13 = (bf16[1792,256]{1,0:T(8,128)(2,1)S(1)}, bf16[1792,256]{1,0:T(8,128)(2,1)S(1)}, u32[]{:S(2)}, u32[]{:S(2)}) collective-permute-start(bf16[1792,256]{1,0:T(8,128)(2,1)S(1)} %get-tuple-element.58), channel_id=1, source_target_pairs={{0,8},{2,10},{4,12},{6,14},{8,16},{10,18},{12,20},{14,22},{16,24},... | collective-permute-start | bytes 2752520 | tf_op jit(solution)/shard_map/ppermute | solution.py:103
  74.8 19.9 %collective-permute-start.4 = (bf16[1792,256]{1,0:T(8,128)(2,1)S(1)}, bf16[1792,256]{1,0:T(8,128)(2,1)S(1)}, u32[]{:S(2)}, u32[]{:S(2)}) collective-permute-start(bf16[1792,256]{1,0:T(8,128)(2,1)S(1)} %get-tuple-element.61), channel_id=1, source_target_pairs={{0,8},{2,10},{4,12},{6,14},{8,16},{10,18},{12,20},{14,22},{16,24},... | collective-permute-start | bytes 2752520 | tf_op jit(solution)/shard_map/ppermute | solution.py:103
  76.7 23.6 %collective-permute-start.2 = (bf16[1792,256]{1,0:T(8,128)(2,1)S(1)}, bf16[1792,256]{1,0:T(8,128)(2,1)S(1)}, u32[]{:S(2)}, u32[]{:S(2)}) collective-permute-start(bf16[1792,256]{1,0:T(8,128)(2,1)S(1)} %get-tuple-element.60), channel_id=1, source_target_pairs={{8,0},{10,2},{12,4},{14,6},{16,8},{18,10},{20,12},{22,14},{24,16},... | collective-permute-start | bytes 2752520 | tf_op jit(solution)/shard_map/ppermute | solution.py:103
  94.7 26.0 %collective-permute-start.9 = (bf16[1792,256]{1,0:T(8,128)(2,1)S(1)}, bf16[1792,256]{1,0:T(8,128)(2,1)S(1)}, u32[]{:S(2)}, u32[]{:S(2)}) collective-permute-start(bf16[1792,256]{1,0:T(8,128)(2,1)S(1)} %broadcast_select_fusion.31), channel_id=1, source_target_pairs={{8,0},{10,2},{12,4},{14,6},{16,8},{18,10},{20,12},{22,14},{9,1},{1... | collective-permute-start | bytes 2752520 | tf_op jit(solution)/shard_map/ppermute | solution.py:103
  100.3 21.5 %collective-permute-start.14 = (bf16[1792,256]{1,0:T(8,128)(2,1)S(1)}, bf16[1792,256]{1,0:T(8,128)(2,1)S(1)}, u32[]{:S(2)}, u32[]{:S(2)}) collective-permute-start(bf16[1792,256]{1,0:T(8,128)(2,1)S(1)} %broadcast_select_fusion.21), channel_id=1, source_target_pairs={{8,16},{10,18},{12,20},{14,22},{16,24},{18,26},{20,28},{22,30},{9,... | collective-permute-start | bytes 2752520 | tf_op jit(solution)/shard_map/ppermute | solution.py:103
  120.7 4.1 collective-permute-start.20
  121.8 23.1 %collective-permute-start.18 = (bf16[1792,256]{1,0:T(8,128)(2,1)S(1)}, bf16[1792,256]{1,0:T(8,128)(2,1)S(1)}, u32[]{:S(2)}, u32[]{:S(2)}) collective-permute-start(bf16[1792,256]{1,0:T(8,128)(2,1)S(1)} %broadcast_select_fusion.28), channel_id=1, source_target_pairs={{8,0},{10,2},{12,4},{14,6},{16,8},{18,10},{20,12},{22,14},{9,1},{1... | collective-permute-start | bytes 2752520 | tf_op jit(solution)/shard_map/ppermute | solution.py:103
  123.6 41.1 %collective-permute-start.10 = (bf16[1792,256]{1,0:T(8,128)(2,1)S(1)}, bf16[1792,256]{1,0:T(8,128)(2,1)S(1)}, u32[]{:S(2)}, u32[]{:S(2)}) collective-permute-start(bf16[1792,256]{1,0:T(8,128)(2,1)S(1)} %broadcast_select_fusion.30), channel_id=1, source_target_pairs={{8,0},{10,2},{12,4},{14,6},{16,8},{18,10},{20,12},{22,14},{9,1},{1... | collective-permute-start | bytes 2752520 | tf_op jit(solution)/shard_map/ppermute | solution.py:103
  124.9 43.0 %collective-permute-start.15 = (bf16[1792,256]{1,0:T(8,128)(2,1)S(1)}, bf16[1792,256]{1,0:T(8,128)(2,1)S(1)}, u32[]{:S(2)}, u32[]{:S(2)}) collective-permute-start(bf16[1792,256]{1,0:T(8,128)(2,1)S(1)} %broadcast_select_fusion.20), channel_id=1, source_target_pairs={{8,16},{10,18},{12,20},{14,22},{16,24},{18,26},{20,28},{22,30},{9,... | collective-permute-start | bytes 2752520 | tf_op jit(solution)/shard_map/ppermute | solution.py:103
  144.9 5.5 %collective-permute-start.58 = (bf16[4,16,2048]{2,1,0:T(8,128)(2,1)S(1)}, bf16[4,16,2048]{2,1,0:T(8,128)(2,1)S(1)}, u32[]{:S(2)}, u32[]{:S(2)}) collective-permute-start(bf16[4,16,2048]{2,1,0:T(8,128)(2,1)S(1)} %fusion.92), channel_id=1, source_target_pairs={{0,4},{2,6},{4,0},{6,2},{8,12},{10,14},{12,8},{14,10},{16,20},{18,... | collective-permute-start | bytes 786440 | tf_op jit(solution)/shard_map/ppermute | solution.py:114
  150.5 20.7 %collective-permute-start.21 = (bf16[1792,256]{1,0:T(8,128)(2,1)S(1)}, bf16[1792,256]{1,0:T(8,128)(2,1)S(1)}, u32[]{:S(2)}, u32[]{:S(2)}) collective-permute-start(bf16[1792,256]{1,0:T(8,128)(2,1)S(1)} %broadcast_select_fusion.17), channel_id=1, source_target_pairs={{8,16},{10,18},{12,20},{14,22},{16,24},{18,26},{20,28},{22,30},{9,... | collective-permute-start | bytes 2752520 | tf_op jit(solution)/shard_map/ppermute | solution.py:103
  164.6 22.0 %collective-permute-start.19 = (bf16[1792,256]{1,0:T(8,128)(2,1)S(1)}, bf16[1792,256]{1,0:T(8,128)(2,1)S(1)}, u32[]{:S(2)}, u32[]{:S(2)}) collective-permute-start(bf16[1792,256]{1,0:T(8,128)(2,1)S(1)} %broadcast_select_fusion.27), channel_id=1, source_target_pairs={{8,0},{10,2},{12,4},{14,6},{16,8},{18,10},{20,12},{22,14},{9,1},{1... | collective-permute-start | bytes 2752520 | tf_op jit(solution)/shard_map/ppermute | solution.py:103
  167.9 168.4 %collective-permute-start.32 = (bf16[512,7168]{1,0:T(8,128)(2,1)S(1)}, bf16[512,7168]{1,0:T(8,128)(2,1)}, u32[]{:S(2)}, u32[]{:S(2)}) collective-permute-start(bf16[512,7168]{1,0:T(8,128)(2,1)S(1)} %bitcast.188), channel_id=1, source_target_pairs={{0,2},{2,0},{4,6},{6,4},{8,10},{10,8},{12,14},{14,12},{16,18},{18,... | collective-permute-start | bytes 22020104 | tf_op jit(solution)/shard_map/ppermute | solution.py:150
  171.3 29.1 %collective-permute-start.62 = (f32[16,2048]{1,0:T(8,128)}, f32[16,2048]{1,0:T(8,128)S(1)}, u32[]{:S(2)}, u32[]{:S(2)}) collective-permute-start(f32[16,2048]{1,0:T(8,128)} %get-tuple-element.87), channel_id=1, source_target_pairs={{0,8},{2,10},{4,12},{6,14},{1,9},{3,11},{5,13},{7,15}} | collective-permute-start | bytes 393224 | tf_op jit(solution)/shard_map/ppermute | solution.py:126
  187.6 14.3 %collective-permute-start.59 = (f32[16,2048]{1,0:T(8,128)S(1)}, f32[16,2048]{1,0:T(8,128)S(1)}, u32[]{:S(2)}, u32[]{:S(2)}) collective-permute-start(f32[16,2048]{1,0:T(8,128)S(1)} %get-tuple-element.86), channel_id=1, source_target_pairs={{24,16},{26,18},{28,20},{30,22},{25,17},{27,19},{29,21},{31,23}} | collective-permute-start | bytes 393224 | tf_op jit(solution)/shard_map/ppermute | solution.py:125
  193.9 46.1 %collective-permute-start.37 = (bf16[1792,256]{1,0:T(8,128)(2,1)}, bf16[1792,256]{1,0:T(8,128)(2,1)}, u32[]{:S(2)}, u32[]{:S(2)}) collective-permute-start(bf16[1792,256]{1,0:T(8,128)(2,1)} %get-tuple-element.56), channel_id=1, source_target_pairs={{8,0},{10,2},{12,4},{14,6},{9,1},{11,3},{13,5},{15,7}} | collective-permute-start | bytes 2752520 | tf_op jit(solution)/shard_map/ppermute | solution.py:103
  200.4 41.0 %collective-permute-start.38 = (bf16[1792,256]{1,0:T(8,128)(2,1)}, bf16[1792,256]{1,0:T(8,128)(2,1)}, u32[]{:S(2)}, u32[]{:S(2)}) collective-permute-start(bf16[1792,256]{1,0:T(8,128)(2,1)} %get-tuple-element.54), channel_id=1, source_target_pairs={{16,24},{18,26},{20,28},{22,30},{17,25},{19,27},{21,29},{23,31}} | collective-permute-start | bytes 2752520 | tf_op jit(solution)/shard_map/ppermute | solution.py:103
  202.0 32.7 %collective-permute-start.39 = (bf16[1792,256]{1,0:T(8,128)(2,1)}, bf16[1792,256]{1,0:T(8,128)(2,1)}, u32[]{:S(2)}, u32[]{:S(2)}) collective-permute-start(bf16[1792,256]{1,0:T(8,128)(2,1)} %get-tuple-element.55), channel_id=1, source_target_pairs={{8,0},{10,2},{12,4},{14,6},{9,1},{11,3},{13,5},{15,7}} | collective-permute-start | bytes 2752520 | tf_op jit(solution)/shard_map/ppermute | solution.py:103
  204.2 31.7 %collective-permute-start.40 = (bf16[1792,256]{1,0:T(8,128)(2,1)}, bf16[1792,256]{1,0:T(8,128)(2,1)}, u32[]{:S(2)}, u32[]{:S(2)}) collective-permute-start(bf16[1792,256]{1,0:T(8,128)(2,1)} %get-tuple-element.57), channel_id=1, source_target_pairs={{16,24},{18,26},{20,28},{22,30},{17,25},{19,27},{21,29},{23,31}} | collective-permute-start | bytes 2752520 | tf_op jit(solution)/shard_map/ppermute | solution.py:103
  234.6 20.1 %collective-permute-start.22 = (bf16[1792,256]{1,0:T(8,128)(2,1)}, bf16[1792,256]{1,0:T(8,128)(2,1)S(1)}, u32[]{:S(2)}, u32[]{:S(2)}) collective-permute-start(bf16[1792,256]{1,0:T(8,128)(2,1)} %get-tuple-element.76), channel_id=1, source_target_pairs={{8,0},{10,2},{12,4},{14,6},{9,1},{11,3},{13,5},{15,7}} | collective-permute-start | bytes 2752520 | tf_op jit(solution)/shard_map/ppermute | solution.py:103
  235.9 20.0 %collective-permute-start.23 = (bf16[1792,256]{1,0:T(8,128)(2,1)}, bf16[1792,256]{1,0:T(8,128)(2,1)S(1)}, u32[]{:S(2)}, u32[]{:S(2)}) collective-permute-start(bf16[1792,256]{1,0:T(8,128)(2,1)} %get-tuple-element.74), channel_id=1, source_target_pairs={{16,24},{18,26},{20,28},{22,30},{17,25},{19,27},{21,29},{23,31}} | collective-permute-start | bytes 2752520 | tf_op jit(solution)/shard_map/ppermute | solution.py:103
  239.9 34.5 %collective-permute-start.11 = (bf16[1792,256]{1,0:T(8,128)(2,1)}, bf16[1792,256]{1,0:T(8,128)(2,1)}, u32[]{:S(2)}, u32[]{:S(2)}) collective-permute-start(bf16[1792,256]{1,0:T(8,128)(2,1)} %get-tuple-element.75), channel_id=1, source_target_pairs={{8,0},{10,2},{12,4},{14,6},{9,1},{11,3},{13,5},{15,7}} | collective-permute-start | bytes 2752520 | tf_op jit(solution)/shard_map/ppermute | solution.py:103
  241.4 29.5 %collective-permute-start.60 = (f32[16,2048]{1,0:T(8,128)S(1)}, f32[16,2048]{1,0:T(8,128)}, u32[]{:S(2)}, u32[]{:S(2)}) collective-permute-start(f32[16,2048]{1,0:T(8,128)S(1)} %bitcast_add_fusion.7), channel_id=1, source_target_pairs={{16,8},{18,10},{20,12},{22,14},{24,16},{26,18},{28,20},{30,22},{17... | collective-permute-start | bytes 393224 | tf_op jit(solution)/shard_map/ppermute | solution.py:125
  254.7 12.8 %collective-permute-start.50 = (bf16[4,16,7168]{2,1,0:T(8,128)(2,1)S(1)}, bf16[4,16,7168]{2,1,0:T(8,128)(2,1)S(1)}, u32[]{:S(2)}, u32[]{:S(2)}) collective-permute-start(bf16[4,16,7168]{2,1,0:T(8,128)(2,1)S(1)} %fusion.72), channel_id=1, source_target_pairs={{0,4},{2,6},{4,0},{6,2},{8,12},{10,14},{12,8},{14,10},{16,20},{18,... | collective-permute-start | bytes 2752520 | tf_op jit(solution)/shard_map/ppermute | solution.py:114
  256.0 18.5 %collective-permute-start.16 = (bf16[1792,256]{1,0:T(8,128)(2,1)}, bf16[1792,256]{1,0:T(8,128)(2,1)}, u32[]{:S(2)}, u32[]{:S(2)}) collective-permute-start(bf16[1792,256]{1,0:T(8,128)(2,1)} %get-tuple-element.83), channel_id=1, source_target_pairs={{16,24},{18,26},{20,28},{22,30},{17,25},{19,27},{21,29},{23,31}} | collective-permute-start | bytes 2752520 | tf_op jit(solution)/shard_map/ppermute | solution.py:103
  268.8 28.7 %collective-permute-start.54 = (f32[16,7168]{1,0:T(8,128)}, f32[16,7168]{1,0:T(8,128)}, u32[]{:S(2)}, u32[]{:S(2)}) collective-permute-start(f32[16,7168]{1,0:T(8,128)} %get-tuple-element.67), channel_id=1, source_target_pairs={{0,8},{2,10},{4,12},{6,14},{1,9},{3,11},{5,13},{7,15}} | collective-permute-start | bytes 1376264 | tf_op jit(solution)/shard_map/ppermute | solution.py:126
  270.9 21.5 %collective-permute-start.51 = (f32[16,7168]{1,0:T(8,128)}, f32[16,7168]{1,0:T(8,128)}, u32[]{:S(2)}, u32[]{:S(2)}) collective-permute-start(f32[16,7168]{1,0:T(8,128)} %get-tuple-element.66), channel_id=1, source_target_pairs={{24,16},{26,18},{28,20},{30,22},{25,17},{27,19},{29,21},{31,23}} | collective-permute-start | bytes 1376264 | tf_op jit(solution)/shard_map/ppermute | solution.py:125
  275.4 47.8 %collective-permute-start.61 = (f32[16,2048]{1,0:T(8,128)S(1)}, f32[16,2048]{1,0:T(8,128)S(1)}, u32[]{:S(2)}, u32[]{:S(2)}) collective-permute-start(f32[16,2048]{1,0:T(8,128)S(1)} %get-tuple-element.84), channel_id=1, source_target_pairs={{8,0},{10,2},{12,4},{14,6},{16,8},{18,10},{20,12},{22,14},{24,16},... | collective-permute-start | bytes 393224 | tf_op jit(solution)/shard_map/ppermute | solution.py:125
  276.7 38.7 %collective-permute-start.63 = (f32[16,2048]{1,0:T(8,128)S(1)}, f32[16,2048]{1,0:T(8,128)S(1)}, u32[]{:S(2)}, u32[]{:S(2)}) collective-permute-start(f32[16,2048]{1,0:T(8,128)S(1)} %get-tuple-element.85), channel_id=1, source_target_pairs={{0,8},{2,10},{4,12},{6,14},{8,16},{10,18},{12,20},{14,22},{1,9},{3... | collective-permute-start | bytes 393224 | tf_op jit(solution)/shard_map/ppermute | solution.py:126
  298.7 20.2 %collective-permute-start.55 = (f32[16,7168]{1,0:T(8,128)S(1)}, f32[16,7168]{1,0:T(8,128)S(1)}, u32[]{:S(2)}, u32[]{:S(2)}) collective-permute-start(f32[16,7168]{1,0:T(8,128)S(1)} %get-tuple-element.65), channel_id=1, source_target_pairs={{0,8},{2,10},{4,12},{6,14},{8,16},{10,18},{12,20},{14,22},{1,9},{3... | collective-permute-start | bytes 1376264 | tf_op jit(solution)/shard_map/ppermute | solution.py:126
  315.4 9.1 %collective-permute-start.64 = (f32[16,2048]{1,0:T(8,128)S(1)}, f32[16,2048]{1,0:T(8,128)S(1)}, u32[]{:S(2)}, u32[]{:S(2)}) collective-permute-start(f32[16,2048]{1,0:T(8,128)S(1)} %bitcast_add_fusion.6), channel_id=1, source_target_pairs={{0,8},{2,10},{4,12},{6,14},{8,16},{10,18},{12,20},{14,22},{16,24},... | collective-permute-start | bytes 393224 | tf_op jit(solution)/shard_map/ppermute | solution.py:126
  317.6 9.2 %collective-permute-start.53 = (f32[16,7168]{1,0:T(8,128)S(1)}, f32[16,7168]{1,0:T(8,128)S(1)}, u32[]{:S(2)}, u32[]{:S(2)}) collective-permute-start(f32[16,7168]{1,0:T(8,128)S(1)} %get-tuple-element.64), channel_id=1, source_target_pairs={{8,0},{10,2},{12,4},{14,6},{16,8},{18,10},{20,12},{22,14},{24,16},... | collective-permute-start | bytes 1376264 | tf_op jit(solution)/shard_map/ppermute | solution.py:125
  319.0 16.4 %collective-permute-start.56 = (f32[16,7168]{1,0:T(8,128)S(1)}, f32[16,7168]{1,0:T(8,128)S(1)}, u32[]{:S(2)}, u32[]{:S(2)}) collective-permute-start(f32[16,7168]{1,0:T(8,128)S(1)} %bitcast_add_fusion.1), channel_id=1, source_target_pairs={{0,8},{2,10},{4,12},{6,14},{8,16},{10,18},{12,20},{14,22},{16,24},... | collective-permute-start | bytes 1376264 | tf_op jit(solution)/shard_map/ppermute | solution.py:126
  323.2 125.3 %collective-permute-start.30 = (bf16[512,256]{1,0:T(8,128)(2,1)S(1)}, bf16[512,256]{1,0:T(8,128)(2,1)S(1)}, u32[]{:S(2)}, u32[]{:S(2)}) collective-permute-start(bf16[512,256]{1,0:T(8,128)(2,1)S(1)} %multiply_convert_fusion.1), channel_id=1, source_target_pairs={{0,4},{2,6},{4,0},{6,2},{8,12},{10,14},{12,8},{14,10},{16,20},{18,... | collective-permute-start | bytes 786440 | tf_op jit(solution)/shard_map/ppermute | solution.py:183
  324.6 75.9 %collective-permute-start.6 = (bf16[256,7168]{1,0:T(8,128)(2,1)S(1)}, bf16[256,7168]{1,0:T(8,128)(2,1)}, u32[]{:S(2)}, u32[]{:S(2)}) collective-permute-start(bf16[256,7168]{1,0:T(8,128)(2,1)S(1)} %copy-done.16), channel_id=1, source_target_pairs={{0,4},{2,6},{4,0},{6,2},{8,12},{10,14},{12,8},{14,10},{16,20},{18,... | collective-permute-start | bytes 11010056 | tf_op jit(solution)/shard_map/ppermute | solution.py:188
  326.8 99.5 %collective-permute-start.5 = (bf16[256,7168]{1,0:T(8,128)(2,1)}, bf16[256,7168]{1,0:T(8,128)(2,1)}, u32[]{:S(2)}, u32[]{:S(2)}) collective-permute-start(bf16[256,7168]{1,0:T(8,128)(2,1)} %collective-permute-done), channel_id=1, source_target_pairs={{0,2},{2,0},{4,6},{6,4},{8,10},{10,8},{12,14},{14,12},{16,18},{18,... | collective-permute-start | bytes 11010056 | tf_op jit(solution)/shard_map/ppermute | solution.py:189
  353.3 89.7 %collective-permute-start.45 = (bf16[512,256]{1,0:T(8,128)(2,1)}, bf16[512,256]{1,0:T(8,128)(2,1)S(1)}, u32[]{:S(2)}, u32[]{:S(2)}) collective-permute-start(bf16[512,256]{1,0:T(8,128)(2,1)} %get-tuple-element.94), channel_id=1, source_target_pairs={{0,1},{1,0},{2,3},{3,2},{4,5},{5,4},{6,7},{7,6},{8,9},{9,8},{10,11... | collective-permute-start | bytes 786440 | tf_op jit(solution)/shard_map/ppermute | solution.py:259
  407.0 43.3 %collective-permute-start.43 = (bf16[512,256]{1,0:T(8,128)(2,1)S(1)}, bf16[512,256]{1,0:T(8,128)(2,1)S(1)}, u32[]{:S(2)}, u32[]{:S(2)}) collective-permute-start(bf16[512,256]{1,0:T(8,128)(2,1)S(1)} %select_convert_fusion.4), channel_id=1, source_target_pairs={{0,1},{1,0},{2,3},{3,2},{4,5},{5,4},{6,7},{7,6},{8,9},{9,8},{10,11... | collective-permute-start | bytes 786440 | tf_op jit(solution)/shard_map/ppermute | solution.py:259
  407.7 50.7 %collective-permute-start.17 = (bf16[256,7168]{1,0:T(8,128)(2,1)}, bf16[256,7168]{1,0:T(8,128)(2,1)}, u32[]{:S(2)}, u32[]{:S(2)}) collective-permute-start(bf16[256,7168]{1,0:T(8,128)(2,1)} %collective-permute-done.6), channel_id=1, source_target_pairs={{0,2},{2,0},{4,6},{6,4},{8,10},{10,8},{12,14},{14,12},{16,18},{18,... | collective-permute-start | bytes 11010056 | tf_op jit(solution)/shard_map/ppermute | solution.py:190
  426.3 24.4 %collective-permute-start.33 = (f32[512,256]{1,0:T(8,128)}, f32[512,256]{1,0:T(8,128)S(1)}, u32[]{:S(2)}, u32[]{:S(2)}) collective-permute-start(f32[512,256]{1,0:T(8,128)} %get-tuple-element.90), channel_id=1, source_target_pairs={{0,1},{1,0},{2,3},{3,2},{4,5},{5,4},{6,7},{7,6},{8,9},{9,8},{10,11... | collective-permute-start | bytes 1572872 | tf_op jit(solution)/shard_map/ppermute | solution.py:259
  443.0 13.3 %collective-permute-start.29 = (f32[512,256]{1,0:T(8,128)S(1)}, f32[512,256]{1,0:T(8,128)S(1)}, u32[]{:S(2)}, u32[]{:S(2)}) collective-permute-start(f32[512,256]{1,0:T(8,128)S(1)} %fusion.88), channel_id=1, source_target_pairs={{0,1},{1,0},{2,3},{3,2},{4,5},{5,4},{6,7},{7,6},{8,9},{9,8},{10,11... | collective-permute-start | bytes 1572872 | tf_op jit(solution)/shard_map/ppermute | solution.py:259
  448.5 22.5 %collective-permute-start.27 = (bf16[512,256]{1,0:T(8,128)(2,1)S(1)}, bf16[512,256]{1,0:T(8,128)(2,1)S(1)}, u32[]{:S(2)}, u32[]{:S(2)}) collective-permute-start(bf16[512,256]{1,0:T(8,128)(2,1)S(1)} %multiply_convert_fusion.1), channel_id=1, source_target_pairs={{0,6},{2,4},{4,2},{6,0},{8,14},{10,12},{12,10},{14,8},{16,22},{18,... | collective-permute-start | bytes 786440 | tf_op jit(solution)/shard_map/ppermute | solution.py:183
  450.3 52.3 %collective-permute-start.36 = (f32[512,256]{1,0:T(8,128)S(1)}, f32[512,256]{1,0:T(8,128)S(1)}, u32[]{:S(2)}, u32[]{:S(2)}) collective-permute-start(f32[512,256]{1,0:T(8,128)S(1)} %copy-done.42), channel_id=1, source_target_pairs={{0,1},{1,0},{2,3},{3,2},{4,5},{5,4},{6,7},{7,6},{8,9},{9,8},{10,11... | collective-permute-start | bytes 1572872 | tf_op jit(solution)/shard_map/ppermute | solution.py:259
  450.8 63.2 %collective-permute-start.47 = (bf16[512,256]{1,0:T(8,128)(2,1)S(1)}, bf16[512,256]{1,0:T(8,128)(2,1)S(1)}, u32[]{:S(2)}, u32[]{:S(2)}) collective-permute-start(bf16[512,256]{1,0:T(8,128)(2,1)S(1)} %get-tuple-element.96), channel_id=1, source_target_pairs={{0,1},{1,0},{2,3},{3,2},{4,5},{5,4},{6,7},{7,6},{8,9},{9,8},{10,11... | collective-permute-start | bytes 786440 | tf_op jit(solution)/shard_map/ppermute | solution.py:259
  456.3 44.0 %collective-permute-start.35 = (bf16[512,256]{1,0:T(8,128)(2,1)S(1)}, bf16[512,256]{1,0:T(8,128)(2,1)S(1)}, u32[]{:S(2)}, u32[]{:S(2)}) collective-permute-start(bf16[512,256]{1,0:T(8,128)(2,1)S(1)} %add_convert_fusion.1), channel_id=1, source_target_pairs={{0,2},{2,0},{4,6},{6,4},{8,10},{10,8},{12,14},{14,12},{16,18},{18,... | collective-permute-start | bytes 786440 | tf_op jit(solution)/shard_map/ppermute | solution.py:262
  464.9 19.6 %collective-permute-start.24 = (f32[512,256]{1,0:T(8,128)S(1)}, f32[512,256]{1,0:T(8,128)S(1)}, u32[]{:S(2)}, u32[]{:S(2)}) collective-permute-start(f32[512,256]{1,0:T(8,128)S(1)} %fusion.89), channel_id=1, source_target_pairs={{0,1},{1,0},{2,3},{3,2},{4,5},{5,4},{6,7},{7,6},{8,9},{9,8},{10,11... | collective-permute-start | bytes 1572872 | tf_op jit(solution)/shard_map/ppermute | solution.py:259
  471.0 19.3 %collective-permute-start.41 = (bf16[512,256]{1,0:T(8,128)(2,1)S(1)}, bf16[512,256]{1,0:T(8,128)(2,1)S(1)}, u32[]{:S(2)}, u32[]{:S(2)}) collective-permute-start(bf16[512,256]{1,0:T(8,128)(2,1)S(1)} %select_convert_fusion.5), channel_id=1, source_target_pairs={{0,1},{1,0},{2,3},{3,2},{4,5},{5,4},{6,7},{7,6},{8,9},{9,8},{10,11... | collective-permute-start | bytes 786440 | tf_op jit(solution)/shard_map/ppermute | solution.py:259
  484.7 10.0 %collective-permute-start.28 = (bf16[512,256]{1,0:T(8,128)(2,1)S(1)}, bf16[512,256]{1,0:T(8,128)(2,1)S(1)}, u32[]{:S(2)}, u32[]{:S(2)}) collective-permute-start(bf16[512,256]{1,0:T(8,128)(2,1)S(1)} %add_convert_fusion.3), channel_id=1, source_target_pairs={{0,6},{2,4},{4,2},{6,0},{8,14},{10,12},{12,10},{14,8},{16,22},{18,... | collective-permute-start | bytes 786440 | tf_op jit(solution)/shard_map/ppermute | solution.py:262
  490.4 9.9 %collective-permute-start.31 = (bf16[512,256]{1,0:T(8,128)(2,1)S(1)}, bf16[512,256]{1,0:T(8,128)(2,1)S(1)}, u32[]{:S(2)}, u32[]{:S(2)}) collective-permute-start(bf16[512,256]{1,0:T(8,128)(2,1)S(1)} %add_convert_fusion.2), channel_id=1, source_target_pairs={{0,4},{2,6},{4,0},{6,2},{8,12},{10,14},{12,8},{14,10},{16,20},{18,... | collective-permute-start | bytes 786440 | tf_op jit(solution)/shard_map/ppermute | solution.py:262
  494.6 19.3 %collective-permute-start.46 = (bf16[512,256]{1,0:T(8,128)(2,1)S(1)}, bf16[512,256]{1,0:T(8,128)(2,1)S(1)}, u32[]{:S(2)}, u32[]{:S(2)}) collective-permute-start(bf16[512,256]{1,0:T(8,128)(2,1)S(1)} %fusion.44), channel_id=1, source_target_pairs={{0,2},{2,0},{4,6},{6,4},{8,10},{10,8},{12,14},{14,12},{16,18},{18,... | collective-permute-start | bytes 786440 | tf_op jit(solution)/shard_map/ppermute | solution.py:262
  500.3 13.7 %collective-permute-start.44 = (bf16[512,256]{1,0:T(8,128)(2,1)S(1)}, bf16[512,256]{1,0:T(8,128)(2,1)S(1)}, u32[]{:S(2)}, u32[]{:S(2)}) collective-permute-start(bf16[512,256]{1,0:T(8,128)(2,1)S(1)} %fusion.84), channel_id=1, source_target_pairs={{0,4},{2,6},{4,0},{6,2},{8,12},{10,14},{12,8},{14,10},{16,20},{18,... | collective-permute-start | bytes 786440 | tf_op jit(solution)/shard_map/ppermute | solution.py:262
  500.3 13.6 %collective-permute-start.42 = (bf16[512,256]{1,0:T(8,128)(2,1)S(1)}, bf16[512,256]{1,0:T(8,128)(2,1)S(1)}, u32[]{:S(2)}, u32[]{:S(2)}) collective-permute-start(bf16[512,256]{1,0:T(8,128)(2,1)S(1)} %fusion.82), channel_id=1, source_target_pairs={{0,6},{2,4},{4,2},{6,0},{8,14},{10,12},{12,10},{14,8},{16,22},{18,... | collective-permute-start | bytes 786440 | tf_op jit(solution)/shard_map/ppermute | solution.py:262
  (48 other events, 604.7 us)

commit v2 on v0

--- a/solution.py
+++ b/solution.py
@@ -1,6 +1,10 @@
+import functools
+
 import jax
 import jax.numpy as jnp
 from jax import lax
+from jax.experimental import pallas as pl
+from jax.experimental.pallas import tpu as pltpu
 from jax.sharding import PartitionSpec as P
 
 adapter_scale = 4.0
@@ -12,7 +16,7 @@
     return jnp.log(value + jnp.sqrt(1.0 + value * value))
 
 
-def shards(hidden, base_weight, adapter_in, adapter_out, cotangent):
+def plain_shards(hidden, base_weight, adapter_in, adapter_out, cotangent):
     feature_count = hidden.shape[1] * lax.axis_size("tensor")
     contract_last = (((1,), (1,)), ((), ()))
     contract_first = (((0,), (0,)), ((), ()))
@@ -59,9 +63,545 @@
     return (output, grad_in, grad_out)
 
 
+GROUP = 4
+LINE = 4
+HALVES = 2
+core_swap = [(d, d ^ 1) for d in range(LINE * GROUP)]
+x_swap = [(d, d ^ 2) for d in range(LINE * GROUP)]
+both_swap = [(d, d ^ 3) for d in range(LINE * GROUP)]
+pair_swap = [(0, 1), (1, 0)]
+
+
+def line_pairs(sources, step):
+    return [(z * GROUP + r, (z + step) * GROUP + r) for z in sources for r in range(GROUP)]
+
+
+def pick(cases, default):
+    out = default
+    for condition, value in cases:
+        out = jnp.where(condition, value, out)
+    return out
+
+
+def dot32(a, b):
+    return jnp.dot(a, b, preferred_element_type=jnp.float32)
+
+
+ROWS = 256
+COST = 0.01
+
+
+def product_kernel(plan, sources, blocks, has_base, *refs):
+    code, refs = refs[0], refs[1:]
+    weights, refs = refs[: sources[0]], refs[sources[0] :]
+    hiddens, refs = refs[: sources[1]], refs[sources[1] :]
+    (base, other, tangent, factor), refs = (refs[:4], refs[4:]) if has_base else ((None,) * 4, refs)
+    out, weight, slots, weight_sem, slot_sems = refs
+    first_column = plan[1]
+    depth = weight.shape[0]
+    step = depth // len(plan[0])
+
+    def weight_copy(c, candidate):
+        source, row = candidate
+        return pltpu.make_async_copy(
+            weights[source].at[pl.ds(row, step)],
+            weight.at[pl.ds(c * step, step)],
+            weight_sem.at[c],
+        )
+
+    def hidden_copies(b):
+        copies, at = [], 0
+        for source, row, rows in blocks[b]:
+            copies.append(
+                pltpu.make_async_copy(
+                    hiddens[source].at[pl.ds(row, rows), pl.ds(first_column, depth)],
+                    slots.at[b % 2, pl.ds(at, rows)],
+                    slot_sems.at[b % 2],
+                )
+            )
+            at += rows
+        return copies
+
+    for copy in hidden_copies(0):
+        copy.start()
+    for c, candidates in enumerate(plan[0]):
+        if len(candidates) == 1:
+            weight_copy(c, candidates[0]).start()
+        for number, candidate in enumerate(candidates if len(candidates) > 1 else ()):
+
+            @pl.when(code[c] == number)
+            def _(c=c, candidate=candidate):
+                weight_copy(c, candidate).start()
+
+    for copy in hidden_copies(1):
+        copy.start()
+    for c, candidates in enumerate(plan[0]):
+        weight_copy(c, candidates[0]).wait()
+
+    def body(b, carry):
+        slot = lax.rem(b, 2)
+        for number in range(len(blocks)):
+
+            @pl.when(b == number)
+            def _(number=number):
+                for copy in hidden_copies(number):
+                    copy.wait()
+
+        rows = pl.ds(pl.multiple_of(b * ROWS, ROWS), ROWS)
+        total = jnp.dot(slots[slot], weight[...], preferred_element_type=jnp.float32)
+        if base is not None:
+            term = jnp.dot(tangent[rows, :], factor[...], preferred_element_type=jnp.float32)
+            total = total + base[rows, :] + other[rows, :].astype(jnp.float32)
+            total = total + jnp.float32(adapter_scale) * term
+        out[rows, :] = total.astype(out.dtype)
+        for number in range(2, len(blocks)):
+
+            @pl.when(b + 2 == number)
+            def _(number=number):
+                for copy in hidden_copies(number):
+                    copy.start()
+
+        return carry
+
+    lax.fori_loop(0, len(blocks), body, 0)
+
+
+def product(code, step, chunks, hiddens, first_column=0, extra=(), dtype=jnp.float32):
+    weights, candidates = [], []
+    for chunk in chunks:
+        for array, _ in chunk:
+            if not any(array is weight for weight in weights):
+                weights.append(array)
+        candidates.append(
+            tuple(
+                ([array is weight for weight in weights].index(True), row) for array, row in chunk
+            )
+        )
+    depth = step * len(chunks)
+    columns = weights[0].shape[1]
+    blocks, room = [], 0
+    for number, array in enumerate(hiddens):
+        row = 0
+        while row < array.shape[0]:
+            if room == 0:
+                blocks.append([])
+                room = ROWS
+            rows = min(room, array.shape[0] - row)
+            blocks[-1].append((number, row, rows))
+            row, room = row + rows, room - rows
+    height = len(blocks) * ROWS
+    anywhere = pl.BlockSpec(memory_space=pl.ANY)
+    whole = pl.BlockSpec(memory_space=pltpu.VMEM)
+    operands = [code, *weights, *hiddens, *extra]
+    in_specs = [pl.BlockSpec(memory_space=pltpu.SMEM)]
+    in_specs += [anywhere] * (len(weights) + len(hiddens)) + [whole] * len(extra)
+    kernel = functools.partial(
+        product_kernel,
+        (tuple(candidates), first_column),
+        (len(weights), len(hiddens)),
+        blocks,
+        len(extra) > 0,
+    )
+    return pl.pallas_call(
+        kernel,
+        out_shape=jax.ShapeDtypeStruct((height, columns), dtype),
+        in_specs=in_specs,
+        out_specs=whole,
+        scratch_shapes=[
+            pltpu.VMEM((depth, columns), jnp.bfloat16),
+            pltpu.VMEM((2, ROWS, depth), jnp.bfloat16),
+            pltpu.SemaphoreType.DMA((len(chunks),)),
+            pltpu.SemaphoreType.DMA((2,)),
+        ],
+        compiler_params=pltpu.CompilerParams(vmem_limit_bytes=32 * 2**20),
+        cost_estimate=pl.CostEstimate(
+            flops=int(2 * height * depth * columns * COST),
+            bytes_accessed=int(2 * depth * (height + columns) * COST),
+            transcendentals=0,
+        ),
+    )(*operands)
+
+
+TILE = 1024
+LANES = 128
+
+
+def shared_kernel(in_steps, hidden, adapter_in, cotangent, adapter_out, out):
+    number = pl.program_id(0)
+    rank = adapter_in.shape[0]
+    contract_last = (((1,), (1,)), ((), ()))
+
+    @pl.when(number == 0)
+    def _():
+        out[...] = jnp.zeros_like(out)
+
+    @pl.when(number < in_steps)
+    def _():
+        rows = hidden[...]
+        out[:, :rank] += lax.dot_general(
+            rows, adapter_in[...], contract_last, preferred_element_type=jnp.float32
+        )
+        wide = rows.astype(jnp.float32)
+        squares = jnp.sum(wide * wide, axis=1, keepdims=True)
+        out[:, 2 * rank :] += jnp.broadcast_to(squares, (rows.shape[0], LANES))
+
+    @pl.when(number >= in_steps)
+    def _():
+        out[:, rank : 2 * rank] += adapter_scale * lax.dot_general(
+            cotangent[...], adapter_out[...], contract_last, preferred_element_type=jnp.float32
+        )
+
+
+def shared_sums(hidden, adapter_in, cotangent, adapter_out):
+    tokens, rank = hidden.shape[0], adapter_in.shape[0]
+    in_steps, out_steps = hidden.shape[1] // TILE, cotangent.shape[1] // TILE
+    early = lambda i: (0, jnp.minimum(i, in_steps - 1))
+    late = lambda i: (0, jnp.maximum(i - in_steps, 0))
+    return pl.pallas_call(
+        functools.partial(shared_kernel, in_steps),
+        grid=(in_steps + out_steps,),
+        out_shape=jax.ShapeDtypeStruct((tokens, 2 * rank + LANES), jnp.float32),
+        in_specs=[
+            pl.BlockSpec((tokens, TILE), early),
+            pl.BlockSpec((rank, TILE), early),
+            pl.BlockSpec((tokens, TILE), late),
+            pl.BlockSpec((rank, TILE), late),
+        ],
+        out_specs=pl.BlockSpec((tokens, 2 * rank + LANES), lambda i: (0, 0)),
+        compiler_params=pltpu.CompilerParams(vmem_limit_bytes=32 * 2**20),
+        cost_estimate=pl.CostEstimate(
+            flops=int(2 * tokens * rank * TILE * (in_steps + out_steps) * COST),
+            bytes_accessed=int(2 * TILE * (tokens + rank) * (in_steps + out_steps) * COST),
+            transcendentals=0,
+        ),
+    )(hidden, adapter_in, cotangent, adapter_out)
+
+
+def lift_of(radius):
+    square = radius * radius
+    series = 1.0 + square / 6.0 * (
+        1.0 + square / 20.0 * (1.0 + square / 42.0 * (1.0 + square / 72.0))
+    )
+    large = (jnp.exp(radius) - jnp.exp(-radius)) * 0.5 / radius
+    return jnp.where(radius < 1.0, series, large)
+
+
+def gradient_kernel(
+    in_steps, feature_count, own, other, order, hidden, cotangent, tangent_out, sent, kept, left_in, left_out
+):
+    number = pl.program_id(0)
+    rank, half = order.shape[0], sent.shape[0]
+
+    @pl.when(number == 0)
+    def _():
+        total = own[...] + other[...]
+        raw, tangent_grad = total[:, :rank], total[:, rank : 2 * rank]
+        square_sum = total[:, 2 * rank : 2 * rank + 1]
+        level = jnp.sqrt(square_sum / feature_count + tiny_eps)
+        lift_factor = lift_of(exp_rate * level)
+        lorentz = lift_factor * raw
+        norm_value = jnp.sqrt(jnp.sum(lorentz * lorentz, axis=1, keepdims=True) + tiny_eps)
+        phi_value = inverse_sinh(norm_value) / norm_value
+        tangent = (phi_value * lorentz).astype(jnp.bfloat16)
+        inner_value = jnp.sum(lorentz * tangent_grad, axis=1, keepdims=True)
+        coefficient = (1.0 / jnp.sqrt(1.0 + norm_value * norm_value) - phi_value) / (
+            norm_value * norm_value
+        )
+        lorentz_grad = phi_value * tangent_grad + (coefficient * inner_value) * lorentz
+        raw_grad = (lift_factor * lorentz_grad).astype(jnp.bfloat16)
+        tangent_out[...] = tangent
+        contract_last = (((1,), (1,)), ((), ()))
+        for target, value in ((left_in, raw_grad), (left_out, tangent)):
+            target[...] = lax.dot_general(
+                order[...], value, contract_last, preferred_element_type=jnp.float32
+            ).astype(jnp.bfloat16)
+
+    @pl.when(number < in_steps)
+    def _():
+        total = jnp.dot(left_in[...], hidden[...], preferred_element_type=jnp.float32)
+        sent[...] = total[:half]
+        kept[...] = total[half:]
+
+    @pl.when(number >= in_steps)
+    def _():
+        total = adapter_scale * jnp.dot(
+            left_out[...], cotangent[...], preferred_element_type=jnp.float32
+        )
+        sent[...] = total[:half]
+        kept[...] = total[half:]
+
+
+def gradients(own, other, order, feature_count, hidden, cotangent):
+    rank, tokens = order.shape[0], hidden.shape[0]
+    in_steps, out_steps = hidden.shape[1] // TILE, cotangent.shape[1] // TILE
+    steps = in_steps + out_steps
+    shape = jax.ShapeDtypeStruct((rank // 2, steps * TILE), jnp.float32)
+    part = pl.BlockSpec((rank // 2, TILE), lambda i: (0, i))
+    return pl.pallas_call(
+        functools.partial(gradient_kernel, in_steps, feature_count),
+        grid=(steps,),
+        out_shape=(jax.ShapeDtypeStruct((tokens, rank), jnp.bfloat16), shape, shape),
+        in_specs=[
+            pl.BlockSpec(own.shape, lambda i: (0, 0)),
+            pl.BlockSpec(own.shape, lambda i: (0, 0)),
+            pl.BlockSpec(order.shape, lambda i: (0, 0)),
+            pl.BlockSpec((tokens, TILE), lambda i: (0, jnp.minimum(i, in_steps - 1))),
+            pl.BlockSpec((tokens, TILE), lambda i: (0, jnp.maximum(i - in_steps, 0))),
+        ],
+        out_specs=(pl.BlockSpec((tokens, rank), lambda i: (0, 0)), part, part),
+        scratch_shapes=[pltpu.VMEM((rank, tokens), jnp.bfloat16)] * 2,
+        compiler_params=pltpu.CompilerParams(vmem_limit_bytes=32 * 2**20),
+        cost_estimate=pl.CostEstimate(
+            flops=int(2 * rank * tokens * steps * TILE * COST),
+            bytes_accessed=int((2 * tokens + 4 * rank) * steps * TILE * COST),
+            transcendentals=0,
+        ),
+    )(own, other, order, hidden, cotangent)
+
+
+def assemble_kernel(code, *refs):
+    out = refs[-1]
+    for number, piece in enumerate(refs[:-1]):
+
+        @pl.when(pl.program_id(0) == number)
+        def _(piece=piece):
+            out[...] = piece[...]
+
+
+def assemble(places, pieces):
+    tokens, columns = pieces[0].shape
+    return pl.pallas_call(
+        assemble_kernel,
+        grid_spec=pltpu.PrefetchScalarGridSpec(
+            num_scalar_prefetch=1,
+            grid=(len(pieces),),
+            in_specs=[pl.BlockSpec((tokens, columns), lambda i, code: (0, 0))] * len(pieces),
+            out_specs=pl.BlockSpec((tokens, columns), lambda i, code: (0, code[i])),
+        ),
+        out_shape=jax.ShapeDtypeStruct((tokens, columns * len(pieces)), pieces[0].dtype),
+        compiler_params=pltpu.CompilerParams(vmem_limit_bytes=32 * 2**20),
+    )(jnp.stack(places).astype(jnp.int32), *pieces)
+
+
+class Held(dict):
+    def gate(self, *names):
+        names = list(dict.fromkeys(names))
+        for name, value in zip(names, lax.optimization_barrier(tuple(self[n] for n in names))):
+            self[name] = value
+
+    def all(self, letter, numbers):
+        return [self[letter, i] for i in numbers]
+
+
+def fast_shards(hidden, base_weight, adapter_in, adapter_out, cotangent):
+    feature_count = hidden.shape[1] * 2
+    tokens, depth = hidden.shape
+    columns = base_weight.shape[1]
+    place = lax.axis_index("dp")
+    z, member = place // GROUP, place % GROUP
+    x, core = member // 2, member % 2
+    y = lax.axis_index("tensor")
+    outer = jnp.logical_or(z == 0, z == LINE - 1)
+    inner = jnp.logical_not(outer)
+    early = (z // 2) == y
+    late = jnp.logical_not(early)
+    side = jnp.where(z < 2, 0, 1)
+    scale = jnp.float32(adapter_scale)
+    parts, slots = 4, 3 * HALVES
+    rows, step = depth // HALVES, tokens // parts
+    held = Held()
+    held["own", 0], held["x", 0] = base_weight[:rows], hidden[:step]
+    held["weight"], held["hidden"] = base_weight, hidden
+
+    def send_weight(s):
+        hop = s // HALVES
+        if hop == LINE - 2:
+            far = [jnp.where(side == 0, held["left", q], held["right", q]) for q in (2, 3)]
+            far.append(held["own", 1])
+            sent = jnp.where(jnp.logical_and(early, inner), far[s - 3], far[s - 4])
+            pairs = line_pairs([1], -1) + line_pairs([LINE - 2], 1)
+            held["left", s] = held["right", s] = lax.ppermute(sent, "dp", pairs)
+            return
+        for name, sign, last in (("left", -1, 1), ("right", 1, LINE - 2)):
+            sent = held["own", s] if s < HALVES else held[name, s - HALVES]
+            if s > 0:
+                other = held[name, s - 1]
+                sent = jnp.where(jnp.logical_and(early, z == last), other, sent)
+            sources = [q for q in range(LINE) if 0 <= q + sign < LINE and 0 <= q - sign * hop < LINE]
+            held[name, s] = lax.ppermute(sent, "dp", line_pairs(sources, sign))
+
+    def send_hidden(i):
+        if i:
+            held["x", i] = held["hidden"][i * step : (i + 1) * step]
+        held["x", i] = lax.ppermute(held["x", i], "dp", x_swap)
+
+    def over_core(name, result=None):
+        held[result or name] = lax.ppermute(held[name], "dp", core_swap)
+
+    def pass_hidden(i):
+        over_core(("x", i), ("far", i))
+
+    def send_sums(k):
+        sent = lax.dynamic_index_in_dim(held["mine"], z ^ k, 0, False).astype(jnp.bfloat16)
+        pairs = [(q * GROUP + r, (q ^ k) * GROUP + r) for q in range(LINE) for r in range(GROUP)]
+        held["got", k] = lax.ppermute(sent, "dp", pairs)
+
+    def codes(default, *cases):
+        return pick(cases, default).astype(jnp.int32)[None]
+
+    def streams(*numbers):
+        return [(held[name, s], 0) for s in numbers for name in ("left", "right")]
+
+    def window(s, *names):
+        names = [("left", s), ("right", s), "weight", *names]
+        held.gate(*names)
+        held["own", 1] = held["weight"][rows:]
+        if s < LINE - 1:
+            send_weight(s + 1)
+        if s == LINE - 1:
+            send_weight(s + 1)
+            send_weight(s + 2)
+
+    end_early = jnp.logical_and(outer, early)
+    end_late = jnp.logical_and(outer, late)
+    inner_late = jnp.logical_and(inner, late)
+    none = jnp.zeros((1,), jnp.int32)
+    first_code = codes(2 + side, (end_early, side), (inner_late, 3 - side))
+    first_code = jnp.concatenate([first_code] * HALVES)
+    second_code = codes(4 + side, (end_early, side), (inner_late, 2 + side))
+    second_code = jnp.concatenate([second_code] * HALVES)
+    third_code = [
+        codes(
+            1 - side,
+            (end_early, side + (0 if q == 0 else 2)),
+            (end_late, 2 + side),
+            (inner_late, 4 + side),
+        )
+        for q in range(HALVES)
+    ]
+
+    send_weight(0)
+    send_hidden(0)
+    held["core"] = lax.ppermute(hidden, "dp", core_swap)
+    held["shared"] = shared_sums(hidden, adapter_in, cotangent, adapter_out)
+    held["shared other"] = lax.ppermute(held["shared"], "tensor", pair_swap)
+    rank = adapter_in.shape[0]
+    share = rank // (LINE * GROUP)
+    row = jnp.arange(rank)
+    which = row // (LINE * share)
+    owner = member ^ jnp.where(which == 0, 3, jnp.where(which == 1, 1, jnp.where(which == 2, 2, 0)))
+    column = (row // share % LINE) * (GROUP * share) + owner * share + row % share
+    held["order"] = (column[:, None] == jnp.arange(rank)[None, :]).astype(jnp.bfloat16)
+
+    window(0, ("x", 0), "hidden")
+    send_hidden(1)
+    held["t", 0], held["sent"], held["kept"] = gradients(
+        held["shared"], held["shared other"], held["order"], feature_count, hidden, cotangent
+    )
+    over_core("sent")
+
+    window(1, ("x", 1), "hidden", "core", "kept", ("t", 0))
+    send_hidden(2)
+    pass_hidden(0)
+    near = [hidden, held["core"]]
+    whole_weight = [[(base_weight, 0)]]
+    held["own sum", 0] = product(none, depth, whole_weight, near)
+
+    window(2, ("x", 2), "hidden", ("far", 0), "sent", "kept", ("own sum", 0))
+    send_hidden(3)
+    pass_hidden(1)
+    pass_hidden(2)
+    sums = held["kept"] + held["sent"]
+    flat = sums[: rank // 4].astype(jnp.bfloat16)
+    held["sent"] = jnp.concatenate([flat, held["t", 0].reshape(flat.shape[0], -1)], axis=1)
+    held["kept"] = sums[rank // 4 :]
+    first = [streams(1 + q, q) for q in range(HALVES)]
+    held["first sum", 0] = product(first_code, rows, first, near)
+
+    held["y", 0] = jnp.where(early, held["first sum", 0], held["own sum", 0])
+
+    window(3, ("x", 3), ("far", 1), ("far", 2), "sent", "kept", ("first sum", 0), ("y", 0))
+    pass_hidden(3)
+    held["sent"] = lax.ppermute(held["sent"], "dp", x_swap)
+    held["y", 0] = lax.ppermute(held["y", 0], "tensor", pair_swap)
+    half = parts // 2
+    for h in (1, 2):
+        pieces = range((h - 1) * half, h * half)
+        members = held.all("x", pieces) + held.all("far", pieces)
+        held["own sum", h] = product(none, depth, whole_weight, members)
+        held["first sum", h] = product(first_code, rows, first, members)
+
+    def in_order(name):
+        a, b = held[name, 1], held[name, 2]
+        cut = a.shape[0] // 2
+        return jnp.concatenate([a[:cut], b[:cut], a[cut:], b[cut:]])
+
+    first_sums = [held["first sum", 0], in_order("first sum")]
+    own_sums = [held["own sum", 0], in_order("own sum")]
+    held["y", 1] = lax.ppermute(
+        jnp.where(early, first_sums[1], own_sums[1]), "tensor", pair_swap
+    )
+
+    window(4, "sent", "kept", *[("far", i) for i in range(parts)], ("y", 0), ("y", 1), ("t", 0))
+    width = held["kept"].shape[1]
+    held["t", 2] = held["sent"][:, width:].reshape(tokens, -1)
+    for m in (0, 2):
+        held["t", m + 1] = held["t", m]
+        over_core(("t", m + 1))
+    held["mine"] = held["kept"] + held["sent"][:, :width].astype(jnp.float32)
+    held["mine"] = held["mine"].reshape(LINE, share, -1)
+    for k in (1, 2, 3):
+        send_sums(k)
+    far = held.all("x", range(parts)) + held.all("far", range(parts))
+    groups = (near, far)
+    second = [streams(3 + q, q, 2 + q) for q in range(HALVES)]
+    third = [streams(q, 4 + q, 2 + q) for q in range(HALVES)]
+    for h in (1, 0):
+        held["second sum", h] = product(second_code, rows, second, groups[h])
+        sent = jnp.where(early, held["second sum", h], first_sums[h])
+        held["w", h] = lax.ppermute(sent.astype(jnp.bfloat16), "tensor", pair_swap)
+    parity = (z % 2) ^ inner_late.astype(jnp.int32)
+    blocks = [(parity ^ turn) * GROUP for turn in range(2)]
+    factors = [
+        lax.dynamic_slice_in_dim(adapter_out, (block + member) * columns, columns, 1)
+        for block in blocks
+    ]
+    swaps = (None, core_swap, x_swap, both_swap)
+    numbers = ((0, 1), (2, 3))
+    places, pieces = [], []
+
+    def give_out(turn, h, value):
+        for i, m in reversed(list(enumerate(numbers[h]))):
+            piece = value[i * tokens : (i + 1) * tokens]
+            if m:
+                piece = lax.ppermute(piece, "dp", swaps[m])
+            places.append(blocks[turn] + (member ^ m))
+            pieces.append(piece)
+
+    for h in (1, 0):
+        held["third sum", h] = product(third_code[0], rows, third[:1], groups[h])
+    group_tangents = [jnp.concatenate(held.all("t", numbers[h])) for h in range(2)]
+    for h in (1, 0):
+        total = jnp.where(early, own_sums[h], held["second sum", h]) + held["y", h]
+        total = total + scale * dot32(group_tangents[h], factors[0])
+        give_out(0, h, total.astype(jnp.bfloat16))
+
+    window(5, ("third sum", 0), ("third sum", 1))
+    for h in (1, 0):
+        chunk = [streams(1, 5, 3)]
+        extra = (held["third sum", h], held["w", h], group_tangents[h], factors[1])
+        value = product(third_code[1], rows, chunk, groups[h], rows, extra, jnp.bfloat16)
+        give_out(1, h, value)
+    output = assemble(places, pieces)
+    grads = lax.dynamic_index_in_dim(held["mine"], z, 0, False)
+    held["grads"] = sum((held["got", k].astype(jnp.float32) for k in (1, 2, 3)), grads)
+    return (output, held["grads"][:, :depth], held["grads"][:, depth:])
+
+
 def solution(mesh):
+    fits = mesh.shape["dp"] == LINE * GROUP and mesh.shape["tensor"] == 2
     return jax.shard_map(
-        shards,
+        fast_shards if fits else plain_shards,
         mesh=mesh,
         in_specs=(
             P("dp", "tensor"),

time: 617 us -> 362 us (0.59)
  waiting for transfers between devices: 524 us -> 124 us
  Pallas kernels: 0 us -> 92.1 us
  starting transfers between devices: 0.39 us -> 67.5 us
  matrix products: 64.8 us -> 3.33 us
  local copies, waits for them, and re-layouts: 0.82 us -> 40 us
  other arithmetic: 6.24 us -> 31.3 us
  between operations: 15.7 us -> 1.58 us
    all_gather x1 -> x0, waiting for transfers between devices: 291 us -> none  [shards(): lax.all_gather(base_weight, 'dp', axis=1, tiled=True)]
    reduce_scatter x3 -> x0, waiting for transfers between devices: 232 us -> none  [the longest x1 97.1 us: shards(): lax.psum_scatter(in_part, 'dp', scatter_dimension=0, tiled=True)]
    ppermute x0 -> x37, waiting for transfers between devices: none -> 124 us  [the longest x8 72.1 us: send_weight(): held[name, s] = lax.ppermute(sent, 'dp', line_pairs(sources, sign))]
    pallas_call x0 -> x15, Pallas kernels: none -> 92.1 us  [the longest x12 74.8 us: product(): pl.pallas_call(kernel, out_shape=jax.ShapeDtypeStruct((height, columns),...]
    ppermute x0 -> x37, starting transfers between devices: none -> 67.5 us  [the longest x8 20.2 us: send_weight(): held[name, s] = lax.ppermute(sent, 'dp', line_pairs(sources, sign))]
    dot_general x6 -> x2, matrix products: 64.8 us -> 3.33 us  [dot32(): return jnp.dot(a, b, preferred_element_type=jnp.float32)]
    select_n x0 -> x8, other arithmetic: none -> 21.2 us  [the longest x5 13.9 us: send_weight(): sent = jnp.where(jnp.logical_and(early, z == last), other, sent)]
    unnamed x8 -> x118, local copies, waits for them, and re-layouts: 0.82 us -> 20.2 us
  transfers between devices with their start and end apart: 5 -> 37, of which waited for: 4 -> 14; matrix products, arithmetic and copies ran while one was open for 12% -> 15% of each run, Pallas kernels for 0% -> 25%
where the time goes in v2:
time: 362 us; the launch traced here: 360 us
  waiting for transfers between devices  124 us (34%)
  Pallas kernels  92.1 us (25%)
  starting transfers between devices  67.5 us (19%)
  local copies, waits for them, and re-layouts  40 us (11%)
  other arithmetic  31.3 us (9%)
    pallas_call x12, Pallas kernels, product(): pl.pallas_call(kernel, out_shape=jax.ShapeDtypeStruct((height, columns),...  74.8 us
    ppermute x8, waiting for transfers between devices, send_weight(): held[name, s] = lax.ppermute(sent, 'dp', line_pairs(sources, sign))  72.1 us
    ppermute x8, starting transfers between devices, send_weight(): held[name, s] = lax.ppermute(sent, 'dp', line_pairs(sources, sign))  20.2 us
    ppermute x4, waiting for transfers between devices, send_hidden(): held['x', i] = lax.ppermute(held['x', i], 'dp', x_swap)  20.2 us
    unnamed x118, local copies, waits for them, and re-layouts  20.2 us
    ppermute x7, starting transfers between devices, over_core(): held[result or name] = lax.ppermute(held[name], 'dp', core_swap)  17.4 us
    select_n x5, other arithmetic, send_weight(): sent = jnp.where(jnp.logical_and(early, z == last), other, sent)  13.9 us
    ppermute x2, waiting for transfers between devices, send_weight(): held['left', s] = held['right', s] = lax.ppermute(sent, 'dp', pairs)  13.4 us
  transfers between devices with their start and end apart: 37, of which 14 were waited for; matrix products, arithmetic and copies ran while one was open for 15% of the time, Pallas kernels for 25%

profile of v2, /device:TPU:1, one launch (start us, length us, event | category | flops | bytes accessed | tf_op | source)
XLA Modules:
  0.0 359.6 jit_solution(4115329828092544961)
XLA Ops:
  0.8 3.0 slice.88
  3.8 1.5 collective-permute-start
  5.3 6.5 %collective-permute-start.1 = (bf16[3584,256]{1,0:T(8,128)(2,1)}, bf16[3584,256]{1,0:T(8,128)(2,1)}, u32[]{:S(2)}, u32[]{:S(2)}) collective-permute-start(bf16[3584,256]{1,0:T(8,128)(2,1)} %slice.88), channel_id=1, source_target_pairs={{0,8},{2,10},{4,12},{6,14},{8,16},{10,18},{12,20},{14,22},{16,24},... | collective-permute-start | bytes 5505032 | tf_op jit(solution)/shard_map/ppermute | solution.py:431
  11.8 2.9 slice.89
  16.1 3.1 copy-done
  19.2 5.8 %shard_map.76.own = f32[512,640]{1,0:T(8,128)S(1)} custom-call(bf16[512,7168]{1,0:T(8,128)(2,1)S(1)} %copy-done, bf16[256,7168]{1,0:T(8,128)(2,1)S(1)} %copy-done.30, bf16[512,2048]{1,0:T(8,128)(2,1)S(1)} %copy-done.27, bf16[256,2048]{1,0:T(8,128)(2,1)S(1)} %copy-done.31), custom_call_target="tpu_custom_call" | custom-call | flops 24159192 | bytes 141557 | tf_op jit(solution)/shard_map/pallas_call | solution.py:260
  26.4 23.0 %collective-permute-done.refs_3_.refs_1_ = bf16[3584,256]{1,0:T(8,128)(2,1)S(1)} collective-permute-done((bf16[3584,256]{1,0:T(8,128)(2,1)}, bf16[3584,256]{1,0:T(8,128)(2,1)S(1)}, u32[]{:S(2)}, u32[]{:S(2)}) %collective-permute-start) | collective-permute-done | bytes 1835040 | tf_op jit(solution)/shard_map/ppermute | solution.py:431
  50.3 6.1 %collective-permute-done.2.refs_2_.refs_7_.refs_11_ = bf16[128,7168]{1,0:T(8,128)(2,1)} collective-permute-done((bf16[128,7168]{1,0:T(8,128)(2,1)}, bf16[128,7168]{1,0:T(8,128)(2,1)}, u32[]{:S(2)}, u32[]{:S(2)}) %collective-permute-start.2) | collective-permute-done | bytes 1835040 | tf_op jit(solution)/shard_map/ppermute | solution.py:436
  56.4 3.7 %broadcast_select_fusion.3 = (bf16[3584,256]{1,0:T(8,128)(2,1)}, bf16[3584,256]{1,0:T(8,128)(2,1)}) fusion(bf16[3584,256]{1,0:T(8,128)(2,1)} %collective-permute-done.1.refs_4_.refs_2_, pred[]{:T(512)S(6)} %and.97, bf16[7168,256]{1,0:T(8,128)(2,1)} %refs_1_.5, bf16[3584,256]{1,0:T(8,128)(2,1)S(1)} %collective-permute-done.refs_3_.refs_1_, pred[]{:T(512)S(6)} %and.96), kind=kLoop, calls=%fused_computation.7 | loop fusion | flops 1835008 | bytes 9175042 | tf_op jit(solution)/shard_map/jit(_where)/select_n | solution.py:429
  61.3 5.2 %collective-permute-start.4 = (bf16[3584,256]{1,0:T(8,128)(2,1)}, bf16[3584,256]{1,0:T(8,128)(2,1)}, u32[]{:S(2)}, u32[]{:S(2)}) collective-permute-start(bf16[3584,256]{1,0:T(8,128)(2,1)} %get-tuple-element.105), channel_id=1, source_target_pairs={{0,8},{2,10},{4,12},{6,14},{8,16},{10,18},{12,20},{14,22},{16,24},... | collective-permute-start | bytes 5505032 | tf_op jit(solution)/shard_map/ppermute | solution.py:431
  66.6 2.9 slice.91
  70.6 3.1 copy-done.1
  73.7 1.6 copy-done.28
  75.3 7.9 %shard_map.77 = (bf16[512,256]{1,0:T(8,128)(2,1)S(1)}, f32[128,9216]{1,0:T(8,128)S(1)}, f32[128,9216]{1,0:T(8,128)S(1)}) custom-call(f32[512,640]{1,0:T(8,128)S(1)} %shard_map.76.own, f32[512,640]{1,0:T(8,128)} %collective-permute-done.7.other, bf16[256,256]{1,0:T(8,128)(2,1)S(1)} %fusion.6.order, bf16[512,7168]{1,0:T(8,128)(2,1)S(1)} %copy-done.1, ...), custom_call_target="tpu_custom_call" | custom-call | flops 24159192 | bytes 188743 | tf_op jit(solution)/shard_map/pallas_call | solution.py:340
  83.2 2.2 copy-done.29
  85.5 2.3 collective-permute-start.12
  87.8 14.9 %collective-permute-done.3.refs_1_.refs_9_ = bf16[3584,256]{1,0:T(8,128)(2,1)} collective-permute-done((bf16[3584,256]{1,0:T(8,128)(2,1)}, bf16[3584,256]{1,0:T(8,128)(2,1)}, u32[]{:S(2)}, u32[]{:S(2)}) %collective-permute-start.3) | collective-permute-done | bytes 1835040 | tf_op jit(solution)/shard_map/ppermute | solution.py:431
  102.6 2.1 collective-permute-start.11
  104.7 4.9 %collective-permute-done.5.refs_3_.refs_8_.refs_12_ = bf16[128,7168]{1,0:T(8,128)(2,1)} collective-permute-done((bf16[128,7168]{1,0:T(8,128)(2,1)}, bf16[128,7168]{1,0:T(8,128)(2,1)}, u32[]{:S(2)}, u32[]{:S(2)}) %collective-permute-start.5) | collective-permute-done | bytes 1835040 | tf_op jit(solution)/shard_map/ppermute | solution.py:436
  111.0 1.5 collective-permute-start.8
  112.6 3.0 broadcast_select_fusion.2
  117.6 6.2 %shard_map.78 = f32[1024,256]{1,0:T(8,128)S(1)} custom-call(s32[1]{0:T(128)} %constant.113.clone.1.refs_0_, bf16[7168,256]{1,0:T(8,128)(2,1)S(1)} %copy-done.16, bf16[512,7168]{1,0:T(8,128)(2,1)S(1)} %bitcast.28, bf16[512,7168]{1,0:T(8,128)(2,1)} %collective-permute-done.6.refs_3_.refs_8_.refs_12_), custom_call_target="tpu_custom_call" | custom-call | flops 37580964 | bytes 183500 | tf_op jit(solution)/shard_map/pallas_call | solution.py:205
  124.7 3.0 collective-permute-start.16
  127.8 24.6 %collective-permute-done.8.refs_5_ = bf16[3584,256]{1,0:T(8,128)(2,1)S(1)} collective-permute-done((bf16[3584,256]{1,0:T(8,128)(2,1)}, bf16[3584,256]{1,0:T(8,128)(2,1)S(1)}, u32[]{:S(2)}, u32[]{:S(2)}) %collective-permute-start.8) | collective-permute-done | bytes 1835040 | tf_op jit(solution)/shard_map/ppermute | solution.py:431
  152.4 3.3 collective-permute-done.10.refs_2_.refs_7_.refs_13_.refs_9_
  155.6 2.9 broadcast_select_fusion.4
  159.8 3.0 broadcast_select_fusion.1
  162.8 1.9 collective-permute-start.14
  166.5 4.1 %collective-permute-start.17 = (bf16[128,7168]{1,0:T(8,128)(2,1)}, bf16[128,7168]{1,0:T(8,128)(2,1)}, u32[]{:S(2)}, u32[]{:S(2)}) collective-permute-start(bf16[128,7168]{1,0:T(8,128)(2,1)} %collective-permute-done.10.refs_2_.refs_7_.refs_13_.refs_9_), channel_id=1, source_target_pairs={{0,2},{2,0},{4,6},{6,4},{8,10},{10,8},{12,14},{14,12},{16,18},{18,... | collective-permute-start | bytes 5505032 | tf_op jit(solution)/shard_map/ppermute | solution.py:439
  171.5 4.5 %add.149 = f32[128,9216]{1,0:T(8,128)S(1)} add(f32[128,9216]{1,0:T(8,128)} %copy-done.29, f32[128,9216]{1,0:T(8,128)} %collective-permute-done.12) | non-fusion elementwise | flops 1179648 | bytes 14155776 | tf_op jit(solution)/shard_map/add | solution.py:514
  176.2 1.6 slice.118
  179.5 7.8 %shard_map.79 = f32[1024,256]{1,0:T(8,128)S(1)} custom-call(s32[2]{0:T(128)S(1)} %pad_add_fusion.refs_0_, bf16[3584,256]{1,0:T(8,128)(2,1)} %collective-permute-done.3.refs_1_.refs_9_, bf16[3584,256]{1,0:T(8,128)(2,1)} %collective-permute-done.4.refs_2_.refs_10_, bf16[3584,256]{1,0:T(8,128)(2,1)S(1)} %copy-done.4, ...), custom_call_target="tpu_custom_call" | custom-call | flops 37580964 | bytes 183500 | tf_op jit(solution)/shard_map/pallas_call | solution.py:205
  189.6 8.7 %collective-permute-done.13.refs_1_.refs_5_ = bf16[3584,256]{1,0:T(8,128)(2,1)} collective-permute-done((bf16[3584,256]{1,0:T(8,128)(2,1)}, bf16[3584,256]{1,0:T(8,128)(2,1)}, u32[]{:S(2)}, u32[]{:S(2)}) %collective-permute-start.13) | collective-permute-done | bytes 1835040 | tf_op jit(solution)/shard_map/ppermute | solution.py:431
  198.3 6.0 %collective-permute-done.15.refs_3_.refs_8_.refs_14_.refs_10_ = bf16[128,7168]{1,0:T(8,128)(2,1)} collective-permute-done((bf16[128,7168]{1,0:T(8,128)(2,1)}, bf16[128,7168]{1,0:T(8,128)(2,1)}, u32[]{:S(2)}, u32[]{:S(2)}) %collective-permute-start.15) | collective-permute-done | bytes 1835040 | tf_op jit(solution)/shard_map/ppermute | solution.py:436
  204.4 4.5 %collective-permute-start.18 = (bf16[128,7168]{1,0:T(8,128)(2,1)}, bf16[128,7168]{1,0:T(8,128)(2,1)}, u32[]{:S(2)}, u32[]{:S(2)}) collective-permute-start(bf16[128,7168]{1,0:T(8,128)(2,1)} %collective-permute-done.15.refs_3_.refs_8_.refs_14_.refs_10_), channel_id=1, source_target_pairs={{0,2},{2,0},{4,6},{6,4},{8,10},{10,8},{12,14},{14,12},{16,18},{18,... | collective-permute-start | bytes 5505032 | tf_op jit(solution)/shard_map/ppermute | solution.py:439
  208.8 5.1 %slice_select_fusion = (bf16[3584,256]{1,0:T(8,128)(2,1)}, bf16[3584,256]{1,0:T(8,128)(2,1)}) fusion(bf16[7168,256]{1,0:T(8,128)(2,1)} %refs_1_.5, pred[]{:T(512)S(6)} %and.103, bf16[3584,256]{1,0:T(8,128)(2,1)} %collective-permute-done.13.refs_1_.refs_5_, bf16[3584,256]{1,0:T(8,128)(2,1)} %collective-permute-done.14.refs_2_.refs_6_, pred[]{:T(512)S(6)} %eq.81, ...), kind=kLoop, calls=%fused_computation.2 | loop fusion | flops 3670016 | bytes 12845058 | tf_op jit(solution)/shard_map/jit(_where)/select_n | solution.py:421
  218.4 5.7 %shard_map.82 = f32[512,256]{1,0:T(8,128)S(1)} custom-call(s32[2]{0:T(128)S(1)} %pad_add_fusion.refs_0_, bf16[3584,256]{1,0:T(8,128)(2,1)} %collective-permute-done.3.refs_1_.refs_9_, bf16[3584,256]{1,0:T(8,128)(2,1)} %collective-permute-done.4.refs_2_.refs_10_, bf16[3584,256]{1,0:T(8,128)(2,1)S(1)} %copy-done.5, ...), custom_call_target="tpu_custom_call" | custom-call | flops 18790480 | bytes 110100 | tf_op jit(solution)/shard_map/pallas_call | solution.py:205
  224.1 4.3 %shard_map.80 = f32[512,256]{1,0:T(8,128)S(1)} custom-call(s32[1]{0:T(128)} %constant.113.clone.1.refs_0_, bf16[7168,256]{1,0:T(8,128)(2,1)S(1)} %copy-done.17, bf16[128,7168]{1,0:T(8,128)(2,1)} %collective-permute-done.2.refs_2_.refs_7_.refs_11_, bf16[128,7168]{1,0:T(8,128)(2,1)} %collective-permute-done.5.refs_3_.refs_8_.refs_12_, ...), custom_call_target="tpu_custom_call" | custom-call | flops 18790480 | bytes 110100 | tf_op jit(solution)/shard_map/pallas_call | solution.py:205
  228.5 5.4 %shard_map.83 = f32[512,256]{1,0:T(8,128)S(1)} custom-call(s32[2]{0:T(128)S(1)} %pad_add_fusion.refs_0_, bf16[3584,256]{1,0:T(8,128)(2,1)} %collective-permute-done.3.refs_1_.refs_9_, bf16[3584,256]{1,0:T(8,128)(2,1)} %collective-permute-done.4.refs_2_.refs_10_, bf16[3584,256]{1,0:T(8,128)(2,1)S(1)} %copy-done.5, ...), custom_call_target="tpu_custom_call" | custom-call | flops 18790480 | bytes 110100 | tf_op jit(solution)/shard_map/pallas_call | solution.py:205
  234.0 4.5 %shard_map.81 = f32[512,256]{1,0:T(8,128)S(1)} custom-call(s32[1]{0:T(128)} %constant.113.clone.1.refs_0_, bf16[7168,256]{1,0:T(8,128)(2,1)S(1)} %copy-done.17, bf16[128,7168]{1,0:T(8,128)(2,1)} %collective-permute-done.10.refs_2_.refs_7_.refs_13_.refs_9_, bf16[128,7168]{1,0:T(8,128)(2,1)} %collective-permute-done.15.refs_3_.refs_8_.refs_14_.refs_10_, ...), custom_call_target="tpu_custom_call" | custom-call | flops 18790480 | bytes 110100 | tf_op jit(solution)/shard_map/pallas_call | solution.py:205
  242.2 6.7 %collective-permute-done.20 = bf16[64,11264]{1,0:T(8,128)(2,1)} collective-permute-done((bf16[64,11264]{1,0:T(8,128)(2,1)}, bf16[64,11264]{1,0:T(8,128)(2,1)}, u32[]{:S(2)}, u32[]{:S(2)}) %collective-permute-start.20) | collective-permute-done | bytes 1441824 | tf_op jit(solution)/shard_map/ppermute | solution.py:525
  248.9 13.4 %collective-permute-done.19.refs_7_.refs_8_.refs_3_.refs_4_ = bf16[3584,256]{1,0:T(8,128)(2,1)} collective-permute-done((bf16[3584,256]{1,0:T(8,128)(2,1)}, bf16[3584,256]{1,0:T(8,128)(2,1)}, u32[]{:S(2)}, u32[]{:S(2)}) %collective-permute-start.19) | collective-permute-done | bytes 1835040 | tf_op jit(solution)/shard_map/ppermute | solution.py:423
  262.3 1.9 collective-permute-done.22
  266.0 1.4 collective-permute-start.23
  267.5 3.1 copy-done.2
  270.6 1.5 copy-done.9
  272.1 1.5 copy-done.14
  273.6 4.4 %shard_map.86.refs_9_ = f32[1024,256]{1,0:T(8,128)S(1)} custom-call(s32[1]{0:T(128)} %bitcast.11.refs_0_, bf16[3584,256]{1,0:T(8,128)(2,1)S(1)} %copy-done.5, bf16[3584,256]{1,0:T(8,128)(2,1)} %collective-permute-done.1.refs_4_.refs_2_, bf16[3584,256]{1,0:T(8,128)(2,1)} %collective-permute-done.19.refs_7_.refs_8_.refs_3_.refs_4_, ...), custom_call_target="tpu_custom_call" | custom-call | flops 18790480 | bytes 91750 | tf_op jit(solution)/shard_map/pallas_call | solution.py:205
  278.0 5.0 %shard_map.87.refs_15_ = f32[1024,256]{1,0:T(8,128)S(1)} custom-call(s32[1]{0:T(128)} %bitcast.11.refs_0_, bf16[3584,256]{1,0:T(8,128)(2,1)S(1)} %copy-done.5, bf16[3584,256]{1,0:T(8,128)(2,1)} %collective-permute-done.1.refs_4_.refs_2_, bf16[3584,256]{1,0:T(8,128)(2,1)} %collective-permute-done.19.refs_7_.refs_8_.refs_3_.refs_4_, ...), custom_call_target="tpu_custom_call" | custom-call | flops 18790480 | bytes 91750 | tf_op jit(solution)/shard_map/pallas_call | solution.py:205
  283.1 9.7 %shard_map.84 = f32[1024,256]{1,0:T(8,128)S(1)} custom-call(s32[2]{0:T(128)S(1)} %pad_add_fusion.1.refs_0_, bf16[3584,256]{1,0:T(8,128)(2,1)} %collective-permute-done.13.refs_1_.refs_5_, bf16[3584,256]{1,0:T(8,128)(2,1)} %collective-permute-done.14.refs_2_.refs_6_, bf16[3584,256]{1,0:T(8,128)(2,1)S(1)} %copy-done.5, ...), custom_call_target="tpu_custom_call" | custom-call | flops 37580964 | bytes 183500 | tf_op jit(solution)/shard_map/pallas_call | solution.py:205
  292.8 10.2 %shard_map.85 = f32[1024,256]{1,0:T(8,128)S(1)} custom-call(s32[2]{0:T(128)S(1)} %pad_add_fusion.1.refs_0_, bf16[3584,256]{1,0:T(8,128)(2,1)} %collective-permute-done.13.refs_1_.refs_5_, bf16[3584,256]{1,0:T(8,128)(2,1)} %collective-permute-done.14.refs_2_.refs_6_, bf16[3584,256]{1,0:T(8,128)(2,1)S(1)} %copy-done.5, ...), custom_call_target="tpu_custom_call" | custom-call | flops 37580964 | bytes 183500 | tf_op jit(solution)/shard_map/pallas_call | solution.py:205
  303.3 2.3 collective-permute-start.29
  307.4 1.5 convert_add_fusion
  309.9 5.1 %collective-permute-start.36 = (bf16[16,9216]{1,0:T(8,128)(2,1)}, bf16[16,9216]{1,0:T(8,128)(2,1)}, u32[]{:S(2)}, u32[]{:S(2)}) collective-permute-start(bf16[16,9216]{1,0:T(8,128)(2,1)} %get-tuple-element.108), channel_id=1, source_target_pairs={{0,24},{2,26},{4,28},{6,30},{8,16},{10,18},{12,20},{14,22},{16,8},... | collective-permute-start | bytes 884744 | tf_op jit(solution)/shard_map/ppermute | solution.py:447
  316.0 5.4 %collective-permute-start.35 = (bf16[16,9216]{1,0:T(8,128)(2,1)}, bf16[16,9216]{1,0:T(8,128)(2,1)}, u32[]{:S(2)}, u32[]{:S(2)}) collective-permute-start(bf16[16,9216]{1,0:T(8,128)(2,1)} %get-tuple-element.109), channel_id=1, source_target_pairs={{0,16},{2,18},{4,20},{6,22},{8,24},{10,26},{12,28},{14,30},{16,0},... | collective-permute-start | bytes 884744 | tf_op jit(solution)/shard_map/ppermute | solution.py:447
  321.5 1.7 add_convert_fusion
  323.3 1.6 add_convert_fusion.1
  326.6 2.1 collective-permute-start.24
  328.8 6.3 %shard_map.88 = bf16[1024,256]{1,0:T(8,128)(2,1)S(1)} custom-call(s32[1]{0:T(128)} %bitcast.10.refs_0_, bf16[3584,256]{1,0:T(8,128)(2,1)} %collective-permute-done.3.refs_1_.refs_9_, bf16[3584,256]{1,0:T(8,128)(2,1)} %collective-permute-done.4.refs_2_.refs_10_, bf16[3584,256]{1,0:T(8,128)(2,1)} %collective-permute-done.28.refs_3_.refs_4_, ...), custom_call_target="tpu_custom_call" | custom-call | flops 18790480 | bytes 91750 | tf_op jit(solution)/shard_map/pallas_call | solution.py:205
  336.0 5.2 %shard_map.89 = bf16[1024,256]{1,0:T(8,128)(2,1)S(1)} custom-call(s32[1]{0:T(128)} %bitcast.10.refs_0_, bf16[3584,256]{1,0:T(8,128)(2,1)} %collective-permute-done.3.refs_1_.refs_9_, bf16[3584,256]{1,0:T(8,128)(2,1)} %collective-permute-done.4.refs_2_.refs_10_, bf16[3584,256]{1,0:T(8,128)(2,1)} %collective-permute-done.28.refs_3_.refs_4_, ...), custom_call_target="tpu_custom_call" | custom-call | flops 18790480 | bytes 91750 | tf_op jit(solution)/shard_map/pallas_call | solution.py:205
  343.7 1.5 fusion.2
  346.6 3.8 %collective-permute-done.30.refs_4_ = bf16[512,256]{1,0:T(8,128)(2,1)S(1)} collective-permute-done((bf16[512,256]{1,0:T(8,128)(2,1)S(1)}, bf16[512,256]{1,0:T(8,128)(2,1)S(1)}, u32[]{:S(2)}, u32[]{:S(2)}) %collective-permute-start.30) | collective-permute-done | bytes 262176 | tf_op jit(solution)/shard_map/ppermute | solution.py:577
  350.4 5.6 %collective-permute-done.31.refs_5_ = bf16[512,256]{1,0:T(8,128)(2,1)S(1)} collective-permute-done((bf16[512,256]{1,0:T(8,128)(2,1)S(1)}, bf16[512,256]{1,0:T(8,128)(2,1)S(1)}, u32[]{:S(2)}, u32[]{:S(2)}) %collective-permute-start.31) | collective-permute-done | bytes 262176 | tf_op jit(solution)/shard_map/ppermute | solution.py:577
  356.0 3.6 %shard_map.90 = bf16[512,2048]{1,0:T(8,128)(2,1)} custom-call(s32[8]{0:T(128)S(1)} %stack.35.code, bf16[512,256]{1,0:T(8,128)(2,1)S(1)} %collective-permute-done.24.refs_0_, bf16[512,256]{1,0:T(8,128)(2,1)S(1)} %collective-permute-done.25.refs_1_, bf16[512,256]{1,0:T(8,128)(2,1)S(1)} %collective-permute-done.27.refs_2_, ...), custom_call_target="tpu_custom_call" | custom-call | tf_op jit(solution)/shard_map/pallas_call | solution.py:373
  (191 shorter events, 39.3 us)
Async XLA Ops:
  0.6 109.0 %collective-permute-start.6 = (bf16[512,7168]{1,0:T(8,128)(2,1)}, bf16[512,7168]{1,0:T(8,128)(2,1)}, u32[]{:S(2)}, u32[]{:S(2)}) collective-permute-start(bf16[512,7168]{1,0:T(8,128)(2,1)} %refs_7_.5), channel_id=1, source_target_pairs={{0,2},{2,0},{4,6},{6,4},{8,10},{10,8},{12,14},{14,12},{16,18},{18,... | collective-permute-start | bytes 22020104 | tf_op jit(solution)/shard_map/ppermute | solution.py:485
  0.8 15.4 %copy-start.30 = (bf16[256,7168]{1,0:T(8,128)(2,1)S(1)}, bf16[256,7168]{1,0:T(8,128)(2,1)}, u32[]{:S(2)}) copy-start(bf16[256,7168]{1,0:T(8,128)(2,1)} %adapter_in.1) | copy-start | bytes 11010052
  3.8 12.4 %copy-start.27 = (bf16[512,2048]{1,0:T(8,128)(2,1)S(1)}, bf16[512,2048]{1,0:T(8,128)(2,1)}, u32[]{:S(2)}) copy-start(bf16[512,2048]{1,0:T(8,128)(2,1)} %cotangent.3) | copy-start | bytes 6291460
  3.8 12.4 %copy-start.31 = (bf16[256,2048]{1,0:T(8,128)(2,1)S(1)}, bf16[256,2048]{1,0:T(8,128)(2,1)}, u32[]{:S(2)}) copy-start(bf16[256,2048]{1,0:T(8,128)(2,1)} %adapter_out.1) | copy-start | bytes 3145732
  3.8 45.6 %collective-permute-start = (bf16[3584,256]{1,0:T(8,128)(2,1)}, bf16[3584,256]{1,0:T(8,128)(2,1)S(1)}, u32[]{:S(2)}, u32[]{:S(2)}) collective-permute-start(bf16[3584,256]{1,0:T(8,128)(2,1)} %slice.88), channel_id=1, source_target_pairs={{8,0},{10,2},{12,4},{14,6},{16,8},{18,10},{20,12},{22,14},{24,16},... | collective-permute-start | bytes 5505032 | tf_op jit(solution)/shard_map/ppermute | solution.py:431
  5.3 45.0 %collective-permute-start.1 = (bf16[3584,256]{1,0:T(8,128)(2,1)}, bf16[3584,256]{1,0:T(8,128)(2,1)}, u32[]{:S(2)}, u32[]{:S(2)}) collective-permute-start(bf16[3584,256]{1,0:T(8,128)(2,1)} %slice.88), channel_id=1, source_target_pairs={{0,8},{2,10},{4,12},{6,14},{8,16},{10,18},{12,20},{14,22},{16,24},... | collective-permute-start | bytes 5505032 | tf_op jit(solution)/shard_map/ppermute | solution.py:431
  14.7 41.6 %collective-permute-start.2 = (bf16[128,7168]{1,0:T(8,128)(2,1)}, bf16[128,7168]{1,0:T(8,128)(2,1)}, u32[]{:S(2)}, u32[]{:S(2)}) collective-permute-start(bf16[128,7168]{1,0:T(8,128)(2,1)} %slice.89), channel_id=1, source_target_pairs={{0,4},{2,6},{4,0},{6,2},{8,12},{10,14},{12,8},{14,10},{16,20},{18,... | collective-permute-start | bytes 5505032 | tf_op jit(solution)/shard_map/ppermute | solution.py:436
  25.1 45.6 %collective-permute-start.7 = (f32[512,640]{1,0:T(8,128)S(1)}, f32[512,640]{1,0:T(8,128)}, u32[]{:S(2)}, u32[]{:S(2)}) collective-permute-start(f32[512,640]{1,0:T(8,128)S(1)} %shard_map.76.own), channel_id=1, source_target_pairs={{0,1},{1,0},{2,3},{3,2},{4,5},{5,4},{6,7},{7,6},{8,9},{9,8},{10,11... | collective-permute-start | bytes 3932168 | tf_op jit(solution)/shard_map/ppermute | solution.py:487
  49.3 60.3 %copy-start.3 = (bf16[3584,256]{1,0:T(8,128)(2,1)}, bf16[3584,256]{1,0:T(8,128)(2,1)S(1)}, u32[]{:S(2)}) copy-start(bf16[3584,256]{1,0:T(8,128)(2,1)S(1)} %collective-permute-done.refs_3_.refs_1_) | copy-start | bytes 5505028
  60.1 42.6 %collective-permute-start.3 = (bf16[3584,256]{1,0:T(8,128)(2,1)}, bf16[3584,256]{1,0:T(8,128)(2,1)}, u32[]{:S(2)}, u32[]{:S(2)}) collective-permute-start(bf16[3584,256]{1,0:T(8,128)(2,1)} %get-tuple-element.106), channel_id=1, source_target_pairs={{8,0},{10,2},{12,4},{14,6},{16,8},{18,10},{20,12},{22,14},{24,16},... | collective-permute-start | bytes 5505032 | tf_op jit(solution)/shard_map/ppermute | solution.py:431
  61.3 43.3 %collective-permute-start.4 = (bf16[3584,256]{1,0:T(8,128)(2,1)}, bf16[3584,256]{1,0:T(8,128)(2,1)}, u32[]{:S(2)}, u32[]{:S(2)}) collective-permute-start(bf16[3584,256]{1,0:T(8,128)(2,1)} %get-tuple-element.105), channel_id=1, source_target_pairs={{0,8},{2,10},{4,12},{6,14},{8,16},{10,18},{12,20},{14,22},{16,24},... | collective-permute-start | bytes 5505032 | tf_op jit(solution)/shard_map/ppermute | solution.py:431
  69.4 40.1 %collective-permute-start.5 = (bf16[128,7168]{1,0:T(8,128)(2,1)}, bf16[128,7168]{1,0:T(8,128)(2,1)}, u32[]{:S(2)}, u32[]{:S(2)}) collective-permute-start(bf16[128,7168]{1,0:T(8,128)(2,1)} %slice.91), channel_id=1, source_target_pairs={{0,4},{2,6},{4,0},{6,2},{8,12},{10,14},{12,8},{14,10},{16,20},{18,... | collective-permute-start | bytes 5505032 | tf_op jit(solution)/shard_map/ppermute | solution.py:436
  85.5 42.3 %collective-permute-start.12 = (f32[128,9216]{1,0:T(8,128)S(1)}, f32[128,9216]{1,0:T(8,128)}, u32[]{:S(2)}, u32[]{:S(2)}) collective-permute-start(f32[128,9216]{1,0:T(8,128)S(1)} %get-tuple-element.65), channel_id=1, source_target_pairs={{0,2},{2,0},{4,6},{6,4},{8,10},{10,8},{12,14},{14,12},{16,18},{18,... | collective-permute-start | bytes 14155784 | tf_op jit(solution)/shard_map/ppermute | solution.py:439
  102.6 22.1 %collective-permute-start.11 = (bf16[128,7168]{1,0:T(8,128)(2,1)}, bf16[128,7168]{1,0:T(8,128)(2,1)S(1)}, u32[]{:S(2)}, u32[]{:S(2)}) collective-permute-start(bf16[128,7168]{1,0:T(8,128)(2,1)} %collective-permute-done.2.refs_2_.refs_7_.refs_11_), channel_id=1, source_target_pairs={{0,2},{2,0},{4,6},{6,4},{8,10},{10,8},{12,14},{14,12},{16,18},{18,... | collective-permute-start | bytes 5505032 | tf_op jit(solution)/shard_map/ppermute | solution.py:439
  109.6 7.8 %slice-start = ((s8[7340032]{0:T(1024)(128)(4,1)}), s8[4194304]{0:T(1024)(128)(4,1)S(1)}, s32[]{:S(2)}) async-start(s8[7340032]{0:T(1024)(128)(4,1)} %bitcast.27), calls=%async_computation | async-start | bytes 8388608
  111.0 41.4 %collective-permute-start.8 = (bf16[3584,256]{1,0:T(8,128)(2,1)}, bf16[3584,256]{1,0:T(8,128)(2,1)S(1)}, u32[]{:S(2)}, u32[]{:S(2)}) collective-permute-start(bf16[3584,256]{1,0:T(8,128)(2,1)} %broadcast_select_fusion.5), channel_id=1, source_target_pairs={{8,0},{10,2},{12,4},{14,6},{16,8},{18,10},{20,12},{22,14},{9,1},{1... | collective-permute-start | bytes 5505032 | tf_op jit(solution)/shard_map/ppermute | solution.py:431
  115.5 36.8 %collective-permute-start.9 = (bf16[3584,256]{1,0:T(8,128)(2,1)}, bf16[3584,256]{1,0:T(8,128)(2,1)S(1)}, u32[]{:S(2)}, u32[]{:S(2)}) collective-permute-start(bf16[3584,256]{1,0:T(8,128)(2,1)} %broadcast_select_fusion.2), channel_id=1, source_target_pairs={{8,16},{10,18},{12,20},{14,22},{16,24},{18,26},{20,28},{22,30},{9,... | collective-permute-start | bytes 5505032 | tf_op jit(solution)/shard_map/ppermute | solution.py:431
  116.6 39.1 %collective-permute-start.10 = (bf16[128,7168]{1,0:T(8,128)(2,1)S(1)}, bf16[128,7168]{1,0:T(8,128)(2,1)}, u32[]{:S(2)}, u32[]{:S(2)}) collective-permute-start(bf16[128,7168]{1,0:T(8,128)(2,1)S(1)} %slice.92), channel_id=1, source_target_pairs={{0,4},{2,6},{4,0},{6,2},{8,12},{10,14},{12,8},{14,10},{16,20},{18,... | collective-permute-start | bytes 5505032 | tf_op jit(solution)/shard_map/ppermute | solution.py:436
  124.7 33.8 %copy-start.18 = (bf16[128,7168]{1,0:T(8,128)(2,1)}, bf16[128,7168]{1,0:T(8,128)(2,1)S(1)}, u32[]{:S(2)}) copy-start(bf16[128,7168]{1,0:T(8,128)(2,1)S(1)} %collective-permute-done.11.refs_4_.refs_9_.refs_15_.refs_11_) | copy-start | bytes 5505028
  124.7 64.9 %collective-permute-start.16 = (bf16[128,7168]{1,0:T(8,128)(2,1)}, bf16[128,7168]{1,0:T(8,128)(2,1)}, u32[]{:S(2)}, u32[]{:S(2)}) collective-permute-start(bf16[128,7168]{1,0:T(8,128)(2,1)} %collective-permute-done.5.refs_3_.refs_8_.refs_12_), channel_id=1, source_target_pairs={{0,2},{2,0},{4,6},{6,4},{8,10},{10,8},{12,14},{14,12},{16,18},{18,... | collective-permute-start | bytes 5505032 | tf_op jit(solution)/shard_map/ppermute | solution.py:439
  152.4 7.5 %copy-start.11 = (bf16[3584,256]{1,0:T(8,128)(2,1)}, bf16[3584,256]{1,0:T(8,128)(2,1)S(1)}, u32[]{:S(2)}) copy-start(bf16[3584,256]{1,0:T(8,128)(2,1)S(1)} %collective-permute-done.9.refs_6_) | copy-start | bytes 5505028
  158.5 39.8 %collective-permute-start.13 = (bf16[3584,256]{1,0:T(8,128)(2,1)}, bf16[3584,256]{1,0:T(8,128)(2,1)}, u32[]{:S(2)}, u32[]{:S(2)}) collective-permute-start(bf16[3584,256]{1,0:T(8,128)(2,1)} %broadcast_select_fusion.4), channel_id=1, source_target_pairs={{8,0},{10,2},{12,4},{14,6},{16,8},{18,10},{20,12},{22,14},{9,1},{1... | collective-permute-start | bytes 5505032 | tf_op jit(solution)/shard_map/ppermute | solution.py:431
  162.8 35.5 %collective-permute-start.14 = (bf16[3584,256]{1,0:T(8,128)(2,1)}, bf16[3584,256]{1,0:T(8,128)(2,1)}, u32[]{:S(2)}, u32[]{:S(2)}) collective-permute-start(bf16[3584,256]{1,0:T(8,128)(2,1)} %broadcast_select_fusion.1), channel_id=1, source_target_pairs={{8,16},{10,18},{12,20},{14,22},{16,24},{18,26},{20,28},{22,30},{9,... | collective-permute-start | bytes 5505032 | tf_op jit(solution)/shard_map/ppermute | solution.py:431
  164.7 13.0 %slice-start.2 = ((s8[7340032]{0:T(1024)(128)(4,1)}), s8[3145728]{0:T(1024)(128)(4,1)S(1)}, s32[]{:S(2)}) async-start(s8[7340032]{0:T(1024)(128)(4,1)} %bitcast.29), calls=%async_computation.2 | async-start | bytes 6291456
  166.1 38.3 %collective-permute-start.15 = (bf16[128,7168]{1,0:T(8,128)(2,1)}, bf16[128,7168]{1,0:T(8,128)(2,1)}, u32[]{:S(2)}, u32[]{:S(2)}) collective-permute-start(bf16[128,7168]{1,0:T(8,128)(2,1)} %slice.93), channel_id=1, source_target_pairs={{0,4},{2,6},{4,0},{6,2},{8,12},{10,14},{12,8},{14,10},{16,20},{18,... | collective-permute-start | bytes 5505032 | tf_op jit(solution)/shard_map/ppermute | solution.py:436
  166.5 37.9 %collective-permute-start.17 = (bf16[128,7168]{1,0:T(8,128)(2,1)}, bf16[128,7168]{1,0:T(8,128)(2,1)}, u32[]{:S(2)}, u32[]{:S(2)}) collective-permute-start(bf16[128,7168]{1,0:T(8,128)(2,1)} %collective-permute-done.10.refs_2_.refs_7_.refs_13_.refs_9_), channel_id=1, source_target_pairs={{0,2},{2,0},{4,6},{6,4},{8,10},{10,8},{12,14},{14,12},{16,18},{18,... | collective-permute-start | bytes 5505032 | tf_op jit(solution)/shard_map/ppermute | solution.py:439
  179.5 7.8 %copy-start.23 = (f32[1024,256]{1,0:T(8,128)S(1)}, f32[1024,256]{1,0:T(8,128)}, u32[]{:S(2)}) copy-start(f32[1024,256]{1,0:T(8,128)} %copy-done.22) | copy-start | bytes 3145732
  204.4 24.2 %collective-permute-start.18 = (bf16[128,7168]{1,0:T(8,128)(2,1)}, bf16[128,7168]{1,0:T(8,128)(2,1)}, u32[]{:S(2)}, u32[]{:S(2)}) collective-permute-start(bf16[128,7168]{1,0:T(8,128)(2,1)} %collective-permute-done.15.refs_3_.refs_8_.refs_14_.refs_10_), channel_id=1, source_target_pairs={{0,2},{2,0},{4,6},{6,4},{8,10},{10,8},{12,14},{14,12},{16,18},{18,... | collective-permute-start | bytes 5505032 | tf_op jit(solution)/shard_map/ppermute | solution.py:439
  208.8 9.5 %copy-start.5 = (bf16[3584,256]{1,0:T(8,128)(2,1)S(1)}, bf16[3584,256]{1,0:T(8,128)(2,1)}, u32[]{:S(2)}) copy-start(bf16[3584,256]{1,0:T(8,128)(2,1)} %copy-done.3) | copy-start | bytes 5505028
  208.8 9.5 %copy-start.8 = (bf16[3584,256]{1,0:T(8,128)(2,1)S(1)}, bf16[3584,256]{1,0:T(8,128)(2,1)}, u32[]{:S(2)}) copy-start(bf16[3584,256]{1,0:T(8,128)(2,1)} %copy-done.6) | copy-start | bytes 5505028
  208.8 9.5 %copy-start.13 = (bf16[3584,256]{1,0:T(8,128)(2,1)S(1)}, bf16[3584,256]{1,0:T(8,128)(2,1)}, u32[]{:S(2)}) copy-start(bf16[3584,256]{1,0:T(8,128)(2,1)} %copy-done.11) | copy-start | bytes 5505028
  208.8 9.5 %copy-start.19 = (bf16[128,7168]{1,0:T(8,128)(2,1)S(1)}, bf16[128,7168]{1,0:T(8,128)(2,1)}, u32[]{:S(2)}) copy-start(bf16[128,7168]{1,0:T(8,128)(2,1)} %copy-done.18) | copy-start | bytes 5505028
  213.9 48.4 %collective-permute-start.19 = (bf16[3584,256]{1,0:T(8,128)(2,1)}, bf16[3584,256]{1,0:T(8,128)(2,1)}, u32[]{:S(2)}, u32[]{:S(2)}) collective-permute-start(bf16[3584,256]{1,0:T(8,128)(2,1)} %get-tuple-element.104), channel_id=1, source_target_pairs={{8,0},{10,2},{12,4},{14,6},{16,24},{18,26},{20,28},{22,30},{9,1},{... | collective-permute-start | bytes 5505032 | tf_op jit(solution)/shard_map/ppermute | solution.py:423
  215.3 33.6 %collective-permute-start.20 = (bf16[64,11264]{1,0:T(8,128)(2,1)}, bf16[64,11264]{1,0:T(8,128)(2,1)}, u32[]{:S(2)}, u32[]{:S(2)}) collective-permute-start(bf16[64,11264]{1,0:T(8,128)(2,1)} %pad_maximum_fusion), channel_id=1, source_target_pairs={{0,4},{2,6},{4,0},{6,2},{8,12},{10,14},{12,8},{14,10},{16,20},{18,... | collective-permute-start | bytes 4325384 | tf_op jit(solution)/shard_map/ppermute | solution.py:525
  215.8 26.4 %collective-permute-start.21 = (f32[1024,256]{1,0:T(8,128)}, f32[1024,256]{1,0:T(8,128)}, u32[]{:S(2)}, u32[]{:S(2)}) collective-permute-start(f32[1024,256]{1,0:T(8,128)} %broadcast_select_fusion.7), channel_id=1, source_target_pairs={{0,1},{1,0},{2,3},{3,2},{4,5},{5,4},{6,7},{7,6},{8,9},{9,8},{10,11... | collective-permute-start | bytes 3145736 | tf_op jit(solution)/shard_map/ppermute | solution.py:526
  217.0 86.0 %collective-permute-start.28 = (bf16[3584,256]{1,0:T(8,128)(2,1)}, bf16[3584,256]{1,0:T(8,128)(2,1)}, u32[]{:S(2)}, u32[]{:S(2)}) collective-permute-start(bf16[3584,256]{1,0:T(8,128)(2,1)} %get-tuple-element.103), channel_id=1, source_target_pairs={{8,0},{10,2},{12,4},{14,6},{16,24},{18,26},{20,28},{22,30},{9,1},{... | collective-permute-start | bytes 5505032 | tf_op jit(solution)/shard_map/ppermute | solution.py:423
  228.4 10.2 %copy-start.42 = (f32[256,256]{1,0:T(8,128)}, f32[256,256]{1,0:T(8,128)S(1)}, u32[]{:S(2)}) copy-start(f32[256,256]{1,0:T(8,128)S(1)} %get-tuple-element.122) | copy-start | bytes 786436
  228.5 10.2 %copy-start.44 = (f32[256,256]{1,0:T(8,128)}, f32[256,256]{1,0:T(8,128)S(1)}, u32[]{:S(2)}) copy-start(f32[256,256]{1,0:T(8,128)S(1)} %get-tuple-element.123) | copy-start | bytes 786436
  228.5 10.1 %copy-start.34 = (f32[256,256]{1,0:T(8,128)}, f32[256,256]{1,0:T(8,128)S(1)}, u32[]{:S(2)}) copy-start(f32[256,256]{1,0:T(8,128)S(1)} %get-tuple-element.118) | copy-start | bytes 786436
  228.5 10.1 %copy-start.36 = (f32[256,256]{1,0:T(8,128)}, f32[256,256]{1,0:T(8,128)S(1)}, u32[]{:S(2)}) copy-start(f32[256,256]{1,0:T(8,128)S(1)} %get-tuple-element.119) | copy-start | bytes 786436
  238.6 26.6 %copy-start.38 = (f32[256,256]{1,0:T(8,128)}, f32[256,256]{1,0:T(8,128)S(1)}, u32[]{:S(2)}) copy-start(f32[256,256]{1,0:T(8,128)S(1)} %get-tuple-element.120) | copy-start | bytes 786436
  238.6 26.6 %copy-start.40 = (f32[256,256]{1,0:T(8,128)}, f32[256,256]{1,0:T(8,128)S(1)}, u32[]{:S(2)}) copy-start(f32[256,256]{1,0:T(8,128)S(1)} %get-tuple-element.121) | copy-start | bytes 786436
  239.8 24.4 %collective-permute-start.22 = (f32[1024,256]{1,0:T(8,128)}, f32[1024,256]{1,0:T(8,128)}, u32[]{:S(2)}, u32[]{:S(2)}) collective-permute-start(f32[1024,256]{1,0:T(8,128)} %fusion), channel_id=1, source_target_pairs={{0,1},{1,0},{2,3},{3,2},{4,5},{5,4},{6,7},{7,6},{8,9},{9,8},{10,11... | collective-permute-start | bytes 3145736 | tf_op jit(solution)/shard_map/ppermute | solution.py:541
  266.0 57.2 %collective-permute-start.23 = (bf16[512,256]{1,0:T(8,128)(2,1)}, bf16[512,256]{1,0:T(8,128)(2,1)S(1)}, u32[]{:S(2)}, u32[]{:S(2)}) collective-permute-start(bf16[512,256]{1,0:T(8,128)(2,1)} %reshape.69), channel_id=1, source_target_pairs={{0,2},{2,0},{4,6},{6,4},{8,10},{10,8},{12,14},{14,12},{16,18},{18,... | collective-permute-start | bytes 786440 | tf_op jit(solution)/shard_map/ppermute | solution.py:439
  267.5 48.5 %collective-permute-start.26 = (bf16[512,256]{1,0:T(8,128)(2,1)S(1)}, bf16[512,256]{1,0:T(8,128)(2,1)S(1)}, u32[]{:S(2)}, u32[]{:S(2)}) collective-permute-start(bf16[512,256]{1,0:T(8,128)(2,1)S(1)} %get-tuple-element.96), channel_id=1, source_target_pairs={{0,2},{2,0},{4,6},{6,4},{8,10},{10,8},{12,14},{14,12},{16,18},{18,... | collective-permute-start | bytes 786440 | tf_op jit(solution)/shard_map/ppermute | solution.py:439
  292.8 10.3 %copy-start.43 = (f32[256,256]{1,0:T(8,128)S(1)}, f32[256,256]{1,0:T(8,128)}, u32[]{:S(2)}) copy-start(f32[256,256]{1,0:T(8,128)} %copy-done.42) | copy-start | bytes 786436
  292.8 10.3 %copy-start.45 = (f32[256,256]{1,0:T(8,128)S(1)}, f32[256,256]{1,0:T(8,128)}, u32[]{:S(2)}) copy-start(f32[256,256]{1,0:T(8,128)} %copy-done.44) | copy-start | bytes 786436
  292.8 10.3 %copy-start.47 = (f32[256,256]{1,0:T(8,128)S(1)}, f32[256,256]{1,0:T(8,128)}, u32[]{:S(2)}) copy-start(f32[256,256]{1,0:T(8,128)} %copy-done.46) | copy-start | bytes 786436
  292.8 10.3 %copy-start.49 = (f32[256,256]{1,0:T(8,128)S(1)}, f32[256,256]{1,0:T(8,128)}, u32[]{:S(2)}) copy-start(f32[256,256]{1,0:T(8,128)} %copy-done.48) | copy-start | bytes 786436
  303.3 23.3 %collective-permute-start.29 = (bf16[1024,256]{1,0:T(8,128)(2,1)S(1)}, bf16[1024,256]{1,0:T(8,128)(2,1)S(1)}, u32[]{:S(2)}, u32[]{:S(2)}) collective-permute-start(bf16[1024,256]{1,0:T(8,128)(2,1)S(1)} %select_convert_fusion.1), channel_id=1, source_target_pairs={{0,1},{1,0},{2,3},{3,2},{4,5},{5,4},{6,7},{7,6},{8,9},{9,8},{10,11... | collective-permute-start | bytes 1572872 | tf_op jit(solution)/shard_map/ppermute | solution.py:562
  306.5 28.6 %collective-permute-start.32 = (bf16[1024,256]{1,0:T(8,128)(2,1)}, bf16[1024,256]{1,0:T(8,128)(2,1)S(1)}, u32[]{:S(2)}, u32[]{:S(2)}) collective-permute-start(bf16[1024,256]{1,0:T(8,128)(2,1)} %select_convert_fusion), channel_id=1, source_target_pairs={{0,1},{1,0},{2,3},{3,2},{4,5},{5,4},{6,7},{7,6},{8,9},{9,8},{10,11... | collective-permute-start | bytes 1572872 | tf_op jit(solution)/shard_map/ppermute | solution.py:562
  308.9 14.2 %copy-start.33 = (f32[64,9216]{1,0:T(8,128)}, f32[64,9216]{1,0:T(8,128)S(1)}, u32[]{:S(2)}) copy-start(f32[64,9216]{1,0:T(8,128)S(1)} %convert_add_fusion) | copy-start | bytes 7077892
  309.0 12.5 %copy-start.24 = (f32[1024,256]{1,0:T(8,128)S(1)}, f32[1024,256]{1,0:T(8,128)}, u32[]{:S(2)}) copy-start(f32[1024,256]{1,0:T(8,128)} %copy-done.22) | copy-start | bytes 3145732
  309.9 31.4 %collective-permute-start.36 = (bf16[16,9216]{1,0:T(8,128)(2,1)}, bf16[16,9216]{1,0:T(8,128)(2,1)}, u32[]{:S(2)}, u32[]{:S(2)}) collective-permute-start(bf16[16,9216]{1,0:T(8,128)(2,1)} %get-tuple-element.108), channel_id=1, source_target_pairs={{0,24},{2,26},{4,28},{6,30},{8,16},{10,18},{12,20},{14,22},{16,8},... | collective-permute-start | bytes 884744 | tf_op jit(solution)/shard_map/ppermute | solution.py:447
  316.0 25.4 %collective-permute-start.35 = (bf16[16,9216]{1,0:T(8,128)(2,1)}, bf16[16,9216]{1,0:T(8,128)(2,1)}, u32[]{:S(2)}, u32[]{:S(2)}) collective-permute-start(bf16[16,9216]{1,0:T(8,128)(2,1)} %get-tuple-element.109), channel_id=1, source_target_pairs={{0,16},{2,18},{4,20},{6,22},{8,24},{10,26},{12,28},{14,30},{16,0},... | collective-permute-start | bytes 884744 | tf_op jit(solution)/shard_map/ppermute | solution.py:447
  323.2 19.3 %collective-permute-start.34 = (bf16[16,9216]{1,0:T(8,128)(2,1)}, bf16[16,9216]{1,0:T(8,128)(2,1)}, u32[]{:S(2)}, u32[]{:S(2)}) collective-permute-start(bf16[16,9216]{1,0:T(8,128)(2,1)} %get-tuple-element.107), channel_id=1, source_target_pairs={{0,8},{2,10},{4,12},{6,14},{8,0},{10,2},{12,4},{14,6},{16,24},{18,... | collective-permute-start | bytes 884744 | tf_op jit(solution)/shard_map/ppermute | solution.py:447
  326.6 17.0 %collective-permute-start.24 = (bf16[512,256]{1,0:T(8,128)(2,1)}, bf16[512,256]{1,0:T(8,128)(2,1)S(1)}, u32[]{:S(2)}, u32[]{:S(2)}) collective-permute-start(bf16[512,256]{1,0:T(8,128)(2,1)} %get-tuple-element.117), channel_id=1, source_target_pairs={{0,6},{2,4},{4,2},{6,0},{8,14},{10,12},{12,10},{14,8},{16,22},{18,... | collective-permute-start | bytes 786440 | tf_op jit(solution)/shard_map/ppermute | solution.py:577
  328.8 7.3 %slice-start.4 = ((s8[7340032]{0:T(1024)(128)(4,1)}), s8[4194304]{0:T(1024)(128)(4,1)S(1)}, s32[]{:S(2)}) async-start(s8[7340032]{0:T(1024)(128)(4,1)} %bitcast.31), calls=%async_computation.4 | async-start | bytes 8388608
  328.8 7.3 %slice-start.5 = ((s8[7340032]{0:T(1024)(128)(4,1)}), s8[3145728]{0:T(1024)(128)(4,1)S(1)}, s32[]{:S(2)}) async-start(s8[7340032]{0:T(1024)(128)(4,1)} %bitcast.31), calls=%async_computation.5 | async-start | bytes 6291456
  335.1 11.5 %collective-permute-start.25 = (bf16[512,256]{1,0:T(8,128)(2,1)}, bf16[512,256]{1,0:T(8,128)(2,1)S(1)}, u32[]{:S(2)}, u32[]{:S(2)}) collective-permute-start(bf16[512,256]{1,0:T(8,128)(2,1)} %get-tuple-element.116), channel_id=1, source_target_pairs={{0,4},{2,6},{4,0},{6,2},{8,12},{10,14},{12,8},{14,10},{16,20},{18,... | collective-permute-start | bytes 786440 | tf_op jit(solution)/shard_map/ppermute | solution.py:577
  341.4 5.2 %collective-permute-start.27 = (bf16[512,256]{1,0:T(8,128)(2,1)S(1)}, bf16[512,256]{1,0:T(8,128)(2,1)S(1)}, u32[]{:S(2)}, u32[]{:S(2)}) collective-permute-start(bf16[512,256]{1,0:T(8,128)(2,1)S(1)} %copy-done.51), channel_id=1, source_target_pairs={{0,2},{2,0},{4,6},{6,4},{8,10},{10,8},{12,14},{14,12},{16,18},{18,... | collective-permute-start | bytes 786440 | tf_op jit(solution)/shard_map/ppermute | solution.py:577
  341.5 8.9 %collective-permute-start.30 = (bf16[512,256]{1,0:T(8,128)(2,1)S(1)}, bf16[512,256]{1,0:T(8,128)(2,1)S(1)}, u32[]{:S(2)}, u32[]{:S(2)}) collective-permute-start(bf16[512,256]{1,0:T(8,128)(2,1)S(1)} %get-tuple-element.113), channel_id=1, source_target_pairs={{0,6},{2,4},{4,2},{6,0},{8,14},{10,12},{12,10},{14,8},{16,22},{18,... | collective-permute-start | bytes 786440 | tf_op jit(solution)/shard_map/ppermute | solution.py:577
  342.5 13.5 %collective-permute-start.31 = (bf16[512,256]{1,0:T(8,128)(2,1)S(1)}, bf16[512,256]{1,0:T(8,128)(2,1)S(1)}, u32[]{:S(2)}, u32[]{:S(2)}) collective-permute-start(bf16[512,256]{1,0:T(8,128)(2,1)S(1)} %get-tuple-element.112), channel_id=1, source_target_pairs={{0,4},{2,6},{4,0},{6,2},{8,12},{10,14},{12,8},{14,10},{16,20},{18,... | collective-permute-start | bytes 786440 | tf_op jit(solution)/shard_map/ppermute | solution.py:577
  343.6 12.4 %collective-permute-start.33 = (bf16[512,256]{1,0:T(8,128)(2,1)S(1)}, bf16[512,256]{1,0:T(8,128)(2,1)S(1)}, u32[]{:S(2)}, u32[]{:S(2)}) collective-permute-start(bf16[512,256]{1,0:T(8,128)(2,1)S(1)} %get-tuple-element.111), channel_id=1, source_target_pairs={{0,2},{2,0},{4,6},{6,4},{8,10},{10,8},{12,14},{14,12},{16,18},{18,... | collective-permute-start | bytes 786440 | tf_op jit(solution)/shard_map/ppermute | solution.py:577
  (31 other events, 102.2 us)

commit v3 on v2

--- a/solution.py
+++ b/solution.py
@@ -95,8 +95,9 @@
     code, refs = refs[0], refs[1:]
     weights, refs = refs[: sources[0]], refs[sources[0] :]
     hiddens, refs = refs[: sources[1]], refs[sources[1] :]
-    (base, other, tangent, factor), refs = (refs[:4], refs[4:]) if has_base else ((None,) * 4, refs)
-    out, weight, slots, weight_sem, slot_sems = refs
+    extra, refs = refs[:has_base], refs[has_base:]
+    outs, (weight, slots, weight_sem, slot_sems) = refs[:-4], refs[-4:]
+    out = outs[0]
     first_column = plan[1]
     depth = weight.shape[0]
     step = depth // len(plan[0])
@@ -148,11 +149,27 @@
                     copy.wait()
 
         rows = pl.ds(pl.multiple_of(b * ROWS, ROWS), ROWS)
-        total = jnp.dot(slots[slot], weight[...], preferred_element_type=jnp.float32)
-        if base is not None:
+        if len(extra) == 6:
+            third = jnp.dot(
+                slots[slot, :, :step], weight[:step], preferred_element_type=jnp.float32
+            )
+            outs[2][rows, :] = third
+            total = extra[0][rows, :] + jnp.dot(
+                slots[slot, :, step:], weight[step:], preferred_element_type=jnp.float32
+            )
+        else:
+            total = jnp.dot(slots[slot], weight[...], preferred_element_type=jnp.float32)
+        if len(extra) > 0:
+            other, tangent, factor = extra[-3:]
             term = jnp.dot(tangent[rows, :], factor[...], preferred_element_type=jnp.float32)
-            total = total + base[rows, :] + other[rows, :].astype(jnp.float32)
-            total = total + jnp.float32(adapter_scale) * term
+            term = other[rows, :].astype(jnp.float32) + jnp.float32(adapter_scale) * term
+        if len(extra) == 6:
+            gives = code[len(plan[0])] == 1
+            first, own = extra[1][rows, :], extra[2][rows, :]
+            outs[1][rows, :] = (jnp.where(gives, own, total) + term).astype(outs[1].dtype)
+            total = jnp.where(gives, total, first)
+        elif len(extra) == 4:
+            total = total + extra[0][rows, :] + term
         out[rows, :] = total.astype(out.dtype)
         for number in range(2, len(blocks)):
 
@@ -200,20 +217,23 @@
         (tuple(candidates), first_column),
         (len(weights), len(hiddens)),
         blocks,
-        len(extra) > 0,
-    )
+        len(extra),
+    )
+    shape = jax.ShapeDtypeStruct((height, columns), dtype)
+    shapes = (shape, shape, jax.ShapeDtypeStruct((height, columns), jnp.float32))
+    several = len(extra) == 6
     return pl.pallas_call(
         kernel,
-        out_shape=jax.ShapeDtypeStruct((height, columns), dtype),
+        out_shape=shapes if several else shape,
         in_specs=in_specs,
-        out_specs=whole,
+        out_specs=(whole,) * 3 if several else whole,
         scratch_shapes=[
             pltpu.VMEM((depth, columns), jnp.bfloat16),
             pltpu.VMEM((2, ROWS, depth), jnp.bfloat16),
             pltpu.SemaphoreType.DMA((len(chunks),)),
             pltpu.SemaphoreType.DMA((2,)),
         ],
-        compiler_params=pltpu.CompilerParams(vmem_limit_bytes=32 * 2**20),
+        compiler_params=pltpu.CompilerParams(vmem_limit_bytes=40 * 2**20),
         cost_estimate=pl.CostEstimate(
             flops=int(2 * height * depth * columns * COST),
             bytes_accessed=int(2 * depth * (height + columns) * COST),
@@ -542,24 +562,23 @@
         jnp.where(early, first_sums[1], own_sums[1]), "tensor", pair_swap
     )
 
-    window(4, "sent", "kept", *[("far", i) for i in range(parts)], ("y", 0), ("y", 1), ("t", 0))
+    far = held.all("x", range(parts)) + held.all("far", range(parts))
+    groups = (near, far)
+    second = [streams(3, 0, 2)]
+    for h in range(2):
+        held["half", h] = product(second_code[:1], rows, second, groups[h])
     width = held["kept"].shape[1]
     held["t", 2] = held["sent"][:, width:].reshape(tokens, -1)
+    held["mine"] = held["kept"] + held["sent"][:, :width].astype(jnp.float32)
+    held["mine"] = held["mine"].reshape(LINE, share, -1)
+
+    window(4, "mine", ("t", 2), ("far", 3), ("y", 0), ("y", 1), ("t", 0), ("half", 0), ("half", 1))
     for m in (0, 2):
         held["t", m + 1] = held["t", m]
         over_core(("t", m + 1))
-    held["mine"] = held["kept"] + held["sent"][:, :width].astype(jnp.float32)
-    held["mine"] = held["mine"].reshape(LINE, share, -1)
     for k in (1, 2, 3):
         send_sums(k)
-    far = held.all("x", range(parts)) + held.all("far", range(parts))
-    groups = (near, far)
-    second = [streams(3 + q, q, 2 + q) for q in range(HALVES)]
-    third = [streams(q, 4 + q, 2 + q) for q in range(HALVES)]
-    for h in (1, 0):
-        held["second sum", h] = product(second_code, rows, second, groups[h])
-        sent = jnp.where(early, held["second sum", h], first_sums[h])
-        held["w", h] = lax.ppermute(sent.astype(jnp.bfloat16), "tensor", pair_swap)
+    mixed = [streams(0, 4, 2), streams(4, 1, 3)]
     parity = (z % 2) ^ inner_late.astype(jnp.int32)
     blocks = [(parity ^ turn) * GROUP for turn in range(2)]
     factors = [
@@ -578,13 +597,18 @@
             places.append(blocks[turn] + (member ^ m))
             pieces.append(piece)
 
+    group_tangents = [jnp.concatenate(held.all("t", numbers[h])) for h in range(2)]
+    mixed_code = jnp.concatenate([third_code[0], second_code[1:], early.astype(jnp.int32)[None]])
     for h in (1, 0):
-        held["third sum", h] = product(third_code[0], rows, third[:1], groups[h])
-    group_tangents = [jnp.concatenate(held.all("t", numbers[h])) for h in range(2)]
+        extra = (
+            held["half", h], first_sums[h], own_sums[h], held["y", h], group_tangents[h], factors[0]
+        )
+        held["w", h], held["total", h], held["third sum", h] = product(
+            mixed_code, rows, mixed, groups[h], extra=extra, dtype=jnp.bfloat16
+        )
+        held["w", h] = lax.ppermute(held["w", h], "tensor", pair_swap)
     for h in (1, 0):
-        total = jnp.where(early, own_sums[h], held["second sum", h]) + held["y", h]
-        total = total + scale * dot32(group_tangents[h], factors[0])
-        give_out(0, h, total.astype(jnp.bfloat16))
+        give_out(0, h, held["total", h])
 
     window(5, ("third sum", 0), ("third sum", 1))
     for h in (1, 0):

time: 362 us -> 348 us (0.961)
  waiting for transfers between devices: 124 us -> 116 us
  local copies, waits for them, and re-layouts: 40 us -> 35.7 us
    ppermute x2, waiting for transfers between devices: 13.4 us -> 6.29 us  [send_weight(): held['left', s] = held['right', s] = lax.ppermute(sent, 'dp', pairs)]
    ppermute x1, waiting for transfers between devices: 6.71 us -> 0.01 us  [fast_shards(): held['sent'] = lax.ppermute(held['sent'], 'dp', x_swap)]
    ppermute x1, waiting for transfers between devices: 1.86 us -> 8.44 us  [fast_shards(): lax.ppermute(jnp.where(early, first_sums[1], own_sums[1]), 'tensor', pair...]
    unnamed x118 -> x62, local copies, waits for them, and re-layouts: 20.2 us -> 15.9 us
  transfers between devices with their start and end apart: 37 -> 37, of which waited for: 14 -> 13; matrix products, arithmetic and copies ran while one was open for 15% -> 14% of each run, Pallas kernels for 25% -> 27%
where the time goes in v3:
time: 348 us; the launch traced here: 346 us
  waiting for transfers between devices  116 us (33%)
  Pallas kernels  95.3 us (27%)
  starting transfers between devices  67.8 us (19%)
  local copies, waits for them, and re-layouts  35.7 us (10%)
  other arithmetic  29.5 us (8%)
    pallas_call x12, Pallas kernels, product(): pl.pallas_call(kernel, out_shape=shapes if several else shape, in_specs=i...  78 us
    ppermute x8, waiting for transfers between devices, send_weight(): held[name, s] = lax.ppermute(sent, 'dp', line_pairs(sources, sign))  70.3 us
    ppermute x4, waiting for transfers between devices, send_hidden(): held['x', i] = lax.ppermute(held['x', i], 'dp', x_swap)  21.7 us
    ppermute x8, starting transfers between devices, send_weight(): held[name, s] = lax.ppermute(sent, 'dp', line_pairs(sources, sign))  20.3 us
    ppermute x7, starting transfers between devices, over_core(): held[result or name] = lax.ppermute(held[name], 'dp', core_swap)  17.2 us
    unnamed x62, local copies, waits for them, and re-layouts  15.9 us
    select_n x5, other arithmetic, send_weight(): sent = jnp.where(jnp.logical_and(early, z == last), other, sent)  13.9 us
    ppermute x3, starting transfers between devices, send_sums(): held['got', k] = lax.ppermute(sent, 'dp', pairs)  10.8 us
  transfers between devices with their start and end apart: 37, of which 13 were waited for; matrix products, arithmetic and copies ran while one was open for 14% of the time, Pallas kernels for 27%

profile of v3, /device:TPU:1, one launch (start us, length us, event | category | flops | bytes accessed | tf_op | source)
XLA Modules:
  0.0 345.9 jit_solution(2028612930790709202)
XLA Ops:
  0.8 3.0 slice.88
  3.8 1.5 collective-permute-start
  5.3 6.6 %collective-permute-start.1 = (bf16[3584,256]{1,0:T(8,128)(2,1)}, bf16[3584,256]{1,0:T(8,128)(2,1)}, u32[]{:S(2)}, u32[]{:S(2)}) collective-permute-start(bf16[3584,256]{1,0:T(8,128)(2,1)} %slice.88), channel_id=1, source_target_pairs={{0,8},{2,10},{4,12},{6,14},{8,16},{10,18},{12,20},{14,22},{16,24},... | collective-permute-start | bytes 5505032 | tf_op jit(solution)/shard_map/ppermute | solution.py:451
  11.9 2.9 slice.89
  16.1 3.1 copy-done
  19.2 5.8 %shard_map.76.own = f32[512,640]{1,0:T(8,128)S(1)} custom-call(bf16[512,7168]{1,0:T(8,128)(2,1)S(1)} %copy-done, bf16[256,7168]{1,0:T(8,128)(2,1)S(1)} %copy-done.23, bf16[512,2048]{1,0:T(8,128)(2,1)S(1)} %copy-done.18, bf16[256,2048]{1,0:T(8,128)(2,1)S(1)} %copy-done.24), custom_call_target="tpu_custom_call" | custom-call | flops 24159192 | bytes 141557 | tf_op jit(solution)/shard_map/pallas_call | solution.py:280
  26.4 22.9 %collective-permute-done.refs_3_.refs_1_ = bf16[3584,256]{1,0:T(8,128)(2,1)S(1)} collective-permute-done((bf16[3584,256]{1,0:T(8,128)(2,1)}, bf16[3584,256]{1,0:T(8,128)(2,1)S(1)}, u32[]{:S(2)}, u32[]{:S(2)}) %collective-permute-start) | collective-permute-done | bytes 1835040 | tf_op jit(solution)/shard_map/ppermute | solution.py:451
  50.3 6.1 %collective-permute-done.2.refs_7_.refs_2_.refs_11_ = bf16[128,7168]{1,0:T(8,128)(2,1)} collective-permute-done((bf16[128,7168]{1,0:T(8,128)(2,1)}, bf16[128,7168]{1,0:T(8,128)(2,1)}, u32[]{:S(2)}, u32[]{:S(2)}) %collective-permute-start.2) | collective-permute-done | bytes 1835040 | tf_op jit(solution)/shard_map/ppermute | solution.py:456
  56.4 3.6 %broadcast_select_fusion.2 = (bf16[3584,256]{1,0:T(8,128)(2,1)}, bf16[3584,256]{1,0:T(8,128)(2,1)}) fusion(bf16[3584,256]{1,0:T(8,128)(2,1)} %collective-permute-done.1.refs_4_.refs_2_, pred[]{:T(512)S(6)} %and.100, bf16[7168,256]{1,0:T(8,128)(2,1)} %refs_1_.5, bf16[3584,256]{1,0:T(8,128)(2,1)S(1)} %collective-permute-done.refs_3_.refs_1_, pred[]{:T(512)S(6)} %and.99), kind=kLoop, calls=%fused_computation.6 | loop fusion | flops 1835008 | bytes 9175042 | tf_op jit(solution)/shard_map/jit(_where)/select_n | solution.py:449
  61.3 5.2 %collective-permute-start.4 = (bf16[3584,256]{1,0:T(8,128)(2,1)}, bf16[3584,256]{1,0:T(8,128)(2,1)}, u32[]{:S(2)}, u32[]{:S(2)}) collective-permute-start(bf16[3584,256]{1,0:T(8,128)(2,1)} %get-tuple-element.113), channel_id=1, source_target_pairs={{0,8},{2,10},{4,12},{6,14},{8,16},{10,18},{12,20},{14,22},{16,24},... | collective-permute-start | bytes 5505032 | tf_op jit(solution)/shard_map/ppermute | solution.py:451
  66.5 2.9 slice.91
  70.6 3.1 copy-done.1
  73.7 1.6 copy-done.19
  75.3 7.9 %shard_map.77 = (bf16[512,256]{1,0:T(8,128)(2,1)S(1)}, f32[128,9216]{1,0:T(8,128)S(1)}, f32[128,9216]{1,0:T(8,128)S(1)}) custom-call(f32[512,640]{1,0:T(8,128)S(1)} %shard_map.76.own, f32[512,640]{1,0:T(8,128)} %collective-permute-done.7.other, bf16[256,256]{1,0:T(8,128)(2,1)S(1)} %fusion.5.order, bf16[512,7168]{1,0:T(8,128)(2,1)S(1)} %copy-done.1, ...), custom_call_target="tpu_custom_call" | custom-call | flops 24159192 | bytes 188743 | tf_op jit(solution)/shard_map/pallas_call | solution.py:360
  83.2 2.2 copy-done.20
  85.4 2.3 collective-permute-start.12
  87.7 14.9 %collective-permute-done.3.refs_1_.refs_7_ = bf16[3584,256]{1,0:T(8,128)(2,1)} collective-permute-done((bf16[3584,256]{1,0:T(8,128)(2,1)}, bf16[3584,256]{1,0:T(8,128)(2,1)}, u32[]{:S(2)}, u32[]{:S(2)}) %collective-permute-start.3) | collective-permute-done | bytes 1835040 | tf_op jit(solution)/shard_map/ppermute | solution.py:451
  102.6 2.1 collective-permute-start.11
  104.6 4.9 %collective-permute-done.5.refs_8_.refs_3_.refs_12_ = bf16[128,7168]{1,0:T(8,128)(2,1)} collective-permute-done((bf16[128,7168]{1,0:T(8,128)(2,1)}, bf16[128,7168]{1,0:T(8,128)(2,1)}, u32[]{:S(2)}, u32[]{:S(2)}) %collective-permute-start.5) | collective-permute-done | bytes 1835040 | tf_op jit(solution)/shard_map/ppermute | solution.py:456
  109.6 1.4 broadcast_select_fusion.4
  111.0 1.5 collective-permute-start.8
  112.5 3.0 broadcast_select_fusion.1
  118.5 6.2 %shard_map.78.refs_15_ = f32[1024,256]{1,0:T(8,128)S(1)} custom-call(s32[1]{0:T(128)} %constant.117.clone.1.refs_0_, bf16[7168,256]{1,0:T(8,128)(2,1)S(1)} %copy-done.9, bf16[512,7168]{1,0:T(8,128)(2,1)S(1)} %bitcast.27, bf16[512,7168]{1,0:T(8,128)(2,1)} %collective-permute-done.6.refs_3_.refs_8_.refs_12_), custom_call_target="tpu_custom_call" | custom-call | flops 37580964 | bytes 183500 | tf_op jit(solution)/shard_map/pallas_call | solution.py:225
  124.8 3.3 collective-permute-start.16
  128.0 24.3 %collective-permute-done.8.refs_5_ = bf16[3584,256]{1,0:T(8,128)(2,1)S(1)} collective-permute-done((bf16[3584,256]{1,0:T(8,128)(2,1)}, bf16[3584,256]{1,0:T(8,128)(2,1)S(1)}, u32[]{:S(2)}, u32[]{:S(2)}) %collective-permute-start.8) | collective-permute-done | bytes 1835040 | tf_op jit(solution)/shard_map/ppermute | solution.py:451
  152.4 4.7 %collective-permute-done.10.refs_7_.refs_2_.refs_9_.refs_13_ = bf16[128,7168]{1,0:T(8,128)(2,1)} collective-permute-done((bf16[128,7168]{1,0:T(8,128)(2,1)}, bf16[128,7168]{1,0:T(8,128)(2,1)}, u32[]{:S(2)}, u32[]{:S(2)}) %collective-permute-start.10) | collective-permute-done | bytes 1835040 | tf_op jit(solution)/shard_map/ppermute | solution.py:456
  157.0 2.9 broadcast_select_fusion.3
  161.2 2.9 broadcast_select_fusion
  164.1 2.0 collective-permute-start.14
  166.1 1.4 slice.93
  167.9 4.1 %collective-permute-start.17 = (bf16[128,7168]{1,0:T(8,128)(2,1)}, bf16[128,7168]{1,0:T(8,128)(2,1)}, u32[]{:S(2)}, u32[]{:S(2)}) collective-permute-start(bf16[128,7168]{1,0:T(8,128)(2,1)} %collective-permute-done.10.refs_7_.refs_2_.refs_9_.refs_13_), channel_id=1, source_target_pairs={{0,2},{2,0},{4,6},{6,4},{8,10},{10,8},{12,14},{14,12},{16,18},{18,... | collective-permute-start | bytes 5505032 | tf_op jit(solution)/shard_map/ppermute | solution.py:459
  174.0 4.3 %add.139 = f32[128,9216]{1,0:T(8,128)S(1)} add(f32[128,9216]{1,0:T(8,128)} %copy-done.20, f32[128,9216]{1,0:T(8,128)} %collective-permute-done.12) | non-fusion elementwise | flops 1179648 | bytes 14155776 | tf_op jit(solution)/shard_map/add | solution.py:534
  180.6 8.6 %shard_map.79.refs_14_ = f32[1024,256]{1,0:T(8,128)S(1)} custom-call(s32[2]{0:T(128)S(1)} %pad_add_fusion.1.refs_0_, bf16[3584,256]{1,0:T(8,128)(2,1)} %collective-permute-done.3.refs_1_.refs_7_, bf16[3584,256]{1,0:T(8,128)(2,1)} %collective-permute-done.4.refs_2_.refs_8_, bf16[3584,256]{1,0:T(8,128)(2,1)S(1)} %collective-permute-done.refs_3_.refs_1_, ...), custom_call_target="tpu_custom_call" | custom-call | flops 37580964 | bytes 183500 | tf_op jit(solution)/shard_map/pallas_call | solution.py:225
  192.5 7.3 %collective-permute-done.13.refs_1_.refs_9_.refs_5_ = bf16[3584,256]{1,0:T(8,128)(2,1)} collective-permute-done((bf16[3584,256]{1,0:T(8,128)(2,1)}, bf16[3584,256]{1,0:T(8,128)(2,1)}, u32[]{:S(2)}, u32[]{:S(2)}) %collective-permute-start.13) | collective-permute-done | bytes 1835040 | tf_op jit(solution)/shard_map/ppermute | solution.py:451
  199.8 6.0 %collective-permute-done.15.refs_8_.refs_3_.refs_10_.refs_14_ = bf16[128,7168]{1,0:T(8,128)(2,1)} collective-permute-done((bf16[128,7168]{1,0:T(8,128)(2,1)}, bf16[128,7168]{1,0:T(8,128)(2,1)}, u32[]{:S(2)}, u32[]{:S(2)}) %collective-permute-start.15) | collective-permute-done | bytes 1835040 | tf_op jit(solution)/shard_map/ppermute | solution.py:456
  205.8 4.5 %collective-permute-start.20 = (bf16[128,7168]{1,0:T(8,128)(2,1)}, bf16[128,7168]{1,0:T(8,128)(2,1)S(1)}, u32[]{:S(2)}, u32[]{:S(2)}) collective-permute-start(bf16[128,7168]{1,0:T(8,128)(2,1)} %collective-permute-done.15.refs_8_.refs_3_.refs_10_.refs_14_), channel_id=1, source_target_pairs={{0,2},{2,0},{4,6},{6,4},{8,10},{10,8},{12,14},{14,12},{16,18},{18,... | collective-permute-start | bytes 5505032 | tf_op jit(solution)/shard_map/ppermute | solution.py:459
  210.8 3.9 %slice_select_fusion = (bf16[3584,256]{1,0:T(8,128)(2,1)}, bf16[3584,256]{1,0:T(8,128)(2,1)}) fusion(bf16[7168,256]{1,0:T(8,128)(2,1)S(1)} %copy-done.10, pred[]{:T(512)S(6)} %and.98, bf16[3584,256]{1,0:T(8,128)(2,1)} %collective-permute-done.13.refs_1_.refs_9_.refs_5_, bf16[3584,256]{1,0:T(8,128)(2,1)} %collective-permute-done.14.refs_2_.refs_10_.refs_6_, ...), kind=kLoop, calls=%fused_computation.2 | loop fusion | flops 3670016 | bytes 12845058 | tf_op jit(solution)/shard_map/jit(_where)/select_n | solution.py:441
  217.1 1.5 collective-permute-start.28
  218.6 4.3 %shard_map.82 = f32[512,256]{1,0:T(8,128)S(1)} custom-call(s32[1]{0:T(128)} %constant.117.clone.1.refs_0_, bf16[7168,256]{1,0:T(8,128)(2,1)S(1)} %copy-done.10, bf16[128,7168]{1,0:T(8,128)(2,1)} %collective-permute-done.2.refs_7_.refs_2_.refs_11_, bf16[128,7168]{1,0:T(8,128)(2,1)} %collective-permute-done.5.refs_8_.refs_3_.refs_12_, ...), custom_call_target="tpu_custom_call" | custom-call | flops 18790480 | bytes 110100 | tf_op jit(solution)/shard_map/pallas_call | solution.py:225
  222.9 5.4 %shard_map.80 = f32[512,256]{1,0:T(8,128)S(1)} custom-call(s32[2]{0:T(128)S(1)} %pad_add_fusion.1.refs_0_, bf16[3584,256]{1,0:T(8,128)(2,1)} %collective-permute-done.3.refs_1_.refs_7_, bf16[3584,256]{1,0:T(8,128)(2,1)} %collective-permute-done.4.refs_2_.refs_8_, bf16[3584,256]{1,0:T(8,128)(2,1)S(1)} %collective-permute-done.refs_3_.refs_1_, ...), custom_call_target="tpu_custom_call" | custom-call | flops 18790480 | bytes 110100 | tf_op jit(solution)/shard_map/pallas_call | solution.py:225
  228.3 5.5 %shard_map.84.refs_13_ = f32[1024,256]{1,0:T(8,128)S(1)} custom-call(s32[1]{0:T(128)} %bitcast.9.refs_0_, bf16[3584,256]{1,0:T(8,128)(2,1)} %collective-permute-done.13.refs_1_.refs_9_.refs_5_, bf16[3584,256]{1,0:T(8,128)(2,1)} %collective-permute-done.14.refs_2_.refs_10_.refs_6_, bf16[3584,256]{1,0:T(8,128)(2,1)S(1)} %collective-permute-done.refs_3_.refs_1_, ...), custom_call_target="tpu_custom_call" | custom-call | flops 18790480 | bytes 91750 | tf_op jit(solution)/shard_map/pallas_call | solution.py:225
  233.9 5.0 %shard_map.83 = f32[512,256]{1,0:T(8,128)S(1)} custom-call(s32[1]{0:T(128)} %constant.117.clone.1.refs_0_, bf16[7168,256]{1,0:T(8,128)(2,1)S(1)} %copy-done.10, bf16[128,7168]{1,0:T(8,128)(2,1)} %collective-permute-done.10.refs_7_.refs_2_.refs_9_.refs_13_, bf16[128,7168]{1,0:T(8,128)(2,1)} %collective-permute-done.15.refs_8_.refs_3_.refs_10_.refs_14_, ...), custom_call_target="tpu_custom_call" | custom-call | flops 18790480 | bytes 110100 | tf_op jit(solution)/shard_map/pallas_call | solution.py:225
  238.9 5.4 %shard_map.81 = f32[512,256]{1,0:T(8,128)S(1)} custom-call(s32[2]{0:T(128)S(1)} %pad_add_fusion.1.refs_0_, bf16[3584,256]{1,0:T(8,128)(2,1)} %collective-permute-done.3.refs_1_.refs_7_, bf16[3584,256]{1,0:T(8,128)(2,1)} %collective-permute-done.4.refs_2_.refs_8_, bf16[3584,256]{1,0:T(8,128)(2,1)S(1)} %collective-permute-done.refs_3_.refs_1_, ...), custom_call_target="tpu_custom_call" | custom-call | flops 18790480 | bytes 110100 | tf_op jit(solution)/shard_map/pallas_call | solution.py:225
  244.4 1.8 pad_maximum_fusion.2
  246.2 2.0 collective-permute-start.22
  248.2 3.0 convert_add_fusion
  251.1 1.7 slice.120
  252.8 1.8 reshape.70
  254.6 1.5 copy-done.4
  256.1 1.5 copy-done.8
  257.6 5.5 %shard_map.85.refs_19_ = f32[1024,256]{1,0:T(8,128)S(1)} custom-call(s32[1]{0:T(128)} %bitcast.9.refs_0_, bf16[3584,256]{1,0:T(8,128)(2,1)} %collective-permute-done.13.refs_1_.refs_9_.refs_5_, bf16[3584,256]{1,0:T(8,128)(2,1)} %collective-permute-done.14.refs_2_.refs_10_.refs_6_, bf16[3584,256]{1,0:T(8,128)(2,1)S(1)} %collective-permute-done.refs_3_.refs_1_, ...), custom_call_target="tpu_custom_call" | custom-call | flops 18790480 | bytes 91750 | tf_op jit(solution)/shard_map/pallas_call | solution.py:225
  263.2 8.4 %collective-permute-done.22.refs_22_ = f32[1024,256]{1,0:T(8,128)} collective-permute-done((f32[1024,256]{1,0:T(8,128)}, f32[1024,256]{1,0:T(8,128)}, u32[]{:S(2)}, u32[]{:S(2)}) %collective-permute-start.22) | collective-permute-done | bytes 1048608 | tf_op jit(solution)/shard_map/ppermute | solution.py:561
  273.4 5.1 %collective-permute-start.36 = (bf16[16,9216]{1,0:T(8,128)(2,1)}, bf16[16,9216]{1,0:T(8,128)(2,1)S(1)}, u32[]{:S(2)}, u32[]{:S(2)}) collective-permute-start(bf16[16,9216]{1,0:T(8,128)(2,1)} %get-tuple-element.116), channel_id=1, source_target_pairs={{0,24},{2,26},{4,28},{6,30},{8,16},{10,18},{12,20},{14,22},{16,8},... | collective-permute-start | bytes 884744 | tf_op jit(solution)/shard_map/ppermute | solution.py:467
  278.5 5.7 %collective-permute-start.35 = (bf16[16,9216]{1,0:T(8,128)(2,1)S(1)}, bf16[16,9216]{1,0:T(8,128)(2,1)S(1)}, u32[]{:S(2)}, u32[]{:S(2)}) collective-permute-start(bf16[16,9216]{1,0:T(8,128)(2,1)S(1)} %get-tuple-element.117), channel_id=1, source_target_pairs={{0,16},{2,18},{4,20},{6,22},{8,24},{10,26},{12,28},{14,30},{16,0},... | collective-permute-start | bytes 884744 | tf_op jit(solution)/shard_map/ppermute | solution.py:467
  284.4 10.2 %shard_map.86 = (bf16[1024,256]{1,0:T(8,128)(2,1)S(1)}, bf16[1024,256]{1,0:T(8,128)(2,1)S(1)}, f32[1024,256]{1,0:T(8,128)S(1)}) custom-call(s32[3]{0:T(128)S(1)} %pad_add_fusion.refs_0_, bf16[3584,256]{1,0:T(8,128)(2,1)S(1)} %collective-permute-done.refs_3_.refs_1_, bf16[3584,256]{1,0:T(8,128)(2,1)} %collective-permute-done.1.refs_4_.refs_2_, ...), custom_call_target="tpu_custom_call" | custom-call | flops 37580964 | bytes 183500 | tf_op jit(solution)/shard_map/pallas_call | solution.py:225
  294.6 2.5 collective-permute-start.29
  297.2 10.6 %shard_map.87 = (bf16[1024,256]{1,0:T(8,128)(2,1)S(1)}, bf16[1024,256]{1,0:T(8,128)(2,1)S(1)}, f32[1024,256]{1,0:T(8,128)S(1)}) custom-call(s32[3]{0:T(128)S(1)} %pad_add_fusion.refs_0_, bf16[3584,256]{1,0:T(8,128)(2,1)S(1)} %collective-permute-done.refs_3_.refs_1_, bf16[3584,256]{1,0:T(8,128)(2,1)} %collective-permute-done.1.refs_4_.refs_2_, ...), custom_call_target="tpu_custom_call" | custom-call | flops 37580964 | bytes 183500 | tf_op jit(solution)/shard_map/pallas_call | solution.py:225
  308.4 6.3 %collective-permute-done.28.refs_3_.refs_4_ = bf16[3584,256]{1,0:T(8,128)(2,1)} collective-permute-done((bf16[3584,256]{1,0:T(8,128)(2,1)}, bf16[3584,256]{1,0:T(8,128)(2,1)}, u32[]{:S(2)}, u32[]{:S(2)}) %collective-permute-start.28) | collective-permute-done | bytes 1835040 | tf_op jit(solution)/shard_map/ppermute | solution.py:443
  314.7 1.4 collective-permute-start.24
  316.2 5.6 %shard_map.88 = bf16[1024,256]{1,0:T(8,128)(2,1)S(1)} custom-call(s32[1]{0:T(128)} %bitcast.13.refs_0_, bf16[3584,256]{1,0:T(8,128)(2,1)} %collective-permute-done.3.refs_1_.refs_7_, bf16[3584,256]{1,0:T(8,128)(2,1)} %collective-permute-done.4.refs_2_.refs_8_, bf16[3584,256]{1,0:T(8,128)(2,1)} %collective-permute-done.28.refs_3_.refs_4_, ...), custom_call_target="tpu_custom_call" | custom-call | flops 18790480 | bytes 91750 | tf_op jit(solution)/shard_map/pallas_call | solution.py:225
  322.7 5.6 %shard_map.89 = bf16[1024,256]{1,0:T(8,128)(2,1)S(1)} custom-call(s32[1]{0:T(128)} %bitcast.13.refs_0_, bf16[3584,256]{1,0:T(8,128)(2,1)} %collective-permute-done.3.refs_1_.refs_7_, bf16[3584,256]{1,0:T(8,128)(2,1)} %collective-permute-done.4.refs_2_.refs_8_, bf16[3584,256]{1,0:T(8,128)(2,1)} %collective-permute-done.28.refs_3_.refs_4_, ...), custom_call_target="tpu_custom_call" | custom-call | flops 18790480 | bytes 91750 | tf_op jit(solution)/shard_map/pallas_call | solution.py:225
  332.7 4.8 %collective-permute-done.30.refs_4_ = bf16[512,256]{1,0:T(8,128)(2,1)S(1)} collective-permute-done((bf16[512,256]{1,0:T(8,128)(2,1)S(1)}, bf16[512,256]{1,0:T(8,128)(2,1)S(1)}, u32[]{:S(2)}, u32[]{:S(2)}) %collective-permute-start.30) | collective-permute-done | bytes 262176 | tf_op jit(solution)/shard_map/ppermute | solution.py:596
  337.5 4.8 %collective-permute-done.31.refs_5_ = bf16[512,256]{1,0:T(8,128)(2,1)S(1)} collective-permute-done((bf16[512,256]{1,0:T(8,128)(2,1)S(1)}, bf16[512,256]{1,0:T(8,128)(2,1)S(1)}, u32[]{:S(2)}, u32[]{:S(2)}) %collective-permute-start.31) | collective-permute-done | bytes 262176 | tf_op jit(solution)/shard_map/ppermute | solution.py:596
  342.3 3.6 %shard_map.90 = bf16[512,2048]{1,0:T(8,128)(2,1)} custom-call(s32[8]{0:T(128)S(1)} %stack.35.code, bf16[512,256]{1,0:T(8,128)(2,1)S(1)} %collective-permute-done.24.refs_0_, bf16[512,256]{1,0:T(8,128)(2,1)S(1)} %collective-permute-done.25.refs_1_, bf16[512,256]{1,0:T(8,128)(2,1)S(1)} %collective-permute-done.27.refs_2_, ...), custom_call_target="tpu_custom_call" | custom-call | tf_op jit(solution)/shard_map/pallas_call | solution.py:393
  (129 shorter events, 29.3 us)
Async XLA Ops:
  0.6 108.9 %collective-permute-start.6 = (bf16[512,7168]{1,0:T(8,128)(2,1)}, bf16[512,7168]{1,0:T(8,128)(2,1)}, u32[]{:S(2)}, u32[]{:S(2)}) collective-permute-start(bf16[512,7168]{1,0:T(8,128)(2,1)} %refs_7_.5), channel_id=1, source_target_pairs={{0,2},{2,0},{4,6},{6,4},{8,10},{10,8},{12,14},{14,12},{16,18},{18,... | collective-permute-start | bytes 22020104 | tf_op jit(solution)/shard_map/ppermute | solution.py:505
  0.8 15.4 %copy-start.23 = (bf16[256,7168]{1,0:T(8,128)(2,1)S(1)}, bf16[256,7168]{1,0:T(8,128)(2,1)}, u32[]{:S(2)}) copy-start(bf16[256,7168]{1,0:T(8,128)(2,1)} %adapter_in.1) | copy-start | bytes 11010052
  3.8 12.4 %copy-start.18 = (bf16[512,2048]{1,0:T(8,128)(2,1)S(1)}, bf16[512,2048]{1,0:T(8,128)(2,1)}, u32[]{:S(2)}) copy-start(bf16[512,2048]{1,0:T(8,128)(2,1)} %cotangent.3) | copy-start | bytes 6291460
  3.8 12.4 %copy-start.24 = (bf16[256,2048]{1,0:T(8,128)(2,1)S(1)}, bf16[256,2048]{1,0:T(8,128)(2,1)}, u32[]{:S(2)}) copy-start(bf16[256,2048]{1,0:T(8,128)(2,1)} %adapter_out.1) | copy-start | bytes 3145732
  3.8 45.6 %collective-permute-start = (bf16[3584,256]{1,0:T(8,128)(2,1)}, bf16[3584,256]{1,0:T(8,128)(2,1)S(1)}, u32[]{:S(2)}, u32[]{:S(2)}) collective-permute-start(bf16[3584,256]{1,0:T(8,128)(2,1)} %slice.88), channel_id=1, source_target_pairs={{8,0},{10,2},{12,4},{14,6},{16,8},{18,10},{20,12},{22,14},{24,16},... | collective-permute-start | bytes 5505032 | tf_op jit(solution)/shard_map/ppermute | solution.py:451
  5.3 45.0 %collective-permute-start.1 = (bf16[3584,256]{1,0:T(8,128)(2,1)}, bf16[3584,256]{1,0:T(8,128)(2,1)}, u32[]{:S(2)}, u32[]{:S(2)}) collective-permute-start(bf16[3584,256]{1,0:T(8,128)(2,1)} %slice.88), channel_id=1, source_target_pairs={{0,8},{2,10},{4,12},{6,14},{8,16},{10,18},{12,20},{14,22},{16,24},... | collective-permute-start | bytes 5505032 | tf_op jit(solution)/shard_map/ppermute | solution.py:451
  14.8 41.6 %collective-permute-start.2 = (bf16[128,7168]{1,0:T(8,128)(2,1)}, bf16[128,7168]{1,0:T(8,128)(2,1)}, u32[]{:S(2)}, u32[]{:S(2)}) collective-permute-start(bf16[128,7168]{1,0:T(8,128)(2,1)} %slice.89), channel_id=1, source_target_pairs={{0,4},{2,6},{4,0},{6,2},{8,12},{10,14},{12,8},{14,10},{16,20},{18,... | collective-permute-start | bytes 5505032 | tf_op jit(solution)/shard_map/ppermute | solution.py:456
  16.1 3.1 copy-start
  25.1 45.5 %collective-permute-start.7 = (f32[512,640]{1,0:T(8,128)S(1)}, f32[512,640]{1,0:T(8,128)}, u32[]{:S(2)}, u32[]{:S(2)}) collective-permute-start(f32[512,640]{1,0:T(8,128)S(1)} %shard_map.76.own), channel_id=1, source_target_pairs={{0,1},{1,0},{2,3},{3,2},{4,5},{5,4},{6,7},{7,6},{8,9},{9,8},{10,11... | collective-permute-start | bytes 3932168 | tf_op jit(solution)/shard_map/ppermute | solution.py:507
  60.0 42.6 %collective-permute-start.3 = (bf16[3584,256]{1,0:T(8,128)(2,1)}, bf16[3584,256]{1,0:T(8,128)(2,1)}, u32[]{:S(2)}, u32[]{:S(2)}) collective-permute-start(bf16[3584,256]{1,0:T(8,128)(2,1)} %get-tuple-element.114), channel_id=1, source_target_pairs={{8,0},{10,2},{12,4},{14,6},{16,8},{18,10},{20,12},{22,14},{24,16},... | collective-permute-start | bytes 5505032 | tf_op jit(solution)/shard_map/ppermute | solution.py:451
  61.3 43.3 %collective-permute-start.4 = (bf16[3584,256]{1,0:T(8,128)(2,1)}, bf16[3584,256]{1,0:T(8,128)(2,1)}, u32[]{:S(2)}, u32[]{:S(2)}) collective-permute-start(bf16[3584,256]{1,0:T(8,128)(2,1)} %get-tuple-element.113), channel_id=1, source_target_pairs={{0,8},{2,10},{4,12},{6,14},{8,16},{10,18},{12,20},{14,22},{16,24},... | collective-permute-start | bytes 5505032 | tf_op jit(solution)/shard_map/ppermute | solution.py:451
  69.4 40.1 %collective-permute-start.5 = (bf16[128,7168]{1,0:T(8,128)(2,1)}, bf16[128,7168]{1,0:T(8,128)(2,1)}, u32[]{:S(2)}, u32[]{:S(2)}) collective-permute-start(bf16[128,7168]{1,0:T(8,128)(2,1)} %slice.91), channel_id=1, source_target_pairs={{0,4},{2,6},{4,0},{6,2},{8,12},{10,14},{12,8},{14,10},{16,20},{18,... | collective-permute-start | bytes 5505032 | tf_op jit(solution)/shard_map/ppermute | solution.py:456
  70.6 3.1 copy-start.1
  73.7 1.6 copy-start.19
  83.2 2.2 copy-start.20
  85.4 42.6 %collective-permute-start.12 = (f32[128,9216]{1,0:T(8,128)S(1)}, f32[128,9216]{1,0:T(8,128)}, u32[]{:S(2)}, u32[]{:S(2)}) collective-permute-start(f32[128,9216]{1,0:T(8,128)S(1)} %get-tuple-element.68), channel_id=1, source_target_pairs={{0,2},{2,0},{4,6},{6,4},{8,10},{10,8},{12,14},{14,12},{16,18},{18,... | collective-permute-start | bytes 14155784 | tf_op jit(solution)/shard_map/ppermute | solution.py:459
  102.6 22.2 %collective-permute-start.11 = (bf16[128,7168]{1,0:T(8,128)(2,1)}, bf16[128,7168]{1,0:T(8,128)(2,1)S(1)}, u32[]{:S(2)}, u32[]{:S(2)}) collective-permute-start(bf16[128,7168]{1,0:T(8,128)(2,1)} %collective-permute-done.2.refs_7_.refs_2_.refs_11_), channel_id=1, source_target_pairs={{0,2},{2,0},{4,6},{6,4},{8,10},{10,8},{12,14},{14,12},{16,18},{18,... | collective-permute-start | bytes 5505032 | tf_op jit(solution)/shard_map/ppermute | solution.py:459
  109.6 9.0 %slice-start = ((s8[7340032]{0:T(1024)(128)(4,1)}), s8[4194304]{0:T(1024)(128)(4,1)S(1)}, s32[]{:S(2)}) async-start(s8[7340032]{0:T(1024)(128)(4,1)} %bitcast.26), calls=%async_computation | async-start | bytes 8388608
  111.0 7.5 %slice-start.1 = ((s8[7340032]{0:T(1024)(128)(4,1)}), s8[3145728]{0:T(1024)(128)(4,1)S(1)}, s32[]{:S(2)}) async-start(s8[7340032]{0:T(1024)(128)(4,1)} %bitcast.26), calls=%async_computation.1 | async-start | bytes 6291456
  111.0 41.4 %collective-permute-start.8 = (bf16[3584,256]{1,0:T(8,128)(2,1)}, bf16[3584,256]{1,0:T(8,128)(2,1)S(1)}, u32[]{:S(2)}, u32[]{:S(2)}) collective-permute-start(bf16[3584,256]{1,0:T(8,128)(2,1)} %broadcast_select_fusion.4), channel_id=1, source_target_pairs={{8,0},{10,2},{12,4},{14,6},{16,8},{18,10},{20,12},{22,14},{9,1},{1... | collective-permute-start | bytes 5505032 | tf_op jit(solution)/shard_map/ppermute | solution.py:451
  115.6 3.0 copy-start.9
  115.6 36.8 %collective-permute-start.9 = (bf16[3584,256]{1,0:T(8,128)(2,1)}, bf16[3584,256]{1,0:T(8,128)(2,1)S(1)}, u32[]{:S(2)}, u32[]{:S(2)}) collective-permute-start(bf16[3584,256]{1,0:T(8,128)(2,1)} %broadcast_select_fusion.1), channel_id=1, source_target_pairs={{8,16},{10,18},{12,20},{14,22},{16,24},{18,26},{20,28},{22,30},{9,... | collective-permute-start | bytes 5505032 | tf_op jit(solution)/shard_map/ppermute | solution.py:451
  117.8 39.2 %collective-permute-start.10 = (bf16[128,7168]{1,0:T(8,128)(2,1)}, bf16[128,7168]{1,0:T(8,128)(2,1)}, u32[]{:S(2)}, u32[]{:S(2)}) collective-permute-start(bf16[128,7168]{1,0:T(8,128)(2,1)} %slice.92), channel_id=1, source_target_pairs={{0,4},{2,6},{4,0},{6,2},{8,12},{10,14},{12,8},{14,10},{16,20},{18,... | collective-permute-start | bytes 5505032 | tf_op jit(solution)/shard_map/ppermute | solution.py:456
  124.8 35.2 %copy-start.11 = (bf16[128,7168]{1,0:T(8,128)(2,1)}, bf16[128,7168]{1,0:T(8,128)(2,1)S(1)}, u32[]{:S(2)}) copy-start(bf16[128,7168]{1,0:T(8,128)(2,1)S(1)} %collective-permute-done.11.refs_9_.refs_4_.refs_11_.refs_15_) | copy-start | bytes 5505028
  124.8 67.8 %collective-permute-start.16 = (bf16[128,7168]{1,0:T(8,128)(2,1)}, bf16[128,7168]{1,0:T(8,128)(2,1)}, u32[]{:S(2)}, u32[]{:S(2)}) collective-permute-start(bf16[128,7168]{1,0:T(8,128)(2,1)} %collective-permute-done.5.refs_8_.refs_3_.refs_12_), channel_id=1, source_target_pairs={{0,2},{2,0},{4,6},{6,4},{8,10},{10,8},{12,14},{14,12},{16,18},{18,... | collective-permute-start | bytes 5505032 | tf_op jit(solution)/shard_map/ppermute | solution.py:459
  152.3 7.6 %copy-start.2 = (bf16[3584,256]{1,0:T(8,128)(2,1)}, bf16[3584,256]{1,0:T(8,128)(2,1)S(1)}, u32[]{:S(2)}) copy-start(bf16[3584,256]{1,0:T(8,128)(2,1)S(1)} %collective-permute-done.8.refs_5_) | copy-start | bytes 5505028
  152.3 8.9 %copy-start.6 = (bf16[3584,256]{1,0:T(8,128)(2,1)}, bf16[3584,256]{1,0:T(8,128)(2,1)S(1)}, u32[]{:S(2)}) copy-start(bf16[3584,256]{1,0:T(8,128)(2,1)S(1)} %collective-permute-done.9.refs_6_) | copy-start | bytes 5505028
  159.9 39.9 %collective-permute-start.13 = (bf16[3584,256]{1,0:T(8,128)(2,1)}, bf16[3584,256]{1,0:T(8,128)(2,1)}, u32[]{:S(2)}, u32[]{:S(2)}) collective-permute-start(bf16[3584,256]{1,0:T(8,128)(2,1)} %broadcast_select_fusion.3), channel_id=1, source_target_pairs={{8,0},{10,2},{12,4},{14,6},{16,8},{18,10},{20,12},{22,14},{9,1},{1... | collective-permute-start | bytes 5505032 | tf_op jit(solution)/shard_map/ppermute | solution.py:451
  164.1 35.7 %collective-permute-start.14 = (bf16[3584,256]{1,0:T(8,128)(2,1)}, bf16[3584,256]{1,0:T(8,128)(2,1)}, u32[]{:S(2)}, u32[]{:S(2)}) collective-permute-start(bf16[3584,256]{1,0:T(8,128)(2,1)} %broadcast_select_fusion), channel_id=1, source_target_pairs={{8,16},{10,18},{12,20},{14,22},{16,24},{18,26},{20,28},{22,30},{9,... | collective-permute-start | bytes 5505032 | tf_op jit(solution)/shard_map/ppermute | solution.py:451
  167.5 38.3 %collective-permute-start.15 = (bf16[128,7168]{1,0:T(8,128)(2,1)}, bf16[128,7168]{1,0:T(8,128)(2,1)}, u32[]{:S(2)}, u32[]{:S(2)}) collective-permute-start(bf16[128,7168]{1,0:T(8,128)(2,1)} %slice.93), channel_id=1, source_target_pairs={{0,4},{2,6},{4,0},{6,2},{8,12},{10,14},{12,8},{14,10},{16,20},{18,... | collective-permute-start | bytes 5505032 | tf_op jit(solution)/shard_map/ppermute | solution.py:456
  167.9 37.9 %collective-permute-start.17 = (bf16[128,7168]{1,0:T(8,128)(2,1)}, bf16[128,7168]{1,0:T(8,128)(2,1)}, u32[]{:S(2)}, u32[]{:S(2)}) collective-permute-start(bf16[128,7168]{1,0:T(8,128)(2,1)} %collective-permute-done.10.refs_7_.refs_2_.refs_9_.refs_13_), channel_id=1, source_target_pairs={{0,2},{2,0},{4,6},{6,4},{8,10},{10,8},{12,14},{14,12},{16,18},{18,... | collective-permute-start | bytes 5505032 | tf_op jit(solution)/shard_map/ppermute | solution.py:459
  178.5 1.5 copy-start.3
  178.5 2.0 copy-start.7
  180.6 10.8 %copy-start.27 = (bf16[64,2048]{1,0:T(8,128)(2,1)S(1)}, bf16[64,2048]{1,0:T(8,128)(2,1)}, u32[]{:S(2)}) copy-start(bf16[64,2048]{1,0:T(8,128)(2,1)} %reshape.68) | copy-start | bytes 786436
  189.2 3.3 copy-start.16
  189.2 21.5 %copy-start.10 = (bf16[7168,256]{1,0:T(8,128)(2,1)S(1)}, bf16[7168,256]{1,0:T(8,128)(2,1)}, u32[]{:S(2)}) copy-start(bf16[7168,256]{1,0:T(8,128)(2,1)} %refs_1_.5) | copy-start | bytes 11010052
  205.8 28.1 %collective-permute-start.20 = (bf16[128,7168]{1,0:T(8,128)(2,1)}, bf16[128,7168]{1,0:T(8,128)(2,1)S(1)}, u32[]{:S(2)}, u32[]{:S(2)}) collective-permute-start(bf16[128,7168]{1,0:T(8,128)(2,1)} %collective-permute-done.15.refs_8_.refs_3_.refs_10_.refs_14_), channel_id=1, source_target_pairs={{0,2},{2,0},{4,6},{6,4},{8,10},{10,8},{12,14},{14,12},{16,18},{18,... | collective-permute-start | bytes 5505032 | tf_op jit(solution)/shard_map/ppermute | solution.py:459
  210.3 8.2 %copy-start.12 = (bf16[128,7168]{1,0:T(8,128)(2,1)S(1)}, bf16[128,7168]{1,0:T(8,128)(2,1)}, u32[]{:S(2)}) copy-start(bf16[128,7168]{1,0:T(8,128)(2,1)} %copy-done.11) | copy-start | bytes 5505028
  210.3 37.9 %collective-permute-start.19 = (bf16[64,11264]{1,0:T(8,128)(2,1)}, bf16[64,11264]{1,0:T(8,128)(2,1)}, u32[]{:S(2)}, u32[]{:S(2)}) collective-permute-start(bf16[64,11264]{1,0:T(8,128)(2,1)} %pad_maximum_fusion), channel_id=1, source_target_pairs={{0,4},{2,6},{4,0},{6,2},{8,12},{10,14},{12,8},{14,10},{16,20},{18,... | collective-permute-start | bytes 4325384 | tf_op jit(solution)/shard_map/ppermute | solution.py:545
  214.6 48.6 %collective-permute-start.18 = (bf16[3584,256]{1,0:T(8,128)(2,1)}, bf16[3584,256]{1,0:T(8,128)(2,1)}, u32[]{:S(2)}, u32[]{:S(2)}) collective-permute-start(bf16[3584,256]{1,0:T(8,128)(2,1)} %get-tuple-element.112), channel_id=1, source_target_pairs={{8,0},{10,2},{12,4},{14,6},{16,24},{18,26},{20,28},{22,30},{9,1},{... | collective-permute-start | bytes 5505032 | tf_op jit(solution)/shard_map/ppermute | solution.py:443
  215.9 47.3 %collective-permute-start.21 = (f32[1024,256]{1,0:T(8,128)}, f32[1024,256]{1,0:T(8,128)}, u32[]{:S(2)}, u32[]{:S(2)}) collective-permute-start(f32[1024,256]{1,0:T(8,128)} %broadcast_select_fusion.8), channel_id=1, source_target_pairs={{0,1},{1,0},{2,3},{3,2},{4,5},{5,4},{6,7},{7,6},{8,9},{9,8},{10,11... | collective-permute-start | bytes 3145736 | tf_op jit(solution)/shard_map/ppermute | solution.py:546
  217.1 97.6 %collective-permute-start.28 = (bf16[3584,256]{1,0:T(8,128)(2,1)}, bf16[3584,256]{1,0:T(8,128)(2,1)}, u32[]{:S(2)}, u32[]{:S(2)}) collective-permute-start(bf16[3584,256]{1,0:T(8,128)(2,1)} %get-tuple-element.111), channel_id=1, source_target_pairs={{8,0},{10,2},{12,4},{14,6},{16,24},{18,26},{20,28},{22,30},{9,1},{... | collective-permute-start | bytes 5505032 | tf_op jit(solution)/shard_map/ppermute | solution.py:443
  233.9 5.0 %copy-start.13 = (bf16[128,7168]{1,0:T(8,128)(2,1)}, bf16[128,7168]{1,0:T(8,128)(2,1)S(1)}, u32[]{:S(2)}) copy-start(bf16[128,7168]{1,0:T(8,128)(2,1)S(1)} %collective-permute-done.20.refs_10_.refs_5_.refs_14_.refs_18_) | copy-start | bytes 5505028
  246.2 25.5 %collective-permute-start.22 = (f32[1024,256]{1,0:T(8,128)}, f32[1024,256]{1,0:T(8,128)}, u32[]{:S(2)}, u32[]{:S(2)}) collective-permute-start(f32[1024,256]{1,0:T(8,128)} %get-tuple-element.121), channel_id=1, source_target_pairs={{0,1},{1,0},{2,3},{3,2},{4,5},{5,4},{6,7},{7,6},{8,9},{9,8},{10,11... | collective-permute-start | bytes 3145736 | tf_op jit(solution)/shard_map/ppermute | solution.py:561
  257.6 14.0 %copy-start.26 = (bf16[512,256]{1,0:T(8,128)(2,1)S(1)}, bf16[512,256]{1,0:T(8,128)(2,1)}, u32[]{:S(2)}) copy-start(bf16[512,256]{1,0:T(8,128)(2,1)} %reshape.70) | copy-start | bytes 786436
  257.6 15.0 %copy-start.25 = (f32[64,9216]{1,0:T(8,128)S(1)}, f32[64,9216]{1,0:T(8,128)}, u32[]{:S(2)}) copy-start(f32[64,9216]{1,0:T(8,128)} %convert_add_fusion) | copy-start | bytes 7077892
  257.6 26.7 %copy-start.22 = (f32[1024,256]{1,0:T(8,128)S(1)}, f32[1024,256]{1,0:T(8,128)}, u32[]{:S(2)}) copy-start(f32[1024,256]{1,0:T(8,128)} %get-tuple-element.122.refs_20_) | copy-start | bytes 3145732
  263.2 21.2 %copy-start.5 = (bf16[3584,256]{1,0:T(8,128)(2,1)S(1)}, bf16[3584,256]{1,0:T(8,128)(2,1)}, u32[]{:S(2)}) copy-start(bf16[3584,256]{1,0:T(8,128)(2,1)} %copy-done.2) | copy-start | bytes 5505028
  263.2 21.2 %copy-start.21 = (f32[1024,256]{1,0:T(8,128)S(1)}, f32[1024,256]{1,0:T(8,128)}, u32[]{:S(2)}) copy-start(f32[1024,256]{1,0:T(8,128)} %get-tuple-element.120.refs_21_) | copy-start | bytes 3145732
  271.6 12.6 %collective-permute-start.23 = (bf16[512,256]{1,0:T(8,128)(2,1)S(1)}, bf16[512,256]{1,0:T(8,128)(2,1)S(1)}, u32[]{:S(2)}, u32[]{:S(2)}) collective-permute-start(bf16[512,256]{1,0:T(8,128)(2,1)S(1)} %copy-done.26), channel_id=1, source_target_pairs={{0,2},{2,0},{4,6},{6,4},{8,10},{10,8},{12,14},{14,12},{16,18},{18,... | collective-permute-start | bytes 786440 | tf_op jit(solution)/shard_map/ppermute | solution.py:459
  272.6 24.5 %collective-permute-start.26 = (bf16[512,256]{1,0:T(8,128)(2,1)S(1)}, bf16[512,256]{1,0:T(8,128)(2,1)S(1)}, u32[]{:S(2)}, u32[]{:S(2)}) collective-permute-start(bf16[512,256]{1,0:T(8,128)(2,1)S(1)} %get-tuple-element.100), channel_id=1, source_target_pairs={{0,2},{2,0},{4,6},{6,4},{8,10},{10,8},{12,14},{14,12},{16,18},{18,... | collective-permute-start | bytes 786440 | tf_op jit(solution)/shard_map/ppermute | solution.py:459
  273.4 54.9 %collective-permute-start.36 = (bf16[16,9216]{1,0:T(8,128)(2,1)}, bf16[16,9216]{1,0:T(8,128)(2,1)S(1)}, u32[]{:S(2)}, u32[]{:S(2)}) collective-permute-start(bf16[16,9216]{1,0:T(8,128)(2,1)} %get-tuple-element.116), channel_id=1, source_target_pairs={{0,24},{2,26},{4,28},{6,30},{8,16},{10,18},{12,20},{14,22},{16,8},... | collective-permute-start | bytes 884744 | tf_op jit(solution)/shard_map/ppermute | solution.py:467
  278.5 50.4 %collective-permute-start.35 = (bf16[16,9216]{1,0:T(8,128)(2,1)S(1)}, bf16[16,9216]{1,0:T(8,128)(2,1)S(1)}, u32[]{:S(2)}, u32[]{:S(2)}) collective-permute-start(bf16[16,9216]{1,0:T(8,128)(2,1)S(1)} %get-tuple-element.117), channel_id=1, source_target_pairs={{0,16},{2,18},{4,20},{6,22},{8,24},{10,26},{12,28},{14,30},{16,0},... | collective-permute-start | bytes 884744 | tf_op jit(solution)/shard_map/ppermute | solution.py:467
  284.4 12.8 %copy-start.15 = (f32[1024,256]{1,0:T(8,128)S(1)}, f32[1024,256]{1,0:T(8,128)}, u32[]{:S(2)}) copy-start(f32[1024,256]{1,0:T(8,128)} %copy-done.14) | copy-start | bytes 3145732
  284.4 12.8 %copy-start.17 = (f32[1024,256]{1,0:T(8,128)S(1)}, f32[1024,256]{1,0:T(8,128)}, u32[]{:S(2)}) copy-start(f32[1024,256]{1,0:T(8,128)} %copy-done.16) | copy-start | bytes 3145732
  294.6 20.1 %collective-permute-start.29 = (bf16[1024,256]{1,0:T(8,128)(2,1)S(1)}, bf16[1024,256]{1,0:T(8,128)(2,1)S(1)}, u32[]{:S(2)}, u32[]{:S(2)}) collective-permute-start(bf16[1024,256]{1,0:T(8,128)(2,1)S(1)} %get-tuple-element.107), channel_id=1, source_target_pairs={{0,1},{1,0},{2,3},{3,2},{4,5},{5,4},{6,7},{7,6},{8,9},{9,8},{10,11... | collective-permute-start | bytes 1572872 | tf_op jit(solution)/shard_map/ppermute | solution.py:609
  307.8 14.0 %collective-permute-start.32 = (bf16[1024,256]{1,0:T(8,128)(2,1)S(1)}, bf16[1024,256]{1,0:T(8,128)(2,1)S(1)}, u32[]{:S(2)}, u32[]{:S(2)}) collective-permute-start(bf16[1024,256]{1,0:T(8,128)(2,1)S(1)} %get-tuple-element.109), channel_id=1, source_target_pairs={{0,1},{1,0},{2,3},{3,2},{4,5},{5,4},{6,7},{7,6},{8,9},{9,8},{10,11... | collective-permute-start | bytes 1572872 | tf_op jit(solution)/shard_map/ppermute | solution.py:609
  314.7 15.0 %collective-permute-start.34 = (bf16[16,9216]{1,0:T(8,128)(2,1)S(1)}, bf16[16,9216]{1,0:T(8,128)(2,1)S(1)}, u32[]{:S(2)}, u32[]{:S(2)}) collective-permute-start(bf16[16,9216]{1,0:T(8,128)(2,1)S(1)} %get-tuple-element.115), channel_id=1, source_target_pairs={{0,8},{2,10},{4,12},{6,14},{8,0},{10,2},{12,4},{14,6},{16,24},{18,... | collective-permute-start | bytes 884744 | tf_op jit(solution)/shard_map/ppermute | solution.py:467
  314.7 15.6 %collective-permute-start.24 = (bf16[512,256]{1,0:T(8,128)(2,1)S(1)}, bf16[512,256]{1,0:T(8,128)(2,1)S(1)}, u32[]{:S(2)}, u32[]{:S(2)}) collective-permute-start(bf16[512,256]{1,0:T(8,128)(2,1)S(1)} %get-tuple-element.130), channel_id=1, source_target_pairs={{0,6},{2,4},{4,2},{6,0},{8,14},{10,12},{12,10},{14,8},{16,22},{18,... | collective-permute-start | bytes 786440 | tf_op jit(solution)/shard_map/ppermute | solution.py:596
  321.8 10.9 %collective-permute-start.25 = (bf16[512,256]{1,0:T(8,128)(2,1)S(1)}, bf16[512,256]{1,0:T(8,128)(2,1)S(1)}, u32[]{:S(2)}, u32[]{:S(2)}) collective-permute-start(bf16[512,256]{1,0:T(8,128)(2,1)S(1)} %get-tuple-element.129), channel_id=1, source_target_pairs={{0,4},{2,6},{4,0},{6,2},{8,12},{10,14},{12,8},{14,10},{16,20},{18,... | collective-permute-start | bytes 786440 | tf_op jit(solution)/shard_map/ppermute | solution.py:596
  328.4 4.3 %collective-permute-start.27 = (bf16[512,256]{1,0:T(8,128)(2,1)S(1)}, bf16[512,256]{1,0:T(8,128)(2,1)S(1)}, u32[]{:S(2)}, u32[]{:S(2)}) collective-permute-start(bf16[512,256]{1,0:T(8,128)(2,1)S(1)} %get-tuple-element.128), channel_id=1, source_target_pairs={{0,2},{2,0},{4,6},{6,4},{8,10},{10,8},{12,14},{14,12},{16,18},{18,... | collective-permute-start | bytes 786440 | tf_op jit(solution)/shard_map/ppermute | solution.py:596
  328.9 8.6 %collective-permute-start.30 = (bf16[512,256]{1,0:T(8,128)(2,1)S(1)}, bf16[512,256]{1,0:T(8,128)(2,1)S(1)}, u32[]{:S(2)}, u32[]{:S(2)}) collective-permute-start(bf16[512,256]{1,0:T(8,128)(2,1)S(1)} %get-tuple-element.126), channel_id=1, source_target_pairs={{0,6},{2,4},{4,2},{6,0},{8,14},{10,12},{12,10},{14,8},{16,22},{18,... | collective-permute-start | bytes 786440 | tf_op jit(solution)/shard_map/ppermute | solution.py:596
  329.7 12.6 %collective-permute-start.31 = (bf16[512,256]{1,0:T(8,128)(2,1)S(1)}, bf16[512,256]{1,0:T(8,128)(2,1)S(1)}, u32[]{:S(2)}, u32[]{:S(2)}) collective-permute-start(bf16[512,256]{1,0:T(8,128)(2,1)S(1)} %get-tuple-element.125), channel_id=1, source_target_pairs={{0,4},{2,6},{4,0},{6,2},{8,12},{10,14},{12,8},{14,10},{16,20},{18,... | collective-permute-start | bytes 786440 | tf_op jit(solution)/shard_map/ppermute | solution.py:596
  330.4 11.9 %collective-permute-start.33 = (bf16[512,256]{1,0:T(8,128)(2,1)S(1)}, bf16[512,256]{1,0:T(8,128)(2,1)S(1)}, u32[]{:S(2)}, u32[]{:S(2)}) collective-permute-start(bf16[512,256]{1,0:T(8,128)(2,1)S(1)} %get-tuple-element.124), channel_id=1, source_target_pairs={{0,2},{2,0},{4,6},{6,4},{8,10},{10,8},{12,14},{14,12},{16,18},{18,... | collective-permute-start | bytes 786440 | tf_op jit(solution)/shard_map/ppermute | solution.py:596
  (3 other events, 4.0 us)

commit v4 on v3

--- a/solution.py
+++ b/solution.py
@@ -451,9 +451,9 @@
             held[name, s] = lax.ppermute(sent, "dp", line_pairs(sources, sign))
 
     def send_hidden(i):
-        if i:
-            held["x", i] = held["hidden"][i * step : (i + 1) * step]
         held["x", i] = lax.ppermute(held["x", i], "dp", x_swap)
+        if i + 1 < parts:
+            held["x", i + 1] = held["hidden"][(i + 1) * step : (i + 2) * step]
 
     def over_core(name, result=None):
         held[result or name] = lax.ppermute(held[name], "dp", core_swap)
@@ -513,21 +513,21 @@
     column = (row // share % LINE) * (GROUP * share) + owner * share + row % share
     held["order"] = (column[:, None] == jnp.arange(rank)[None, :]).astype(jnp.bfloat16)
 
-    window(0, ("x", 0), "hidden")
+    window(0, ("x", 0), ("x", 1), "hidden")
     send_hidden(1)
     held["t", 0], held["sent"], held["kept"] = gradients(
         held["shared"], held["shared other"], held["order"], feature_count, hidden, cotangent
     )
     over_core("sent")
 
-    window(1, ("x", 1), "hidden", "core", "kept", ("t", 0))
+    window(1, ("x", 1), ("x", 2), "hidden", "core", "kept", ("t", 0))
     send_hidden(2)
     pass_hidden(0)
     near = [hidden, held["core"]]
     whole_weight = [[(base_weight, 0)]]
     held["own sum", 0] = product(none, depth, whole_weight, near)
 
-    window(2, ("x", 2), "hidden", ("far", 0), "sent", "kept", ("own sum", 0))
+    window(2, ("x", 2), ("x", 3), ("far", 0), "sent", "kept", ("own sum", 0))
     send_hidden(3)
     pass_hidden(1)
     pass_hidden(2)

time: 348 us -> 344 us (0.989)
    ppermute x4, waiting for transfers between devices: 21.7 us -> 16.3 us  [send_hidden(): held['x', i] = lax.ppermute(held['x', i], 'dp', x_swap)]
    ppermute x8, waiting for transfers between devices: 70.3 us -> 73.8 us  [send_weight(): held[name, s] = lax.ppermute(sent, 'dp', line_pairs(sources, sign))]
  transfers between devices with their start and end apart: 37 -> 37, of which waited for: 13 -> 14; matrix products, arithmetic and copies ran while one was open for 14% -> 14% of each run, Pallas kernels for 27% -> 27%
where the time goes in v4:
time: 344 us; the launch traced here: 342 us
  waiting for transfers between devices  115 us (33%)
  Pallas kernels  95.3 us (28%)
  starting transfers between devices  68.6 us (20%)
  local copies, waits for them, and re-layouts  33.1 us (10%)
  other arithmetic  29.6 us (9%)
    pallas_call x12, Pallas kernels, product(): pl.pallas_call(kernel, out_shape=shapes if several else shape, in_specs=i...  78 us
    ppermute x8, waiting for transfers between devices, send_weight(): held[name, s] = lax.ppermute(sent, 'dp', line_pairs(sources, sign))  73.8 us
    ppermute x8, starting transfers between devices, send_weight(): held[name, s] = lax.ppermute(sent, 'dp', line_pairs(sources, sign))  20.1 us
    ppermute x7, starting transfers between devices, over_core(): held[result or name] = lax.ppermute(held[name], 'dp', core_swap)  17.3 us
    ppermute x4, waiting for transfers between devices, send_hidden(): held['x', i] = lax.ppermute(held['x', i], 'dp', x_swap)  16.3 us
    unnamed x62, local copies, waits for them, and re-layouts  14.9 us
    select_n x5, other arithmetic, send_weight(): sent = jnp.where(jnp.logical_and(early, z == last), other, sent)  13.9 us
    ppermute x3, starting transfers between devices, send_sums(): held['got', k] = lax.ppermute(sent, 'dp', pairs)  11.5 us
  transfers between devices with their start and end apart: 37, of which 14 were waited for; matrix products, arithmetic and copies ran while one was open for 14% of the time, Pallas kernels for 27%

profile of v4, /device:TPU:1, one launch (start us, length us, event | category | flops | bytes accessed | tf_op | source)
XLA Modules:
  0.0 342.4 jit_solution(2362823420744989841)
XLA Ops:
  0.8 3.0 slice.88
  5.0 6.6 %collective-permute-start.1 = (bf16[3584,256]{1,0:T(8,128)(2,1)}, bf16[3584,256]{1,0:T(8,128)(2,1)}, u32[]{:S(2)}, u32[]{:S(2)}) collective-permute-start(bf16[3584,256]{1,0:T(8,128)(2,1)} %slice.88), channel_id=1, source_target_pairs={{0,8},{2,10},{4,12},{6,14},{8,16},{10,18},{12,20},{14,22},{16,24},... | collective-permute-start | bytes 5505032 | tf_op jit(solution)/shard_map/ppermute | solution.py:451
  11.6 4.3 %fusion.15 = (bf16[128,7168]{1,0:T(8,128)(2,1)}, bf16[128,7168]{1,0:T(8,128)(2,1)}) fusion(bf16[512,7168]{1,0:T(8,128)(2,1)} %refs_7_.5), kind=kLoop, calls=%fused_computation.58 | loop fusion | bytes 7340032 | tf_op jit(solution)/shard_map/slice | solution.py:456
  15.9 1.4 collective-permute-start.2
  17.3 2.0 copy-done.23
  19.3 5.8 %shard_map.76.own = f32[512,640]{1,0:T(8,128)S(1)} custom-call(bf16[512,7168]{1,0:T(8,128)(2,1)S(1)} %copy-done, bf16[256,7168]{1,0:T(8,128)(2,1)S(1)} %copy-done.23, bf16[512,2048]{1,0:T(8,128)(2,1)S(1)} %copy-done.18, bf16[256,2048]{1,0:T(8,128)(2,1)S(1)} %copy-done.24), custom_call_target="tpu_custom_call" | custom-call | flops 24159192 | bytes 141557 | tf_op jit(solution)/shard_map/pallas_call | solution.py:280
  26.5 22.5 %collective-permute-done.refs_3_.refs_1_ = bf16[3584,256]{1,0:T(8,128)(2,1)S(1)} collective-permute-done((bf16[3584,256]{1,0:T(8,128)(2,1)}, bf16[3584,256]{1,0:T(8,128)(2,1)S(1)}, u32[]{:S(2)}, u32[]{:S(2)}) %collective-permute-start) | collective-permute-done | bytes 1835040 | tf_op jit(solution)/shard_map/ppermute | solution.py:451
  50.0 7.5 %collective-permute-done.2.refs_7_.refs_2_.refs_11_ = bf16[128,7168]{1,0:T(8,128)(2,1)} collective-permute-done((bf16[128,7168]{1,0:T(8,128)(2,1)}, bf16[128,7168]{1,0:T(8,128)(2,1)}, u32[]{:S(2)}, u32[]{:S(2)}) %collective-permute-start.2) | collective-permute-done | bytes 1835040 | tf_op jit(solution)/shard_map/ppermute | solution.py:454
  57.5 3.6 %broadcast_select_fusion.2 = (bf16[3584,256]{1,0:T(8,128)(2,1)}, bf16[3584,256]{1,0:T(8,128)(2,1)}) fusion(bf16[3584,256]{1,0:T(8,128)(2,1)} %collective-permute-done.1.refs_4_.refs_2_, pred[]{:T(512)S(6)} %and.100, bf16[7168,256]{1,0:T(8,128)(2,1)} %refs_1_.5, bf16[3584,256]{1,0:T(8,128)(2,1)S(1)} %collective-permute-done.refs_3_.refs_1_, pred[]{:T(512)S(6)} %and.99), kind=kLoop, calls=%fused_computation.6 | loop fusion | flops 1835008 | bytes 9175042 | tf_op jit(solution)/shard_map/jit(_where)/select_n | solution.py:449
  62.4 5.2 %collective-permute-start.4 = (bf16[3584,256]{1,0:T(8,128)(2,1)}, bf16[3584,256]{1,0:T(8,128)(2,1)}, u32[]{:S(2)}, u32[]{:S(2)}) collective-permute-start(bf16[3584,256]{1,0:T(8,128)(2,1)} %get-tuple-element.119), channel_id=1, source_target_pairs={{0,8},{2,10},{4,12},{6,14},{8,16},{10,18},{12,20},{14,22},{16,24},... | collective-permute-start | bytes 5505032 | tf_op jit(solution)/shard_map/ppermute | solution.py:451
  68.9 3.1 copy-done.1
  72.0 1.6 copy-done.19
  73.6 7.9 %shard_map.77 = (bf16[512,256]{1,0:T(8,128)(2,1)S(1)}, f32[128,9216]{1,0:T(8,128)S(1)}, f32[128,9216]{1,0:T(8,128)S(1)}) custom-call(f32[512,640]{1,0:T(8,128)S(1)} %shard_map.76.own, f32[512,640]{1,0:T(8,128)} %collective-permute-done.7.other, bf16[256,256]{1,0:T(8,128)(2,1)S(1)} %fusion.5.order, bf16[512,7168]{1,0:T(8,128)(2,1)S(1)} %copy-done.1, ...), custom_call_target="tpu_custom_call" | custom-call | flops 24159192 | bytes 188743 | tf_op jit(solution)/shard_map/pallas_call | solution.py:360
  81.5 2.2 copy-done.20
  83.7 2.3 collective-permute-start.12
  86.0 1.4 slice.92
  87.4 16.3 %collective-permute-done.3.refs_1_.refs_7_ = bf16[3584,256]{1,0:T(8,128)(2,1)} collective-permute-done((bf16[3584,256]{1,0:T(8,128)(2,1)}, bf16[3584,256]{1,0:T(8,128)(2,1)}, u32[]{:S(2)}, u32[]{:S(2)}) %collective-permute-start.3) | collective-permute-done | bytes 1835040 | tf_op jit(solution)/shard_map/ppermute | solution.py:451
  103.7 2.1 collective-permute-start.11
  105.8 2.0 collective-permute-done.5.refs_8_.refs_3_.refs_12_
  107.8 1.4 broadcast_select_fusion.4
  109.2 1.5 collective-permute-start.8
  110.8 2.9 broadcast_select_fusion.1
  116.7 6.2 %shard_map.78.refs_15_ = f32[1024,256]{1,0:T(8,128)S(1)} custom-call(s32[1]{0:T(128)} %constant.117.clone.1.refs_0_, bf16[7168,256]{1,0:T(8,128)(2,1)S(1)} %copy-done.9, bf16[512,7168]{1,0:T(8,128)(2,1)S(1)} %bitcast.27, bf16[512,7168]{1,0:T(8,128)(2,1)} %collective-permute-done.6.refs_3_.refs_8_.refs_12_), custom_call_target="tpu_custom_call" | custom-call | flops 37580964 | bytes 183500 | tf_op jit(solution)/shard_map/pallas_call | solution.py:225
  123.0 3.3 collective-permute-start.16
  126.3 24.3 %collective-permute-done.8.refs_5_ = bf16[3584,256]{1,0:T(8,128)(2,1)S(1)} collective-permute-done((bf16[3584,256]{1,0:T(8,128)(2,1)}, bf16[3584,256]{1,0:T(8,128)(2,1)S(1)}, u32[]{:S(2)}, u32[]{:S(2)}) %collective-permute-start.8) | collective-permute-done | bytes 1835040 | tf_op jit(solution)/shard_map/ppermute | solution.py:451
  150.6 3.3 collective-permute-done.10.refs_7_.refs_2_.refs_9_.refs_13_
  153.9 2.9 broadcast_select_fusion.3
  158.1 3.0 broadcast_select_fusion
  161.1 2.0 collective-permute-start.14
  163.5 4.1 %collective-permute-start.17 = (bf16[128,7168]{1,0:T(8,128)(2,1)}, bf16[128,7168]{1,0:T(8,128)(2,1)}, u32[]{:S(2)}, u32[]{:S(2)}) collective-permute-start(bf16[128,7168]{1,0:T(8,128)(2,1)} %collective-permute-done.10.refs_7_.refs_2_.refs_9_.refs_13_), channel_id=1, source_target_pairs={{0,2},{2,0},{4,6},{6,4},{8,10},{10,8},{12,14},{14,12},{16,18},{18,... | collective-permute-start | bytes 5505032 | tf_op jit(solution)/shard_map/ppermute | solution.py:459
  169.6 4.3 %add.139 = f32[128,9216]{1,0:T(8,128)S(1)} add(f32[128,9216]{1,0:T(8,128)} %copy-done.20, f32[128,9216]{1,0:T(8,128)} %collective-permute-done.12) | non-fusion elementwise | flops 1179648 | bytes 14155776 | tf_op jit(solution)/shard_map/add | solution.py:534
  174.3 1.3 copy-done.3
  176.1 8.6 %shard_map.79.refs_14_ = f32[1024,256]{1,0:T(8,128)S(1)} custom-call(s32[2]{0:T(128)S(1)} %pad_add_fusion.1.refs_0_, bf16[3584,256]{1,0:T(8,128)(2,1)} %collective-permute-done.3.refs_1_.refs_7_, bf16[3584,256]{1,0:T(8,128)(2,1)} %collective-permute-done.4.refs_2_.refs_8_, bf16[3584,256]{1,0:T(8,128)(2,1)S(1)} %collective-permute-done.refs_3_.refs_1_, ...), custom_call_target="tpu_custom_call" | custom-call | flops 37580964 | bytes 183500 | tf_op jit(solution)/shard_map/pallas_call | solution.py:225
  188.1 9.7 %collective-permute-done.13.refs_1_.refs_9_.refs_5_ = bf16[3584,256]{1,0:T(8,128)(2,1)} collective-permute-done((bf16[3584,256]{1,0:T(8,128)(2,1)}, bf16[3584,256]{1,0:T(8,128)(2,1)}, u32[]{:S(2)}, u32[]{:S(2)}) %collective-permute-start.13) | collective-permute-done | bytes 1835040 | tf_op jit(solution)/shard_map/ppermute | solution.py:451
  197.8 3.5 %collective-permute-done.15.refs_8_.refs_3_.refs_10_.refs_14_ = bf16[128,7168]{1,0:T(8,128)(2,1)} collective-permute-done((bf16[128,7168]{1,0:T(8,128)(2,1)}, bf16[128,7168]{1,0:T(8,128)(2,1)}, u32[]{:S(2)}, u32[]{:S(2)}) %collective-permute-start.15) | collective-permute-done | bytes 1835040 | tf_op jit(solution)/shard_map/ppermute | solution.py:454
  201.3 4.5 %collective-permute-start.20 = (bf16[128,7168]{1,0:T(8,128)(2,1)}, bf16[128,7168]{1,0:T(8,128)(2,1)S(1)}, u32[]{:S(2)}, u32[]{:S(2)}) collective-permute-start(bf16[128,7168]{1,0:T(8,128)(2,1)} %collective-permute-done.15.refs_8_.refs_3_.refs_10_.refs_14_), channel_id=1, source_target_pairs={{0,2},{2,0},{4,6},{6,4},{8,10},{10,8},{12,14},{14,12},{16,18},{18,... | collective-permute-start | bytes 5505032 | tf_op jit(solution)/shard_map/ppermute | solution.py:459
  206.3 3.9 %slice_select_fusion = (bf16[3584,256]{1,0:T(8,128)(2,1)}, bf16[3584,256]{1,0:T(8,128)(2,1)}) fusion(bf16[7168,256]{1,0:T(8,128)(2,1)S(1)} %copy-done.10, pred[]{:T(512)S(6)} %and.98, bf16[3584,256]{1,0:T(8,128)(2,1)} %collective-permute-done.13.refs_1_.refs_9_.refs_5_, bf16[3584,256]{1,0:T(8,128)(2,1)} %collective-permute-done.14.refs_2_.refs_10_.refs_6_, ...), kind=kLoop, calls=%fused_computation.2 | loop fusion | flops 3670016 | bytes 12845058 | tf_op jit(solution)/shard_map/jit(_where)/select_n | solution.py:441
  212.6 1.5 collective-permute-start.28
  214.1 4.3 %shard_map.82 = f32[512,256]{1,0:T(8,128)S(1)} custom-call(s32[1]{0:T(128)} %constant.117.clone.1.refs_0_, bf16[7168,256]{1,0:T(8,128)(2,1)S(1)} %copy-done.10, bf16[128,7168]{1,0:T(8,128)(2,1)} %collective-permute-done.2.refs_7_.refs_2_.refs_11_, bf16[128,7168]{1,0:T(8,128)(2,1)} %collective-permute-done.5.refs_8_.refs_3_.refs_12_, ...), custom_call_target="tpu_custom_call" | custom-call | flops 18790480 | bytes 110100 | tf_op jit(solution)/shard_map/pallas_call | solution.py:225
  218.4 5.4 %shard_map.80 = f32[512,256]{1,0:T(8,128)S(1)} custom-call(s32[2]{0:T(128)S(1)} %pad_add_fusion.1.refs_0_, bf16[3584,256]{1,0:T(8,128)(2,1)} %collective-permute-done.3.refs_1_.refs_7_, bf16[3584,256]{1,0:T(8,128)(2,1)} %collective-permute-done.4.refs_2_.refs_8_, bf16[3584,256]{1,0:T(8,128)(2,1)S(1)} %collective-permute-done.refs_3_.refs_1_, ...), custom_call_target="tpu_custom_call" | custom-call | flops 18790480 | bytes 110100 | tf_op jit(solution)/shard_map/pallas_call | solution.py:225
  223.9 5.5 %shard_map.84.refs_13_ = f32[1024,256]{1,0:T(8,128)S(1)} custom-call(s32[1]{0:T(128)} %bitcast.9.refs_0_, bf16[3584,256]{1,0:T(8,128)(2,1)} %collective-permute-done.13.refs_1_.refs_9_.refs_5_, bf16[3584,256]{1,0:T(8,128)(2,1)} %collective-permute-done.14.refs_2_.refs_10_.refs_6_, bf16[3584,256]{1,0:T(8,128)(2,1)S(1)} %collective-permute-done.refs_3_.refs_1_, ...), custom_call_target="tpu_custom_call" | custom-call | flops 18790480 | bytes 91750 | tf_op jit(solution)/shard_map/pallas_call | solution.py:225
  229.4 5.0 %shard_map.83 = f32[512,256]{1,0:T(8,128)S(1)} custom-call(s32[1]{0:T(128)} %constant.117.clone.1.refs_0_, bf16[7168,256]{1,0:T(8,128)(2,1)S(1)} %copy-done.10, bf16[128,7168]{1,0:T(8,128)(2,1)} %collective-permute-done.10.refs_7_.refs_2_.refs_9_.refs_13_, bf16[128,7168]{1,0:T(8,128)(2,1)} %collective-permute-done.15.refs_8_.refs_3_.refs_10_.refs_14_, ...), custom_call_target="tpu_custom_call" | custom-call | flops 18790480 | bytes 110100 | tf_op jit(solution)/shard_map/pallas_call | solution.py:225
  234.4 5.4 %shard_map.81 = f32[512,256]{1,0:T(8,128)S(1)} custom-call(s32[2]{0:T(128)S(1)} %pad_add_fusion.1.refs_0_, bf16[3584,256]{1,0:T(8,128)(2,1)} %collective-permute-done.3.refs_1_.refs_7_, bf16[3584,256]{1,0:T(8,128)(2,1)} %collective-permute-done.4.refs_2_.refs_8_, bf16[3584,256]{1,0:T(8,128)(2,1)S(1)} %collective-permute-done.refs_3_.refs_1_, ...), custom_call_target="tpu_custom_call" | custom-call | flops 18790480 | bytes 110100 | tf_op jit(solution)/shard_map/pallas_call | solution.py:225
  239.9 1.8 pad_maximum_fusion.2
  241.7 2.0 collective-permute-start.22
  243.7 3.0 convert_add_fusion
  246.7 1.7 slice.120
  248.3 1.8 reshape.70
  250.1 1.5 copy-done.4
  251.6 1.5 copy-done.8
  253.1 5.5 %shard_map.85.refs_19_ = f32[1024,256]{1,0:T(8,128)S(1)} custom-call(s32[1]{0:T(128)} %bitcast.9.refs_0_, bf16[3584,256]{1,0:T(8,128)(2,1)} %collective-permute-done.13.refs_1_.refs_9_.refs_5_, bf16[3584,256]{1,0:T(8,128)(2,1)} %collective-permute-done.14.refs_2_.refs_10_.refs_6_, bf16[3584,256]{1,0:T(8,128)(2,1)S(1)} %collective-permute-done.refs_3_.refs_1_, ...), custom_call_target="tpu_custom_call" | custom-call | flops 18790480 | bytes 91750 | tf_op jit(solution)/shard_map/pallas_call | solution.py:225
  259.0 8.1 %collective-permute-done.22.refs_22_ = f32[1024,256]{1,0:T(8,128)} collective-permute-done((f32[1024,256]{1,0:T(8,128)}, f32[1024,256]{1,0:T(8,128)}, u32[]{:S(2)}, u32[]{:S(2)}) %collective-permute-start.22) | collective-permute-done | bytes 1048608 | tf_op jit(solution)/shard_map/ppermute | solution.py:561
  269.0 6.6 %collective-permute-start.36 = (bf16[16,9216]{1,0:T(8,128)(2,1)}, bf16[16,9216]{1,0:T(8,128)(2,1)S(1)}, u32[]{:S(2)}, u32[]{:S(2)}) collective-permute-start(bf16[16,9216]{1,0:T(8,128)(2,1)} %get-tuple-element.122), channel_id=1, source_target_pairs={{0,24},{2,26},{4,28},{6,30},{8,16},{10,18},{12,20},{14,22},{16,8},... | collective-permute-start | bytes 884744 | tf_op jit(solution)/shard_map/ppermute | solution.py:467
  275.5 5.0 %collective-permute-start.35 = (bf16[16,9216]{1,0:T(8,128)(2,1)S(1)}, bf16[16,9216]{1,0:T(8,128)(2,1)S(1)}, u32[]{:S(2)}, u32[]{:S(2)}) collective-permute-start(bf16[16,9216]{1,0:T(8,128)(2,1)S(1)} %get-tuple-element.123), channel_id=1, source_target_pairs={{0,16},{2,18},{4,20},{6,22},{8,24},{10,26},{12,28},{14,30},{16,0},... | collective-permute-start | bytes 884744 | tf_op jit(solution)/shard_map/ppermute | solution.py:467
  280.6 10.2 %shard_map.86 = (bf16[1024,256]{1,0:T(8,128)(2,1)S(1)}, bf16[1024,256]{1,0:T(8,128)(2,1)S(1)}, f32[1024,256]{1,0:T(8,128)S(1)}) custom-call(s32[3]{0:T(128)S(1)} %pad_add_fusion.refs_0_, bf16[3584,256]{1,0:T(8,128)(2,1)S(1)} %collective-permute-done.refs_3_.refs_1_, bf16[3584,256]{1,0:T(8,128)(2,1)} %collective-permute-done.1.refs_4_.refs_2_, ...), custom_call_target="tpu_custom_call" | custom-call | flops 37580964 | bytes 183500 | tf_op jit(solution)/shard_map/pallas_call | solution.py:225
  290.9 2.5 collective-permute-start.29
  293.4 10.6 %shard_map.87 = (bf16[1024,256]{1,0:T(8,128)(2,1)S(1)}, bf16[1024,256]{1,0:T(8,128)(2,1)S(1)}, f32[1024,256]{1,0:T(8,128)S(1)}) custom-call(s32[3]{0:T(128)S(1)} %pad_add_fusion.refs_0_, bf16[3584,256]{1,0:T(8,128)(2,1)S(1)} %collective-permute-done.refs_3_.refs_1_, bf16[3584,256]{1,0:T(8,128)(2,1)} %collective-permute-done.1.refs_4_.refs_2_, ...), custom_call_target="tpu_custom_call" | custom-call | flops 37580964 | bytes 183500 | tf_op jit(solution)/shard_map/pallas_call | solution.py:225
  304.7 6.3 %collective-permute-done.28.refs_3_.refs_4_ = bf16[3584,256]{1,0:T(8,128)(2,1)} collective-permute-done((bf16[3584,256]{1,0:T(8,128)(2,1)}, bf16[3584,256]{1,0:T(8,128)(2,1)}, u32[]{:S(2)}, u32[]{:S(2)}) %collective-permute-start.28) | collective-permute-done | bytes 1835040 | tf_op jit(solution)/shard_map/ppermute | solution.py:443
  311.1 1.6 collective-permute-start.24
  312.7 5.6 %shard_map.88 = bf16[1024,256]{1,0:T(8,128)(2,1)S(1)} custom-call(s32[1]{0:T(128)} %bitcast.13.refs_0_, bf16[3584,256]{1,0:T(8,128)(2,1)} %collective-permute-done.3.refs_1_.refs_7_, bf16[3584,256]{1,0:T(8,128)(2,1)} %collective-permute-done.4.refs_2_.refs_8_, bf16[3584,256]{1,0:T(8,128)(2,1)} %collective-permute-done.28.refs_3_.refs_4_, ...), custom_call_target="tpu_custom_call" | custom-call | flops 18790480 | bytes 91750 | tf_op jit(solution)/shard_map/pallas_call | solution.py:225
  318.9 5.6 %shard_map.89 = bf16[1024,256]{1,0:T(8,128)(2,1)S(1)} custom-call(s32[1]{0:T(128)} %bitcast.13.refs_0_, bf16[3584,256]{1,0:T(8,128)(2,1)} %collective-permute-done.3.refs_1_.refs_7_, bf16[3584,256]{1,0:T(8,128)(2,1)} %collective-permute-done.4.refs_2_.refs_8_, bf16[3584,256]{1,0:T(8,128)(2,1)} %collective-permute-done.28.refs_3_.refs_4_, ...), custom_call_target="tpu_custom_call" | custom-call | flops 18790480 | bytes 91750 | tf_op jit(solution)/shard_map/pallas_call | solution.py:225
  329.2 4.8 %collective-permute-done.30.refs_4_ = bf16[512,256]{1,0:T(8,128)(2,1)S(1)} collective-permute-done((bf16[512,256]{1,0:T(8,128)(2,1)S(1)}, bf16[512,256]{1,0:T(8,128)(2,1)S(1)}, u32[]{:S(2)}, u32[]{:S(2)}) %collective-permute-start.30) | collective-permute-done | bytes 262176 | tf_op jit(solution)/shard_map/ppermute | solution.py:596
  334.0 4.8 %collective-permute-done.31.refs_5_ = bf16[512,256]{1,0:T(8,128)(2,1)S(1)} collective-permute-done((bf16[512,256]{1,0:T(8,128)(2,1)S(1)}, bf16[512,256]{1,0:T(8,128)(2,1)S(1)}, u32[]{:S(2)}, u32[]{:S(2)}) %collective-permute-start.31) | collective-permute-done | bytes 262176 | tf_op jit(solution)/shard_map/ppermute | solution.py:596
  338.8 3.6 %shard_map.90 = bf16[512,2048]{1,0:T(8,128)(2,1)} custom-call(s32[8]{0:T(128)S(1)} %stack.35.code, bf16[512,256]{1,0:T(8,128)(2,1)S(1)} %collective-permute-done.24.refs_0_, bf16[512,256]{1,0:T(8,128)(2,1)S(1)} %collective-permute-done.25.refs_1_, bf16[512,256]{1,0:T(8,128)(2,1)S(1)} %collective-permute-done.27.refs_2_, ...), custom_call_target="tpu_custom_call" | custom-call | tf_op jit(solution)/shard_map/pallas_call | solution.py:393
  (128 shorter events, 28.3 us)
Async XLA Ops:
  0.6 107.2 %collective-permute-start.6 = (bf16[512,7168]{1,0:T(8,128)(2,1)}, bf16[512,7168]{1,0:T(8,128)(2,1)}, u32[]{:S(2)}, u32[]{:S(2)}) collective-permute-start(bf16[512,7168]{1,0:T(8,128)(2,1)} %refs_7_.5), channel_id=1, source_target_pairs={{0,2},{2,0},{4,6},{6,4},{8,10},{10,8},{12,14},{14,12},{16,18},{18,... | collective-permute-start | bytes 22020104 | tf_op jit(solution)/shard_map/ppermute | solution.py:505
  0.8 16.5 %copy-start.18 = (bf16[512,2048]{1,0:T(8,128)(2,1)S(1)}, bf16[512,2048]{1,0:T(8,128)(2,1)}, u32[]{:S(2)}) copy-start(bf16[512,2048]{1,0:T(8,128)(2,1)} %cotangent.3) | copy-start | bytes 6291460
  0.8 16.5 %copy-start.24 = (bf16[256,2048]{1,0:T(8,128)(2,1)S(1)}, bf16[256,2048]{1,0:T(8,128)(2,1)}, u32[]{:S(2)}) copy-start(bf16[256,2048]{1,0:T(8,128)(2,1)} %adapter_out.1) | copy-start | bytes 3145732
  3.8 45.3 %collective-permute-start = (bf16[3584,256]{1,0:T(8,128)(2,1)}, bf16[3584,256]{1,0:T(8,128)(2,1)S(1)}, u32[]{:S(2)}, u32[]{:S(2)}) collective-permute-start(bf16[3584,256]{1,0:T(8,128)(2,1)} %slice.88), channel_id=1, source_target_pairs={{8,0},{10,2},{12,4},{14,6},{16,8},{18,10},{20,12},{22,14},{24,16},... | collective-permute-start | bytes 5505032 | tf_op jit(solution)/shard_map/ppermute | solution.py:451
  5.0 45.0 %collective-permute-start.1 = (bf16[3584,256]{1,0:T(8,128)(2,1)}, bf16[3584,256]{1,0:T(8,128)(2,1)}, u32[]{:S(2)}, u32[]{:S(2)}) collective-permute-start(bf16[3584,256]{1,0:T(8,128)(2,1)} %slice.88), channel_id=1, source_target_pairs={{0,8},{2,10},{4,12},{6,14},{8,16},{10,18},{12,20},{14,22},{16,24},... | collective-permute-start | bytes 5505032 | tf_op jit(solution)/shard_map/ppermute | solution.py:451
  11.6 5.7 %copy-start = (bf16[512,7168]{1,0:T(8,128)(2,1)S(1)}, bf16[512,7168]{1,0:T(8,128)(2,1)}, u32[]{:S(2)}) copy-start(bf16[512,7168]{1,0:T(8,128)(2,1)} %refs_7_.5) | copy-start | bytes 22020100
  15.9 41.6 %collective-permute-start.2 = (bf16[128,7168]{1,0:T(8,128)(2,1)}, bf16[128,7168]{1,0:T(8,128)(2,1)}, u32[]{:S(2)}, u32[]{:S(2)}) collective-permute-start(bf16[128,7168]{1,0:T(8,128)(2,1)} %get-tuple-element.116), channel_id=1, source_target_pairs={{0,4},{2,6},{4,0},{6,2},{8,12},{10,14},{12,8},{14,10},{16,20},{18,... | collective-permute-start | bytes 5505032 | tf_op jit(solution)/shard_map/ppermute | solution.py:454
  17.3 2.0 copy-start.23
  25.2 43.7 %collective-permute-start.7 = (f32[512,640]{1,0:T(8,128)S(1)}, f32[512,640]{1,0:T(8,128)}, u32[]{:S(2)}, u32[]{:S(2)}) collective-permute-start(f32[512,640]{1,0:T(8,128)S(1)} %shard_map.76.own), channel_id=1, source_target_pairs={{0,1},{1,0},{2,3},{3,2},{4,5},{5,4},{6,7},{7,6},{8,9},{9,8},{10,11... | collective-permute-start | bytes 3932168 | tf_op jit(solution)/shard_map/ppermute | solution.py:507
  61.2 42.6 %collective-permute-start.3 = (bf16[3584,256]{1,0:T(8,128)(2,1)}, bf16[3584,256]{1,0:T(8,128)(2,1)}, u32[]{:S(2)}, u32[]{:S(2)}) collective-permute-start(bf16[3584,256]{1,0:T(8,128)(2,1)} %get-tuple-element.120), channel_id=1, source_target_pairs={{8,0},{10,2},{12,4},{14,6},{16,8},{18,10},{20,12},{22,14},{24,16},... | collective-permute-start | bytes 5505032 | tf_op jit(solution)/shard_map/ppermute | solution.py:451
  62.4 43.3 %collective-permute-start.4 = (bf16[3584,256]{1,0:T(8,128)(2,1)}, bf16[3584,256]{1,0:T(8,128)(2,1)}, u32[]{:S(2)}, u32[]{:S(2)}) collective-permute-start(bf16[3584,256]{1,0:T(8,128)(2,1)} %get-tuple-element.119), channel_id=1, source_target_pairs={{0,8},{2,10},{4,12},{6,14},{8,16},{10,18},{12,20},{14,22},{16,24},... | collective-permute-start | bytes 5505032 | tf_op jit(solution)/shard_map/ppermute | solution.py:451
  67.7 40.1 %collective-permute-start.5 = (bf16[128,7168]{1,0:T(8,128)(2,1)}, bf16[128,7168]{1,0:T(8,128)(2,1)}, u32[]{:S(2)}, u32[]{:S(2)}) collective-permute-start(bf16[128,7168]{1,0:T(8,128)(2,1)} %get-tuple-element.62), channel_id=1, source_target_pairs={{0,4},{2,6},{4,0},{6,2},{8,12},{10,14},{12,8},{14,10},{16,20},{18,... | collective-permute-start | bytes 5505032 | tf_op jit(solution)/shard_map/ppermute | solution.py:454
  68.9 3.1 copy-start.1
  72.0 1.6 copy-start.19
  81.5 2.2 copy-start.20
  83.7 42.6 %collective-permute-start.12 = (f32[128,9216]{1,0:T(8,128)S(1)}, f32[128,9216]{1,0:T(8,128)}, u32[]{:S(2)}, u32[]{:S(2)}) collective-permute-start(f32[128,9216]{1,0:T(8,128)S(1)} %get-tuple-element.72), channel_id=1, source_target_pairs={{0,2},{2,0},{4,6},{6,4},{8,10},{10,8},{12,14},{14,12},{16,18},{18,... | collective-permute-start | bytes 14155784 | tf_op jit(solution)/shard_map/ppermute | solution.py:459
  103.7 19.2 %collective-permute-start.11 = (bf16[128,7168]{1,0:T(8,128)(2,1)}, bf16[128,7168]{1,0:T(8,128)(2,1)S(1)}, u32[]{:S(2)}, u32[]{:S(2)}) collective-permute-start(bf16[128,7168]{1,0:T(8,128)(2,1)} %collective-permute-done.2.refs_7_.refs_2_.refs_11_), channel_id=1, source_target_pairs={{0,2},{2,0},{4,6},{6,4},{8,10},{10,8},{12,14},{14,12},{16,18},{18,... | collective-permute-start | bytes 5505032 | tf_op jit(solution)/shard_map/ppermute | solution.py:459
  107.8 8.9 %slice-start = ((s8[7340032]{0:T(1024)(128)(4,1)}), s8[4194304]{0:T(1024)(128)(4,1)S(1)}, s32[]{:S(2)}) async-start(s8[7340032]{0:T(1024)(128)(4,1)} %bitcast.26), calls=%async_computation | async-start | bytes 8388608
  109.2 7.5 %slice-start.1 = ((s8[7340032]{0:T(1024)(128)(4,1)}), s8[3145728]{0:T(1024)(128)(4,1)S(1)}, s32[]{:S(2)}) async-start(s8[7340032]{0:T(1024)(128)(4,1)} %bitcast.26), calls=%async_computation.1 | async-start | bytes 6291456
  109.2 41.3 %collective-permute-start.8 = (bf16[3584,256]{1,0:T(8,128)(2,1)}, bf16[3584,256]{1,0:T(8,128)(2,1)S(1)}, u32[]{:S(2)}, u32[]{:S(2)}) collective-permute-start(bf16[3584,256]{1,0:T(8,128)(2,1)} %broadcast_select_fusion.4), channel_id=1, source_target_pairs={{8,0},{10,2},{12,4},{14,6},{16,8},{18,10},{20,12},{22,14},{9,1},{1... | collective-permute-start | bytes 5505032 | tf_op jit(solution)/shard_map/ppermute | solution.py:451
  113.7 3.0 copy-start.9
  113.7 36.9 %collective-permute-start.9 = (bf16[3584,256]{1,0:T(8,128)(2,1)}, bf16[3584,256]{1,0:T(8,128)(2,1)S(1)}, u32[]{:S(2)}, u32[]{:S(2)}) collective-permute-start(bf16[3584,256]{1,0:T(8,128)(2,1)} %broadcast_select_fusion.1), channel_id=1, source_target_pairs={{8,16},{10,18},{12,20},{14,22},{16,24},{18,26},{20,28},{22,30},{9,... | collective-permute-start | bytes 5505032 | tf_op jit(solution)/shard_map/ppermute | solution.py:451
  114.6 39.3 %collective-permute-start.10 = (bf16[128,7168]{1,0:T(8,128)(2,1)}, bf16[128,7168]{1,0:T(8,128)(2,1)}, u32[]{:S(2)}, u32[]{:S(2)}) collective-permute-start(bf16[128,7168]{1,0:T(8,128)(2,1)} %slice.92), channel_id=1, source_target_pairs={{0,4},{2,6},{4,0},{6,2},{8,12},{10,14},{12,8},{14,10},{16,20},{18,... | collective-permute-start | bytes 5505032 | tf_op jit(solution)/shard_map/ppermute | solution.py:454
  123.0 33.8 %copy-start.11 = (bf16[128,7168]{1,0:T(8,128)(2,1)}, bf16[128,7168]{1,0:T(8,128)(2,1)S(1)}, u32[]{:S(2)}) copy-start(bf16[128,7168]{1,0:T(8,128)(2,1)S(1)} %collective-permute-done.11.refs_9_.refs_4_.refs_11_.refs_15_) | copy-start | bytes 5505028
  123.0 65.1 %collective-permute-start.16 = (bf16[128,7168]{1,0:T(8,128)(2,1)}, bf16[128,7168]{1,0:T(8,128)(2,1)}, u32[]{:S(2)}, u32[]{:S(2)}) collective-permute-start(bf16[128,7168]{1,0:T(8,128)(2,1)} %collective-permute-done.5.refs_8_.refs_3_.refs_12_), channel_id=1, source_target_pairs={{0,2},{2,0},{4,6},{6,4},{8,10},{10,8},{12,14},{14,12},{16,18},{18,... | collective-permute-start | bytes 5505032 | tf_op jit(solution)/shard_map/ppermute | solution.py:459
  150.6 6.2 %copy-start.2 = (bf16[3584,256]{1,0:T(8,128)(2,1)}, bf16[3584,256]{1,0:T(8,128)(2,1)S(1)}, u32[]{:S(2)}) copy-start(bf16[3584,256]{1,0:T(8,128)(2,1)S(1)} %collective-permute-done.8.refs_5_) | copy-start | bytes 5505028
  150.6 7.5 %copy-start.6 = (bf16[3584,256]{1,0:T(8,128)(2,1)}, bf16[3584,256]{1,0:T(8,128)(2,1)S(1)}, u32[]{:S(2)}) copy-start(bf16[3584,256]{1,0:T(8,128)(2,1)S(1)} %collective-permute-done.9.refs_6_) | copy-start | bytes 5505028
  156.8 41.0 %collective-permute-start.13 = (bf16[3584,256]{1,0:T(8,128)(2,1)}, bf16[3584,256]{1,0:T(8,128)(2,1)}, u32[]{:S(2)}, u32[]{:S(2)}) collective-permute-start(bf16[3584,256]{1,0:T(8,128)(2,1)} %broadcast_select_fusion.3), channel_id=1, source_target_pairs={{8,0},{10,2},{12,4},{14,6},{16,8},{18,10},{20,12},{22,14},{9,1},{1... | collective-permute-start | bytes 5505032 | tf_op jit(solution)/shard_map/ppermute | solution.py:451
  161.1 36.7 %collective-permute-start.14 = (bf16[3584,256]{1,0:T(8,128)(2,1)}, bf16[3584,256]{1,0:T(8,128)(2,1)}, u32[]{:S(2)}, u32[]{:S(2)}) collective-permute-start(bf16[3584,256]{1,0:T(8,128)(2,1)} %broadcast_select_fusion), channel_id=1, source_target_pairs={{8,16},{10,18},{12,20},{14,22},{16,24},{18,26},{20,28},{22,30},{9,... | collective-permute-start | bytes 5505032 | tf_op jit(solution)/shard_map/ppermute | solution.py:451
  163.0 38.3 %collective-permute-start.15 = (bf16[128,7168]{1,0:T(8,128)(2,1)}, bf16[128,7168]{1,0:T(8,128)(2,1)}, u32[]{:S(2)}, u32[]{:S(2)}) collective-permute-start(bf16[128,7168]{1,0:T(8,128)(2,1)} %slice.93), channel_id=1, source_target_pairs={{0,4},{2,6},{4,0},{6,2},{8,12},{10,14},{12,8},{14,10},{16,20},{18,... | collective-permute-start | bytes 5505032 | tf_op jit(solution)/shard_map/ppermute | solution.py:454
  163.5 37.9 %collective-permute-start.17 = (bf16[128,7168]{1,0:T(8,128)(2,1)}, bf16[128,7168]{1,0:T(8,128)(2,1)}, u32[]{:S(2)}, u32[]{:S(2)}) collective-permute-start(bf16[128,7168]{1,0:T(8,128)(2,1)} %collective-permute-done.10.refs_7_.refs_2_.refs_9_.refs_13_), channel_id=1, source_target_pairs={{0,2},{2,0},{4,6},{6,4},{8,10},{10,8},{12,14},{14,12},{16,18},{18,... | collective-permute-start | bytes 5505032 | tf_op jit(solution)/shard_map/ppermute | solution.py:459
  174.1 1.5 copy-start.3
  174.1 2.0 copy-start.7
  176.1 10.8 %copy-start.27 = (bf16[64,2048]{1,0:T(8,128)(2,1)S(1)}, bf16[64,2048]{1,0:T(8,128)(2,1)}, u32[]{:S(2)}) copy-start(bf16[64,2048]{1,0:T(8,128)(2,1)} %reshape.68) | copy-start | bytes 786436
  184.8 3.3 copy-start.16
  184.8 21.5 %copy-start.10 = (bf16[7168,256]{1,0:T(8,128)(2,1)S(1)}, bf16[7168,256]{1,0:T(8,128)(2,1)}, u32[]{:S(2)}) copy-start(bf16[7168,256]{1,0:T(8,128)(2,1)} %refs_1_.5) | copy-start | bytes 11010052
  201.3 28.1 %collective-permute-start.20 = (bf16[128,7168]{1,0:T(8,128)(2,1)}, bf16[128,7168]{1,0:T(8,128)(2,1)S(1)}, u32[]{:S(2)}, u32[]{:S(2)}) collective-permute-start(bf16[128,7168]{1,0:T(8,128)(2,1)} %collective-permute-done.15.refs_8_.refs_3_.refs_10_.refs_14_), channel_id=1, source_target_pairs={{0,2},{2,0},{4,6},{6,4},{8,10},{10,8},{12,14},{14,12},{16,18},{18,... | collective-permute-start | bytes 5505032 | tf_op jit(solution)/shard_map/ppermute | solution.py:459
  205.9 8.2 %copy-start.12 = (bf16[128,7168]{1,0:T(8,128)(2,1)S(1)}, bf16[128,7168]{1,0:T(8,128)(2,1)}, u32[]{:S(2)}) copy-start(bf16[128,7168]{1,0:T(8,128)(2,1)} %copy-done.11) | copy-start | bytes 5505028
  205.9 37.8 %collective-permute-start.19 = (bf16[64,11264]{1,0:T(8,128)(2,1)}, bf16[64,11264]{1,0:T(8,128)(2,1)}, u32[]{:S(2)}, u32[]{:S(2)}) collective-permute-start(bf16[64,11264]{1,0:T(8,128)(2,1)} %pad_maximum_fusion), channel_id=1, source_target_pairs={{0,4},{2,6},{4,0},{6,2},{8,12},{10,14},{12,8},{14,10},{16,20},{18,... | collective-permute-start | bytes 4325384 | tf_op jit(solution)/shard_map/ppermute | solution.py:545
  210.2 48.9 %collective-permute-start.18 = (bf16[3584,256]{1,0:T(8,128)(2,1)}, bf16[3584,256]{1,0:T(8,128)(2,1)}, u32[]{:S(2)}, u32[]{:S(2)}) collective-permute-start(bf16[3584,256]{1,0:T(8,128)(2,1)} %get-tuple-element.118), channel_id=1, source_target_pairs={{8,0},{10,2},{12,4},{14,6},{16,24},{18,26},{20,28},{22,30},{9,1},{... | collective-permute-start | bytes 5505032 | tf_op jit(solution)/shard_map/ppermute | solution.py:443
  211.5 47.3 %collective-permute-start.21 = (f32[1024,256]{1,0:T(8,128)}, f32[1024,256]{1,0:T(8,128)}, u32[]{:S(2)}, u32[]{:S(2)}) collective-permute-start(f32[1024,256]{1,0:T(8,128)} %broadcast_select_fusion.8), channel_id=1, source_target_pairs={{0,1},{1,0},{2,3},{3,2},{4,5},{5,4},{6,7},{7,6},{8,9},{9,8},{10,11... | collective-permute-start | bytes 3145736 | tf_op jit(solution)/shard_map/ppermute | solution.py:546
  212.6 98.4 %collective-permute-start.28 = (bf16[3584,256]{1,0:T(8,128)(2,1)}, bf16[3584,256]{1,0:T(8,128)(2,1)}, u32[]{:S(2)}, u32[]{:S(2)}) collective-permute-start(bf16[3584,256]{1,0:T(8,128)(2,1)} %get-tuple-element.117), channel_id=1, source_target_pairs={{8,0},{10,2},{12,4},{14,6},{16,24},{18,26},{20,28},{22,30},{9,1},{... | collective-permute-start | bytes 5505032 | tf_op jit(solution)/shard_map/ppermute | solution.py:443
  229.4 5.0 %copy-start.13 = (bf16[128,7168]{1,0:T(8,128)(2,1)}, bf16[128,7168]{1,0:T(8,128)(2,1)S(1)}, u32[]{:S(2)}) copy-start(bf16[128,7168]{1,0:T(8,128)(2,1)S(1)} %collective-permute-done.20.refs_10_.refs_5_.refs_14_.refs_18_) | copy-start | bytes 5505028
  241.7 25.5 %collective-permute-start.22 = (f32[1024,256]{1,0:T(8,128)}, f32[1024,256]{1,0:T(8,128)}, u32[]{:S(2)}, u32[]{:S(2)}) collective-permute-start(f32[1024,256]{1,0:T(8,128)} %get-tuple-element.127), channel_id=1, source_target_pairs={{0,1},{1,0},{2,3},{3,2},{4,5},{5,4},{6,7},{7,6},{8,9},{9,8},{10,11... | collective-permute-start | bytes 3145736 | tf_op jit(solution)/shard_map/ppermute | solution.py:561
  253.1 14.0 %copy-start.26 = (bf16[512,256]{1,0:T(8,128)(2,1)S(1)}, bf16[512,256]{1,0:T(8,128)(2,1)}, u32[]{:S(2)}) copy-start(bf16[512,256]{1,0:T(8,128)(2,1)} %reshape.70) | copy-start | bytes 786436
  253.1 15.0 %copy-start.25 = (f32[64,9216]{1,0:T(8,128)S(1)}, f32[64,9216]{1,0:T(8,128)}, u32[]{:S(2)}) copy-start(f32[64,9216]{1,0:T(8,128)} %convert_add_fusion) | copy-start | bytes 7077892
  253.1 27.4 %copy-start.22 = (f32[1024,256]{1,0:T(8,128)S(1)}, f32[1024,256]{1,0:T(8,128)}, u32[]{:S(2)}) copy-start(f32[1024,256]{1,0:T(8,128)} %get-tuple-element.128.refs_20_) | copy-start | bytes 3145732
  258.7 21.9 %copy-start.5 = (bf16[3584,256]{1,0:T(8,128)(2,1)S(1)}, bf16[3584,256]{1,0:T(8,128)(2,1)}, u32[]{:S(2)}) copy-start(bf16[3584,256]{1,0:T(8,128)(2,1)} %copy-done.2) | copy-start | bytes 5505028
  258.7 21.9 %copy-start.21 = (f32[1024,256]{1,0:T(8,128)S(1)}, f32[1024,256]{1,0:T(8,128)}, u32[]{:S(2)}) copy-start(f32[1024,256]{1,0:T(8,128)} %get-tuple-element.126.refs_21_) | copy-start | bytes 3145732
  267.2 13.4 %collective-permute-start.23 = (bf16[512,256]{1,0:T(8,128)(2,1)S(1)}, bf16[512,256]{1,0:T(8,128)(2,1)S(1)}, u32[]{:S(2)}, u32[]{:S(2)}) collective-permute-start(bf16[512,256]{1,0:T(8,128)(2,1)S(1)} %copy-done.26), channel_id=1, source_target_pairs={{0,2},{2,0},{4,6},{6,4},{8,10},{10,8},{12,14},{14,12},{16,18},{18,... | collective-permute-start | bytes 786440 | tf_op jit(solution)/shard_map/ppermute | solution.py:459
  268.2 25.3 %collective-permute-start.26 = (bf16[512,256]{1,0:T(8,128)(2,1)S(1)}, bf16[512,256]{1,0:T(8,128)(2,1)S(1)}, u32[]{:S(2)}, u32[]{:S(2)}) collective-permute-start(bf16[512,256]{1,0:T(8,128)(2,1)S(1)} %get-tuple-element.104), channel_id=1, source_target_pairs={{0,2},{2,0},{4,6},{6,4},{8,10},{10,8},{12,14},{14,12},{16,18},{18,... | collective-permute-start | bytes 786440 | tf_op jit(solution)/shard_map/ppermute | solution.py:459
  269.0 55.6 %collective-permute-start.36 = (bf16[16,9216]{1,0:T(8,128)(2,1)}, bf16[16,9216]{1,0:T(8,128)(2,1)S(1)}, u32[]{:S(2)}, u32[]{:S(2)}) collective-permute-start(bf16[16,9216]{1,0:T(8,128)(2,1)} %get-tuple-element.122), channel_id=1, source_target_pairs={{0,24},{2,26},{4,28},{6,30},{8,16},{10,18},{12,20},{14,22},{16,8},... | collective-permute-start | bytes 884744 | tf_op jit(solution)/shard_map/ppermute | solution.py:467
  275.5 49.9 %collective-permute-start.35 = (bf16[16,9216]{1,0:T(8,128)(2,1)S(1)}, bf16[16,9216]{1,0:T(8,128)(2,1)S(1)}, u32[]{:S(2)}, u32[]{:S(2)}) collective-permute-start(bf16[16,9216]{1,0:T(8,128)(2,1)S(1)} %get-tuple-element.123), channel_id=1, source_target_pairs={{0,16},{2,18},{4,20},{6,22},{8,24},{10,26},{12,28},{14,30},{16,0},... | collective-permute-start | bytes 884744 | tf_op jit(solution)/shard_map/ppermute | solution.py:467
  280.6 12.8 %copy-start.15 = (f32[1024,256]{1,0:T(8,128)S(1)}, f32[1024,256]{1,0:T(8,128)}, u32[]{:S(2)}) copy-start(f32[1024,256]{1,0:T(8,128)} %copy-done.14) | copy-start | bytes 3145732
  280.6 12.8 %copy-start.17 = (f32[1024,256]{1,0:T(8,128)S(1)}, f32[1024,256]{1,0:T(8,128)}, u32[]{:S(2)}) copy-start(f32[1024,256]{1,0:T(8,128)} %copy-done.16) | copy-start | bytes 3145732
  290.9 20.2 %collective-permute-start.29 = (bf16[1024,256]{1,0:T(8,128)(2,1)S(1)}, bf16[1024,256]{1,0:T(8,128)(2,1)S(1)}, u32[]{:S(2)}, u32[]{:S(2)}) collective-permute-start(bf16[1024,256]{1,0:T(8,128)(2,1)S(1)} %get-tuple-element.111), channel_id=1, source_target_pairs={{0,1},{1,0},{2,3},{3,2},{4,5},{5,4},{6,7},{7,6},{8,9},{9,8},{10,11... | collective-permute-start | bytes 1572872 | tf_op jit(solution)/shard_map/ppermute | solution.py:609
  304.0 14.3 %collective-permute-start.32 = (bf16[1024,256]{1,0:T(8,128)(2,1)S(1)}, bf16[1024,256]{1,0:T(8,128)(2,1)S(1)}, u32[]{:S(2)}, u32[]{:S(2)}) collective-permute-start(bf16[1024,256]{1,0:T(8,128)(2,1)S(1)} %get-tuple-element.113), channel_id=1, source_target_pairs={{0,1},{1,0},{2,3},{3,2},{4,5},{5,4},{6,7},{7,6},{8,9},{9,8},{10,11... | collective-permute-start | bytes 1572872 | tf_op jit(solution)/shard_map/ppermute | solution.py:609
  311.0 15.0 %collective-permute-start.34 = (bf16[16,9216]{1,0:T(8,128)(2,1)S(1)}, bf16[16,9216]{1,0:T(8,128)(2,1)S(1)}, u32[]{:S(2)}, u32[]{:S(2)}) collective-permute-start(bf16[16,9216]{1,0:T(8,128)(2,1)S(1)} %get-tuple-element.121), channel_id=1, source_target_pairs={{0,8},{2,10},{4,12},{6,14},{8,0},{10,2},{12,4},{14,6},{16,24},{18,... | collective-permute-start | bytes 884744 | tf_op jit(solution)/shard_map/ppermute | solution.py:467
  311.1 15.8 %collective-permute-start.24 = (bf16[512,256]{1,0:T(8,128)(2,1)S(1)}, bf16[512,256]{1,0:T(8,128)(2,1)S(1)}, u32[]{:S(2)}, u32[]{:S(2)}) collective-permute-start(bf16[512,256]{1,0:T(8,128)(2,1)S(1)} %get-tuple-element.136), channel_id=1, source_target_pairs={{0,6},{2,4},{4,2},{6,0},{8,14},{10,12},{12,10},{14,8},{16,22},{18,... | collective-permute-start | bytes 786440 | tf_op jit(solution)/shard_map/ppermute | solution.py:596
  318.3 10.9 %collective-permute-start.25 = (bf16[512,256]{1,0:T(8,128)(2,1)S(1)}, bf16[512,256]{1,0:T(8,128)(2,1)S(1)}, u32[]{:S(2)}, u32[]{:S(2)}) collective-permute-start(bf16[512,256]{1,0:T(8,128)(2,1)S(1)} %get-tuple-element.135), channel_id=1, source_target_pairs={{0,4},{2,6},{4,0},{6,2},{8,12},{10,14},{12,8},{14,10},{16,20},{18,... | collective-permute-start | bytes 786440 | tf_op jit(solution)/shard_map/ppermute | solution.py:596
  324.6 4.6 %collective-permute-start.27 = (bf16[512,256]{1,0:T(8,128)(2,1)S(1)}, bf16[512,256]{1,0:T(8,128)(2,1)S(1)}, u32[]{:S(2)}, u32[]{:S(2)}) collective-permute-start(bf16[512,256]{1,0:T(8,128)(2,1)S(1)} %get-tuple-element.134), channel_id=1, source_target_pairs={{0,2},{2,0},{4,6},{6,4},{8,10},{10,8},{12,14},{14,12},{16,18},{18,... | collective-permute-start | bytes 786440 | tf_op jit(solution)/shard_map/ppermute | solution.py:596
  325.4 8.6 %collective-permute-start.30 = (bf16[512,256]{1,0:T(8,128)(2,1)S(1)}, bf16[512,256]{1,0:T(8,128)(2,1)S(1)}, u32[]{:S(2)}, u32[]{:S(2)}) collective-permute-start(bf16[512,256]{1,0:T(8,128)(2,1)S(1)} %get-tuple-element.132), channel_id=1, source_target_pairs={{0,6},{2,4},{4,2},{6,0},{8,14},{10,12},{12,10},{14,8},{16,22},{18,... | collective-permute-start | bytes 786440 | tf_op jit(solution)/shard_map/ppermute | solution.py:596
  326.0 12.8 %collective-permute-start.31 = (bf16[512,256]{1,0:T(8,128)(2,1)S(1)}, bf16[512,256]{1,0:T(8,128)(2,1)S(1)}, u32[]{:S(2)}, u32[]{:S(2)}) collective-permute-start(bf16[512,256]{1,0:T(8,128)(2,1)S(1)} %get-tuple-element.131), channel_id=1, source_target_pairs={{0,4},{2,6},{4,0},{6,2},{8,12},{10,14},{12,8},{14,10},{16,20},{18,... | collective-permute-start | bytes 786440 | tf_op jit(solution)/shard_map/ppermute | solution.py:596
  326.9 11.9 %collective-permute-start.33 = (bf16[512,256]{1,0:T(8,128)(2,1)S(1)}, bf16[512,256]{1,0:T(8,128)(2,1)S(1)}, u32[]{:S(2)}, u32[]{:S(2)}) collective-permute-start(bf16[512,256]{1,0:T(8,128)(2,1)S(1)} %get-tuple-element.130), channel_id=1, source_target_pairs={{0,2},{2,0},{4,6},{6,4},{8,10},{10,8},{12,14},{14,12},{16,18},{18,... | collective-permute-start | bytes 786440 | tf_op jit(solution)/shard_map/ppermute | solution.py:596
  (3 other events, 4.0 us)

commit v5 on v4

--- a/solution.py
+++ b/solution.py
@@ -565,8 +565,10 @@
     far = held.all("x", range(parts)) + held.all("far", range(parts))
     groups = (near, far)
     second = [streams(3, 0, 2)]
+    held["half code"] = second_code[:1]
+    held.gate(("first sum", 1), ("first sum", 2), "half code")
     for h in range(2):
-        held["half", h] = product(second_code[:1], rows, second, groups[h])
+        held["half", h] = product(held["half code"], rows, second, groups[h])
     width = held["kept"].shape[1]
     held["t", 2] = held["sent"][:, width:].reshape(tokens, -1)
     held["mine"] = held["kept"] + held["sent"][:, :width].astype(jnp.float32)
@@ -576,8 +578,6 @@
     for m in (0, 2):
         held["t", m + 1] = held["t", m]
         over_core(("t", m + 1))
-    for k in (1, 2, 3):
-        send_sums(k)
     mixed = [streams(0, 4, 2), streams(4, 1, 3)]
     parity = (z % 2) ^ inner_late.astype(jnp.int32)
     blocks = [(parity ^ turn) * GROUP for turn in range(2)]
@@ -607,6 +607,10 @@
             mixed_code, rows, mixed, groups[h], extra=extra, dtype=jnp.bfloat16
         )
         held["w", h] = lax.ppermute(held["w", h], "tensor", pair_swap)
+        if h:
+            held.gate(("third sum", h), "mine")
+            for k in (1, 2, 3):
+                send_sums(k)
     for h in (1, 0):
         give_out(0, h, held["total", h])
 

time: 344 us -> 342 us (level)
  local copies, waits for them, and re-layouts: 33.1 us -> 36.9 us
    ppermute x3, waiting for transfers between devices: 0.01 us -> 7.22 us  [send_sums(): held['got', k] = lax.ppermute(sent, 'dp', pairs)]
    unnamed x62, local copies, waits for them, and re-layouts: 14.9 us -> 20.8 us
    ppermute x6, waiting for transfers between devices: 9.59 us -> 4.08 us  [give_out(): piece = lax.ppermute(piece, 'dp', swaps[m])]
    ppermute x1, waiting for transfers between devices: 8.14 us -> 3.03 us  [fast_shards(): lax.ppermute(jnp.where(early, first_sums[1], own_sums[1]), 'tensor', pair...]
    ppermute x3, starting transfers between devices: 11.5 us -> 7.92 us  [send_sums(): held['got', k] = lax.ppermute(sent, 'dp', pairs)]
  transfers between devices with their start and end apart: 37 -> 37, of which waited for: 14 -> 16; matrix products, arithmetic and copies ran while one was open for 14% -> 13% of each run, Pallas kernels for 27% -> 27%
where the time goes in v5:
time: 342 us; the launch traced here: 340 us
  waiting for transfers between devices  112 us (33%)
  Pallas kernels  95.3 us (28%)
  starting transfers between devices  66.4 us (19%)
  local copies, waits for them, and re-layouts  36.9 us (11%)
  other arithmetic  28.5 us (8%)
    pallas_call x12, Pallas kernels, product(): pl.pallas_call(kernel, out_shape=shapes if several else shape, in_specs=i...  77.9 us
    ppermute x8, waiting for transfers between devices, send_weight(): held[name, s] = lax.ppermute(sent, 'dp', line_pairs(sources, sign))  76.7 us
    unnamed x62, local copies, waits for them, and re-layouts  20.8 us
    ppermute x8, starting transfers between devices, send_weight(): held[name, s] = lax.ppermute(sent, 'dp', line_pairs(sources, sign))  20.1 us
    ppermute x7, starting transfers between devices, over_core(): held[result or name] = lax.ppermute(held[name], 'dp', core_swap)  17.4 us
    ppermute x4, waiting for transfers between devices, send_hidden(): held['x', i] = lax.ppermute(held['x', i], 'dp', x_swap)  16.3 us
    select_n x5, other arithmetic, send_weight(): sent = jnp.where(jnp.logical_and(early, z == last), other, sent)  13.9 us
    ppermute x3, starting transfers between devices, send_sums(): held['got', k] = lax.ppermute(sent, 'dp', pairs)  7.92 us
  transfers between devices with their start and end apart: 37, of which 16 were waited for; matrix products, arithmetic and copies ran while one was open for 13% of the time, Pallas kernels for 27%

profile of v5, /device:TPU:1, one launch (start us, length us, event | category | flops | bytes accessed | tf_op | source)
XLA Modules:
  0.0 340.0 jit_solution(2632605312094362893)
XLA Ops:
  0.8 3.0 slice.88
  5.0 6.6 %collective-permute-start.1 = (bf16[3584,256]{1,0:T(8,128)(2,1)}, bf16[3584,256]{1,0:T(8,128)(2,1)}, u32[]{:S(2)}, u32[]{:S(2)}) collective-permute-start(bf16[3584,256]{1,0:T(8,128)(2,1)} %slice.88), channel_id=1, source_target_pairs={{0,8},{2,10},{4,12},{6,14},{8,16},{10,18},{12,20},{14,22},{16,24},... | collective-permute-start | bytes 5505032 | tf_op jit(solution)/shard_map/ppermute | solution.py:451
  11.6 4.3 %fusion.15 = (bf16[128,7168]{1,0:T(8,128)(2,1)}, bf16[128,7168]{1,0:T(8,128)(2,1)}) fusion(bf16[512,7168]{1,0:T(8,128)(2,1)} %refs_7_.5), kind=kLoop, calls=%fused_computation.58 | loop fusion | bytes 7340032 | tf_op jit(solution)/shard_map/slice | solution.py:456
  15.9 1.4 collective-permute-start.2
  17.3 2.0 copy-done.25
  19.3 5.8 %shard_map.76.own = f32[512,640]{1,0:T(8,128)S(1)} custom-call(bf16[512,7168]{1,0:T(8,128)(2,1)S(1)} %copy-done, bf16[256,7168]{1,0:T(8,128)(2,1)S(1)} %copy-done.25, bf16[512,2048]{1,0:T(8,128)(2,1)S(1)} %copy-done.18, bf16[256,2048]{1,0:T(8,128)(2,1)S(1)} %copy-done.26), custom_call_target="tpu_custom_call" | custom-call | flops 24159192 | bytes 141557 | tf_op jit(solution)/shard_map/pallas_call | solution.py:280
  25.2 1.3 collective-permute-start.7
  26.5 22.5 %collective-permute-done.refs_3_.refs_1_ = bf16[3584,256]{1,0:T(8,128)(2,1)S(1)} collective-permute-done((bf16[3584,256]{1,0:T(8,128)(2,1)}, bf16[3584,256]{1,0:T(8,128)(2,1)S(1)}, u32[]{:S(2)}, u32[]{:S(2)}) %collective-permute-start) | collective-permute-done | bytes 1835040 | tf_op jit(solution)/shard_map/ppermute | solution.py:451
  50.0 7.5 %collective-permute-done.2.refs_7_.refs_2_.refs_11_ = bf16[128,7168]{1,0:T(8,128)(2,1)} collective-permute-done((bf16[128,7168]{1,0:T(8,128)(2,1)}, bf16[128,7168]{1,0:T(8,128)(2,1)}, u32[]{:S(2)}, u32[]{:S(2)}) %collective-permute-start.2) | collective-permute-done | bytes 1835040 | tf_op jit(solution)/shard_map/ppermute | solution.py:454
  57.5 3.6 %broadcast_select_fusion.2 = (bf16[3584,256]{1,0:T(8,128)(2,1)}, bf16[3584,256]{1,0:T(8,128)(2,1)}) fusion(bf16[3584,256]{1,0:T(8,128)(2,1)} %collective-permute-done.1.refs_4_.refs_2_, pred[]{:T(512)S(6)} %and.100, bf16[7168,256]{1,0:T(8,128)(2,1)} %refs_1_.5, bf16[3584,256]{1,0:T(8,128)(2,1)S(1)} %collective-permute-done.refs_3_.refs_1_, pred[]{:T(512)S(6)} %and.99), kind=kLoop, calls=%fused_computation.6 | loop fusion | flops 1835008 | bytes 9175042 | tf_op jit(solution)/shard_map/jit(_where)/select_n | solution.py:449
  62.4 5.2 %collective-permute-start.4 = (bf16[3584,256]{1,0:T(8,128)(2,1)}, bf16[3584,256]{1,0:T(8,128)(2,1)}, u32[]{:S(2)}, u32[]{:S(2)}) collective-permute-start(bf16[3584,256]{1,0:T(8,128)(2,1)} %get-tuple-element.125), channel_id=1, source_target_pairs={{0,8},{2,10},{4,12},{6,14},{8,16},{10,18},{12,20},{14,22},{16,24},... | collective-permute-start | bytes 5505032 | tf_op jit(solution)/shard_map/ppermute | solution.py:451
  68.9 3.1 copy-done.1
  72.0 1.6 copy-done.19
  73.6 7.9 %shard_map.77 = (bf16[512,256]{1,0:T(8,128)(2,1)S(1)}, f32[128,9216]{1,0:T(8,128)S(1)}, f32[128,9216]{1,0:T(8,128)S(1)}) custom-call(f32[512,640]{1,0:T(8,128)S(1)} %shard_map.76.own, f32[512,640]{1,0:T(8,128)} %collective-permute-done.7.other, bf16[256,256]{1,0:T(8,128)(2,1)S(1)} %fusion.5.order, bf16[512,7168]{1,0:T(8,128)(2,1)S(1)} %copy-done.1, ...), custom_call_target="tpu_custom_call" | custom-call | flops 24159192 | bytes 188743 | tf_op jit(solution)/shard_map/pallas_call | solution.py:360
  81.5 2.2 copy-done.20
  83.7 2.3 collective-permute-start.12
  86.0 1.4 slice.92
  87.4 16.3 %collective-permute-done.3.refs_1_.refs_7_ = bf16[3584,256]{1,0:T(8,128)(2,1)} collective-permute-done((bf16[3584,256]{1,0:T(8,128)(2,1)}, bf16[3584,256]{1,0:T(8,128)(2,1)}, u32[]{:S(2)}, u32[]{:S(2)}) %collective-permute-start.3) | collective-permute-done | bytes 1835040 | tf_op jit(solution)/shard_map/ppermute | solution.py:451
  103.7 2.1 collective-permute-start.11
  105.8 2.0 collective-permute-done.5.refs_8_.refs_3_.refs_12_
  107.8 1.4 broadcast_select_fusion.4
  109.2 1.5 collective-permute-start.8
  110.8 2.9 broadcast_select_fusion.1
  115.4 1.3 slice.93
  116.7 6.2 %shard_map.78.refs_15_ = f32[1024,256]{1,0:T(8,128)S(1)} custom-call(s32[1]{0:T(128)} %constant.117.clone.1.refs_0_, bf16[7168,256]{1,0:T(8,128)(2,1)S(1)} %copy-done.9, bf16[512,7168]{1,0:T(8,128)(2,1)S(1)} %bitcast.27, bf16[512,7168]{1,0:T(8,128)(2,1)} %collective-permute-done.6.refs_3_.refs_8_.refs_12_), custom_call_target="tpu_custom_call" | custom-call | flops 37580964 | bytes 183500 | tf_op jit(solution)/shard_map/pallas_call | solution.py:225
  123.0 3.3 collective-permute-start.16
  126.3 24.3 %collective-permute-done.8.refs_5_ = bf16[3584,256]{1,0:T(8,128)(2,1)S(1)} collective-permute-done((bf16[3584,256]{1,0:T(8,128)(2,1)}, bf16[3584,256]{1,0:T(8,128)(2,1)S(1)}, u32[]{:S(2)}, u32[]{:S(2)}) %collective-permute-start.8) | collective-permute-done | bytes 1835040 | tf_op jit(solution)/shard_map/ppermute | solution.py:451
  150.6 3.3 collective-permute-done.10.refs_7_.refs_2_.refs_9_.refs_13_
  153.9 2.9 broadcast_select_fusion.3
  158.1 3.0 broadcast_select_fusion
  161.1 2.0 collective-permute-start.14
  163.5 4.1 %collective-permute-start.17 = (bf16[128,7168]{1,0:T(8,128)(2,1)}, bf16[128,7168]{1,0:T(8,128)(2,1)}, u32[]{:S(2)}, u32[]{:S(2)}) collective-permute-start(bf16[128,7168]{1,0:T(8,128)(2,1)} %collective-permute-done.10.refs_7_.refs_2_.refs_9_.refs_13_), channel_id=1, source_target_pairs={{0,2},{2,0},{4,6},{6,4},{8,10},{10,8},{12,14},{14,12},{16,18},{18,... | collective-permute-start | bytes 5505032 | tf_op jit(solution)/shard_map/ppermute | solution.py:459
  167.8 4.3 %add.139 = f32[128,9216]{1,0:T(8,128)S(1)} add(f32[128,9216]{1,0:T(8,128)} %copy-done.20, f32[128,9216]{1,0:T(8,128)} %collective-permute-done.12) | non-fusion elementwise | flops 1179648 | bytes 14155776 | tf_op jit(solution)/shard_map/add | solution.py:534
  174.3 8.6 %shard_map.79.refs_14_ = f32[1024,256]{1,0:T(8,128)S(1)} custom-call(s32[2]{0:T(128)S(1)} %pad_add_fusion.1.refs_0_, bf16[3584,256]{1,0:T(8,128)(2,1)} %collective-permute-done.3.refs_1_.refs_7_, bf16[3584,256]{1,0:T(8,128)(2,1)} %collective-permute-done.4.refs_2_.refs_8_, bf16[3584,256]{1,0:T(8,128)(2,1)S(1)} %collective-permute-done.refs_3_.refs_1_, ...), custom_call_target="tpu_custom_call" | custom-call | flops 37580964 | bytes 183500 | tf_op jit(solution)/shard_map/pallas_call | solution.py:225
  185.2 12.6 %collective-permute-done.13.refs_1_.refs_9_.refs_5_ = bf16[3584,256]{1,0:T(8,128)(2,1)} collective-permute-done((bf16[3584,256]{1,0:T(8,128)(2,1)}, bf16[3584,256]{1,0:T(8,128)(2,1)}, u32[]{:S(2)}, u32[]{:S(2)}) %collective-permute-start.13) | collective-permute-done | bytes 1835040 | tf_op jit(solution)/shard_map/ppermute | solution.py:451
  197.8 3.5 %collective-permute-done.15.refs_8_.refs_3_.refs_10_.refs_14_ = bf16[128,7168]{1,0:T(8,128)(2,1)} collective-permute-done((bf16[128,7168]{1,0:T(8,128)(2,1)}, bf16[128,7168]{1,0:T(8,128)(2,1)}, u32[]{:S(2)}, u32[]{:S(2)}) %collective-permute-start.15) | collective-permute-done | bytes 1835040 | tf_op jit(solution)/shard_map/ppermute | solution.py:454
  201.3 4.5 %collective-permute-start.20 = (bf16[128,7168]{1,0:T(8,128)(2,1)}, bf16[128,7168]{1,0:T(8,128)(2,1)S(1)}, u32[]{:S(2)}, u32[]{:S(2)}) collective-permute-start(bf16[128,7168]{1,0:T(8,128)(2,1)} %collective-permute-done.15.refs_8_.refs_3_.refs_10_.refs_14_), channel_id=1, source_target_pairs={{0,2},{2,0},{4,6},{6,4},{8,10},{10,8},{12,14},{14,12},{16,18},{18,... | collective-permute-start | bytes 5505032 | tf_op jit(solution)/shard_map/ppermute | solution.py:459
  207.3 3.8 %slice_select_fusion = (bf16[3584,256]{1,0:T(8,128)(2,1)}, bf16[3584,256]{1,0:T(8,128)(2,1)}) fusion(bf16[7168,256]{1,0:T(8,128)(2,1)S(1)} %copy-done.10, pred[]{:T(512)S(6)} %and.98, bf16[3584,256]{1,0:T(8,128)(2,1)} %collective-permute-done.13.refs_1_.refs_9_.refs_5_, bf16[3584,256]{1,0:T(8,128)(2,1)} %collective-permute-done.14.refs_2_.refs_10_.refs_6_, ...), kind=kLoop, calls=%fused_computation.2 | loop fusion | flops 3670016 | bytes 12845058 | tf_op jit(solution)/shard_map/jit(_where)/select_n | solution.py:441
  214.9 4.3 %shard_map.82 = f32[512,256]{1,0:T(8,128)S(1)} custom-call(s32[1]{0:T(128)} %constant.117.clone.1.refs_0_, bf16[7168,256]{1,0:T(8,128)(2,1)S(1)} %copy-done.10, bf16[128,7168]{1,0:T(8,128)(2,1)} %collective-permute-done.2.refs_7_.refs_2_.refs_11_, bf16[128,7168]{1,0:T(8,128)(2,1)} %collective-permute-done.5.refs_8_.refs_3_.refs_12_, ...), custom_call_target="tpu_custom_call" | custom-call | flops 18790480 | bytes 110100 | tf_op jit(solution)/shard_map/pallas_call | solution.py:225
  219.2 5.4 %shard_map.80 = f32[512,256]{1,0:T(8,128)S(1)} custom-call(s32[2]{0:T(128)S(1)} %pad_add_fusion.1.refs_0_, bf16[3584,256]{1,0:T(8,128)(2,1)} %collective-permute-done.3.refs_1_.refs_7_, bf16[3584,256]{1,0:T(8,128)(2,1)} %collective-permute-done.4.refs_2_.refs_8_, bf16[3584,256]{1,0:T(8,128)(2,1)S(1)} %collective-permute-done.refs_3_.refs_1_, ...), custom_call_target="tpu_custom_call" | custom-call | flops 18790480 | bytes 110100 | tf_op jit(solution)/shard_map/pallas_call | solution.py:225
  224.8 5.0 %shard_map.83 = f32[512,256]{1,0:T(8,128)S(1)} custom-call(s32[1]{0:T(128)} %constant.117.clone.1.refs_0_, bf16[7168,256]{1,0:T(8,128)(2,1)S(1)} %copy-done.10, bf16[128,7168]{1,0:T(8,128)(2,1)} %collective-permute-done.10.refs_7_.refs_2_.refs_9_.refs_13_, bf16[128,7168]{1,0:T(8,128)(2,1)} %collective-permute-done.15.refs_8_.refs_3_.refs_10_.refs_14_, ...), custom_call_target="tpu_custom_call" | custom-call | flops 18790480 | bytes 110100 | tf_op jit(solution)/shard_map/pallas_call | solution.py:225
  229.8 5.4 %shard_map.81 = f32[512,256]{1,0:T(8,128)S(1)} custom-call(s32[2]{0:T(128)S(1)} %pad_add_fusion.1.refs_0_, bf16[3584,256]{1,0:T(8,128)(2,1)} %collective-permute-done.3.refs_1_.refs_7_, bf16[3584,256]{1,0:T(8,128)(2,1)} %collective-permute-done.4.refs_2_.refs_8_, bf16[3584,256]{1,0:T(8,128)(2,1)S(1)} %collective-permute-done.refs_3_.refs_1_, ...), custom_call_target="tpu_custom_call" | custom-call | flops 18790480 | bytes 110100 | tf_op jit(solution)/shard_map/pallas_call | solution.py:225
  235.3 1.8 pad_maximum_fusion.2
  237.1 2.5 collective-permute-start.22
  240.2 3.0 convert_add_fusion
  245.0 1.5 copy-done.4
  246.5 1.5 copy-done.8
  248.0 5.5 %shard_map.84.refs_13_ = f32[1024,256]{1,0:T(8,128)S(1)} custom-call(s32[1]{0:T(128)} %bitcast.9.refs_0_, bf16[3584,256]{1,0:T(8,128)(2,1)} %collective-permute-done.13.refs_1_.refs_9_.refs_5_, bf16[3584,256]{1,0:T(8,128)(2,1)} %collective-permute-done.14.refs_2_.refs_10_.refs_6_, bf16[3584,256]{1,0:T(8,128)(2,1)S(1)} %collective-permute-done.refs_3_.refs_1_, ...), custom_call_target="tpu_custom_call" | custom-call | flops 18790480 | bytes 91750 | tf_op jit(solution)/shard_map/pallas_call | solution.py:225
  253.5 5.4 %shard_map.85.refs_19_ = f32[1024,256]{1,0:T(8,128)S(1)} custom-call(s32[1]{0:T(128)} %bitcast.9.refs_0_, bf16[3584,256]{1,0:T(8,128)(2,1)} %collective-permute-done.13.refs_1_.refs_9_.refs_5_, bf16[3584,256]{1,0:T(8,128)(2,1)} %collective-permute-done.14.refs_2_.refs_10_.refs_6_, bf16[3584,256]{1,0:T(8,128)(2,1)S(1)} %collective-permute-done.refs_3_.refs_1_, ...), custom_call_target="tpu_custom_call" | custom-call | flops 18790480 | bytes 91750 | tf_op jit(solution)/shard_map/pallas_call | solution.py:225
  260.0 3.0 collective-permute-done.22.refs_22_
  266.5 1.5 copy-done.5
  270.5 10.1 %shard_map.86 = (bf16[1024,256]{1,0:T(8,128)(2,1)S(1)}, bf16[1024,256]{1,0:T(8,128)(2,1)S(1)}, f32[1024,256]{1,0:T(8,128)S(1)}) custom-call(s32[3]{0:T(128)S(1)} %pad_add_fusion.refs_0_, bf16[3584,256]{1,0:T(8,128)(2,1)S(1)} %collective-permute-done.refs_3_.refs_1_, bf16[3584,256]{1,0:T(8,128)(2,1)} %collective-permute-done.1.refs_4_.refs_2_, ...), custom_call_target="tpu_custom_call" | custom-call | flops 37580964 | bytes 183500 | tf_op jit(solution)/shard_map/pallas_call | solution.py:225
  280.7 1.3 collective-permute-start.24
  282.0 2.5 collective-permute-start.29
  284.5 10.7 %shard_map.87 = (bf16[1024,256]{1,0:T(8,128)(2,1)S(1)}, bf16[1024,256]{1,0:T(8,128)(2,1)S(1)}, f32[1024,256]{1,0:T(8,128)S(1)}) custom-call(s32[3]{0:T(128)S(1)} %pad_add_fusion.refs_0_, bf16[3584,256]{1,0:T(8,128)(2,1)S(1)} %collective-permute-done.refs_3_.refs_1_, bf16[3584,256]{1,0:T(8,128)(2,1)} %collective-permute-done.1.refs_4_.refs_2_, ...), custom_call_target="tpu_custom_call" | custom-call | flops 37580964 | bytes 183500 | tf_op jit(solution)/shard_map/pallas_call | solution.py:225
  296.0 3.3 collective-permute-done.28.refs_3_.refs_4_
  299.3 2.9 collective-permute-start.36
  302.2 4.9 %collective-permute-start.35 = (bf16[16,9216]{1,0:T(8,128)(2,1)S(1)}, bf16[16,9216]{1,0:T(8,128)(2,1)S(1)}, u32[]{:S(2)}, u32[]{:S(2)}) collective-permute-start(bf16[16,9216]{1,0:T(8,128)(2,1)S(1)} %get-tuple-element.129), channel_id=1, source_target_pairs={{0,16},{2,18},{4,20},{6,22},{8,24},{10,26},{12,28},{14,30},{16,0},... | collective-permute-start | bytes 884744 | tf_op jit(solution)/shard_map/ppermute | solution.py:467
  307.3 5.6 %shard_map.88 = bf16[1024,256]{1,0:T(8,128)(2,1)S(1)} custom-call(s32[1]{0:T(128)} %bitcast.13.refs_0_, bf16[3584,256]{1,0:T(8,128)(2,1)} %collective-permute-done.3.refs_1_.refs_7_, bf16[3584,256]{1,0:T(8,128)(2,1)} %collective-permute-done.4.refs_2_.refs_8_, bf16[3584,256]{1,0:T(8,128)(2,1)} %collective-permute-done.28.refs_3_.refs_4_, ...), custom_call_target="tpu_custom_call" | custom-call | flops 18790480 | bytes 91750 | tf_op jit(solution)/shard_map/pallas_call | solution.py:225
  313.5 5.7 %shard_map.89 = bf16[1024,256]{1,0:T(8,128)(2,1)S(1)} custom-call(s32[1]{0:T(128)} %bitcast.13.refs_0_, bf16[3584,256]{1,0:T(8,128)(2,1)} %collective-permute-done.3.refs_1_.refs_7_, bf16[3584,256]{1,0:T(8,128)(2,1)} %collective-permute-done.4.refs_2_.refs_8_, bf16[3584,256]{1,0:T(8,128)(2,1)} %collective-permute-done.28.refs_3_.refs_4_, ...), custom_call_target="tpu_custom_call" | custom-call | flops 18790480 | bytes 91750 | tf_op jit(solution)/shard_map/pallas_call | solution.py:225
  319.2 1.6 collective-permute-start.27
  321.8 7.2 %collective-permute-done.35 = bf16[16,9216]{1,0:T(8,128)(2,1)S(1)} collective-permute-done((bf16[16,9216]{1,0:T(8,128)(2,1)S(1)}, bf16[16,9216]{1,0:T(8,128)(2,1)S(1)}, u32[]{:S(2)}, u32[]{:S(2)}) %collective-permute-start.35) | collective-permute-done | bytes 294944 | tf_op jit(solution)/shard_map/ppermute | solution.py:467
  332.3 4.1 %collective-permute-done.31.refs_5_ = bf16[512,256]{1,0:T(8,128)(2,1)S(1)} collective-permute-done((bf16[512,256]{1,0:T(8,128)(2,1)S(1)}, bf16[512,256]{1,0:T(8,128)(2,1)S(1)}, u32[]{:S(2)}, u32[]{:S(2)}) %collective-permute-start.31) | collective-permute-done | bytes 262176 | tf_op jit(solution)/shard_map/ppermute | solution.py:596
  336.4 3.6 %shard_map.90 = bf16[512,2048]{1,0:T(8,128)(2,1)} custom-call(s32[8]{0:T(128)S(1)} %stack.35.code, bf16[512,256]{1,0:T(8,128)(2,1)S(1)} %collective-permute-done.24.refs_0_, bf16[512,256]{1,0:T(8,128)(2,1)S(1)} %collective-permute-done.25.refs_1_, bf16[512,256]{1,0:T(8,128)(2,1)S(1)} %collective-permute-done.27.refs_2_, ...), custom_call_target="tpu_custom_call" | custom-call | tf_op jit(solution)/shard_map/pallas_call | solution.py:393
  (128 shorter events, 33.4 us)
Async XLA Ops:
  0.6 107.2 %collective-permute-start.6 = (bf16[512,7168]{1,0:T(8,128)(2,1)}, bf16[512,7168]{1,0:T(8,128)(2,1)}, u32[]{:S(2)}, u32[]{:S(2)}) collective-permute-start(bf16[512,7168]{1,0:T(8,128)(2,1)} %refs_7_.5), channel_id=1, source_target_pairs={{0,2},{2,0},{4,6},{6,4},{8,10},{10,8},{12,14},{14,12},{16,18},{18,... | collective-permute-start | bytes 22020104 | tf_op jit(solution)/shard_map/ppermute | solution.py:505
  0.8 16.5 %copy-start.18 = (bf16[512,2048]{1,0:T(8,128)(2,1)S(1)}, bf16[512,2048]{1,0:T(8,128)(2,1)}, u32[]{:S(2)}) copy-start(bf16[512,2048]{1,0:T(8,128)(2,1)} %cotangent.3) | copy-start | bytes 6291460
  0.8 16.5 %copy-start.26 = (bf16[256,2048]{1,0:T(8,128)(2,1)S(1)}, bf16[256,2048]{1,0:T(8,128)(2,1)}, u32[]{:S(2)}) copy-start(bf16[256,2048]{1,0:T(8,128)(2,1)} %adapter_out.1) | copy-start | bytes 3145732
  3.8 45.3 %collective-permute-start = (bf16[3584,256]{1,0:T(8,128)(2,1)}, bf16[3584,256]{1,0:T(8,128)(2,1)S(1)}, u32[]{:S(2)}, u32[]{:S(2)}) collective-permute-start(bf16[3584,256]{1,0:T(8,128)(2,1)} %slice.88), channel_id=1, source_target_pairs={{8,0},{10,2},{12,4},{14,6},{16,8},{18,10},{20,12},{22,14},{24,16},... | collective-permute-start | bytes 5505032 | tf_op jit(solution)/shard_map/ppermute | solution.py:451
  5.0 45.0 %collective-permute-start.1 = (bf16[3584,256]{1,0:T(8,128)(2,1)}, bf16[3584,256]{1,0:T(8,128)(2,1)}, u32[]{:S(2)}, u32[]{:S(2)}) collective-permute-start(bf16[3584,256]{1,0:T(8,128)(2,1)} %slice.88), channel_id=1, source_target_pairs={{0,8},{2,10},{4,12},{6,14},{8,16},{10,18},{12,20},{14,22},{16,24},... | collective-permute-start | bytes 5505032 | tf_op jit(solution)/shard_map/ppermute | solution.py:451
  11.6 5.7 %copy-start = (bf16[512,7168]{1,0:T(8,128)(2,1)S(1)}, bf16[512,7168]{1,0:T(8,128)(2,1)}, u32[]{:S(2)}) copy-start(bf16[512,7168]{1,0:T(8,128)(2,1)} %refs_7_.5) | copy-start | bytes 22020100
  15.9 41.6 %collective-permute-start.2 = (bf16[128,7168]{1,0:T(8,128)(2,1)}, bf16[128,7168]{1,0:T(8,128)(2,1)}, u32[]{:S(2)}, u32[]{:S(2)}) collective-permute-start(bf16[128,7168]{1,0:T(8,128)(2,1)} %get-tuple-element.122), channel_id=1, source_target_pairs={{0,4},{2,6},{4,0},{6,2},{8,12},{10,14},{12,8},{14,10},{16,20},{18,... | collective-permute-start | bytes 5505032 | tf_op jit(solution)/shard_map/ppermute | solution.py:454
  17.3 2.0 copy-start.25
  25.2 43.7 %collective-permute-start.7 = (f32[512,640]{1,0:T(8,128)S(1)}, f32[512,640]{1,0:T(8,128)}, u32[]{:S(2)}, u32[]{:S(2)}) collective-permute-start(f32[512,640]{1,0:T(8,128)S(1)} %shard_map.76.own), channel_id=1, source_target_pairs={{0,1},{1,0},{2,3},{3,2},{4,5},{5,4},{6,7},{7,6},{8,9},{9,8},{10,11... | collective-permute-start | bytes 3932168 | tf_op jit(solution)/shard_map/ppermute | solution.py:507
  61.2 42.6 %collective-permute-start.3 = (bf16[3584,256]{1,0:T(8,128)(2,1)}, bf16[3584,256]{1,0:T(8,128)(2,1)}, u32[]{:S(2)}, u32[]{:S(2)}) collective-permute-start(bf16[3584,256]{1,0:T(8,128)(2,1)} %get-tuple-element.126), channel_id=1, source_target_pairs={{8,0},{10,2},{12,4},{14,6},{16,8},{18,10},{20,12},{22,14},{24,16},... | collective-permute-start | bytes 5505032 | tf_op jit(solution)/shard_map/ppermute | solution.py:451
  62.4 43.3 %collective-permute-start.4 = (bf16[3584,256]{1,0:T(8,128)(2,1)}, bf16[3584,256]{1,0:T(8,128)(2,1)}, u32[]{:S(2)}, u32[]{:S(2)}) collective-permute-start(bf16[3584,256]{1,0:T(8,128)(2,1)} %get-tuple-element.125), channel_id=1, source_target_pairs={{0,8},{2,10},{4,12},{6,14},{8,16},{10,18},{12,20},{14,22},{16,24},... | collective-permute-start | bytes 5505032 | tf_op jit(solution)/shard_map/ppermute | solution.py:451
  67.7 40.1 %collective-permute-start.5 = (bf16[128,7168]{1,0:T(8,128)(2,1)}, bf16[128,7168]{1,0:T(8,128)(2,1)}, u32[]{:S(2)}, u32[]{:S(2)}) collective-permute-start(bf16[128,7168]{1,0:T(8,128)(2,1)} %get-tuple-element.65), channel_id=1, source_target_pairs={{0,4},{2,6},{4,0},{6,2},{8,12},{10,14},{12,8},{14,10},{16,20},{18,... | collective-permute-start | bytes 5505032 | tf_op jit(solution)/shard_map/ppermute | solution.py:454
  68.9 3.1 copy-start.1
  72.0 1.6 copy-start.19
  81.5 2.2 copy-start.20
  83.7 42.6 %collective-permute-start.12 = (f32[128,9216]{1,0:T(8,128)S(1)}, f32[128,9216]{1,0:T(8,128)}, u32[]{:S(2)}, u32[]{:S(2)}) collective-permute-start(f32[128,9216]{1,0:T(8,128)S(1)} %get-tuple-element.75), channel_id=1, source_target_pairs={{0,2},{2,0},{4,6},{6,4},{8,10},{10,8},{12,14},{14,12},{16,18},{18,... | collective-permute-start | bytes 14155784 | tf_op jit(solution)/shard_map/ppermute | solution.py:459
  103.7 19.2 %collective-permute-start.11 = (bf16[128,7168]{1,0:T(8,128)(2,1)}, bf16[128,7168]{1,0:T(8,128)(2,1)S(1)}, u32[]{:S(2)}, u32[]{:S(2)}) collective-permute-start(bf16[128,7168]{1,0:T(8,128)(2,1)} %collective-permute-done.2.refs_7_.refs_2_.refs_11_), channel_id=1, source_target_pairs={{0,2},{2,0},{4,6},{6,4},{8,10},{10,8},{12,14},{14,12},{16,18},{18,... | collective-permute-start | bytes 5505032 | tf_op jit(solution)/shard_map/ppermute | solution.py:459
  107.8 8.9 %slice-start = ((s8[7340032]{0:T(1024)(128)(4,1)}), s8[4194304]{0:T(1024)(128)(4,1)S(1)}, s32[]{:S(2)}) async-start(s8[7340032]{0:T(1024)(128)(4,1)} %bitcast.26), calls=%async_computation | async-start | bytes 8388608
  109.2 7.5 %slice-start.1 = ((s8[7340032]{0:T(1024)(128)(4,1)}), s8[3145728]{0:T(1024)(128)(4,1)S(1)}, s32[]{:S(2)}) async-start(s8[7340032]{0:T(1024)(128)(4,1)} %bitcast.26), calls=%async_computation.1 | async-start | bytes 6291456
  109.2 41.3 %collective-permute-start.8 = (bf16[3584,256]{1,0:T(8,128)(2,1)}, bf16[3584,256]{1,0:T(8,128)(2,1)S(1)}, u32[]{:S(2)}, u32[]{:S(2)}) collective-permute-start(bf16[3584,256]{1,0:T(8,128)(2,1)} %broadcast_select_fusion.4), channel_id=1, source_target_pairs={{8,0},{10,2},{12,4},{14,6},{16,8},{18,10},{20,12},{22,14},{9,1},{1... | collective-permute-start | bytes 5505032 | tf_op jit(solution)/shard_map/ppermute | solution.py:451
  113.7 3.0 copy-start.9
  113.7 36.9 %collective-permute-start.9 = (bf16[3584,256]{1,0:T(8,128)(2,1)}, bf16[3584,256]{1,0:T(8,128)(2,1)S(1)}, u32[]{:S(2)}, u32[]{:S(2)}) collective-permute-start(bf16[3584,256]{1,0:T(8,128)(2,1)} %broadcast_select_fusion.1), channel_id=1, source_target_pairs={{8,16},{10,18},{12,20},{14,22},{16,24},{18,26},{20,28},{22,30},{9,... | collective-permute-start | bytes 5505032 | tf_op jit(solution)/shard_map/ppermute | solution.py:451
  114.6 39.3 %collective-permute-start.10 = (bf16[128,7168]{1,0:T(8,128)(2,1)}, bf16[128,7168]{1,0:T(8,128)(2,1)}, u32[]{:S(2)}, u32[]{:S(2)}) collective-permute-start(bf16[128,7168]{1,0:T(8,128)(2,1)} %slice.92), channel_id=1, source_target_pairs={{0,4},{2,6},{4,0},{6,2},{8,12},{10,14},{12,8},{14,10},{16,20},{18,... | collective-permute-start | bytes 5505032 | tf_op jit(solution)/shard_map/ppermute | solution.py:454
  123.0 33.8 %copy-start.11 = (bf16[128,7168]{1,0:T(8,128)(2,1)}, bf16[128,7168]{1,0:T(8,128)(2,1)S(1)}, u32[]{:S(2)}) copy-start(bf16[128,7168]{1,0:T(8,128)(2,1)S(1)} %collective-permute-done.11.refs_9_.refs_4_.refs_11_.refs_15_) | copy-start | bytes 5505028
  123.0 62.2 %collective-permute-start.16 = (bf16[128,7168]{1,0:T(8,128)(2,1)}, bf16[128,7168]{1,0:T(8,128)(2,1)}, u32[]{:S(2)}, u32[]{:S(2)}) collective-permute-start(bf16[128,7168]{1,0:T(8,128)(2,1)} %collective-permute-done.5.refs_8_.refs_3_.refs_12_), channel_id=1, source_target_pairs={{0,2},{2,0},{4,6},{6,4},{8,10},{10,8},{12,14},{14,12},{16,18},{18,... | collective-permute-start | bytes 5505032 | tf_op jit(solution)/shard_map/ppermute | solution.py:459
  150.6 6.2 %copy-start.2 = (bf16[3584,256]{1,0:T(8,128)(2,1)}, bf16[3584,256]{1,0:T(8,128)(2,1)S(1)}, u32[]{:S(2)}) copy-start(bf16[3584,256]{1,0:T(8,128)(2,1)S(1)} %collective-permute-done.8.refs_5_) | copy-start | bytes 5505028
  150.6 7.5 %copy-start.6 = (bf16[3584,256]{1,0:T(8,128)(2,1)}, bf16[3584,256]{1,0:T(8,128)(2,1)S(1)}, u32[]{:S(2)}) copy-start(bf16[3584,256]{1,0:T(8,128)(2,1)S(1)} %collective-permute-done.9.refs_6_) | copy-start | bytes 5505028
  156.8 41.0 %collective-permute-start.13 = (bf16[3584,256]{1,0:T(8,128)(2,1)}, bf16[3584,256]{1,0:T(8,128)(2,1)}, u32[]{:S(2)}, u32[]{:S(2)}) collective-permute-start(bf16[3584,256]{1,0:T(8,128)(2,1)} %broadcast_select_fusion.3), channel_id=1, source_target_pairs={{8,0},{10,2},{12,4},{14,6},{16,8},{18,10},{20,12},{22,14},{9,1},{1... | collective-permute-start | bytes 5505032 | tf_op jit(solution)/shard_map/ppermute | solution.py:451
  161.1 36.7 %collective-permute-start.14 = (bf16[3584,256]{1,0:T(8,128)(2,1)}, bf16[3584,256]{1,0:T(8,128)(2,1)}, u32[]{:S(2)}, u32[]{:S(2)}) collective-permute-start(bf16[3584,256]{1,0:T(8,128)(2,1)} %broadcast_select_fusion), channel_id=1, source_target_pairs={{8,16},{10,18},{12,20},{14,22},{16,24},{18,26},{20,28},{22,30},{9,... | collective-permute-start | bytes 5505032 | tf_op jit(solution)/shard_map/ppermute | solution.py:451
  163.0 38.3 %collective-permute-start.15 = (bf16[128,7168]{1,0:T(8,128)(2,1)}, bf16[128,7168]{1,0:T(8,128)(2,1)}, u32[]{:S(2)}, u32[]{:S(2)}) collective-permute-start(bf16[128,7168]{1,0:T(8,128)(2,1)} %slice.93), channel_id=1, source_target_pairs={{0,4},{2,6},{4,0},{6,2},{8,12},{10,14},{12,8},{14,10},{16,20},{18,... | collective-permute-start | bytes 5505032 | tf_op jit(solution)/shard_map/ppermute | solution.py:454
  163.5 37.9 %collective-permute-start.17 = (bf16[128,7168]{1,0:T(8,128)(2,1)}, bf16[128,7168]{1,0:T(8,128)(2,1)}, u32[]{:S(2)}, u32[]{:S(2)}) collective-permute-start(bf16[128,7168]{1,0:T(8,128)(2,1)} %collective-permute-done.10.refs_7_.refs_2_.refs_9_.refs_13_), channel_id=1, source_target_pairs={{0,2},{2,0},{4,6},{6,4},{8,10},{10,8},{12,14},{14,12},{16,18},{18,... | collective-permute-start | bytes 5505032 | tf_op jit(solution)/shard_map/ppermute | solution.py:459
  172.3 1.5 copy-start.3
  172.3 2.0 copy-start.7
  183.0 2.2 copy-start.16
  183.0 24.3 %copy-start.10 = (bf16[7168,256]{1,0:T(8,128)(2,1)S(1)}, bf16[7168,256]{1,0:T(8,128)(2,1)}, u32[]{:S(2)}) copy-start(bf16[7168,256]{1,0:T(8,128)(2,1)} %refs_1_.5) | copy-start | bytes 11010052
  201.3 23.4 %collective-permute-start.20 = (bf16[128,7168]{1,0:T(8,128)(2,1)}, bf16[128,7168]{1,0:T(8,128)(2,1)S(1)}, u32[]{:S(2)}, u32[]{:S(2)}) collective-permute-start(bf16[128,7168]{1,0:T(8,128)(2,1)} %collective-permute-done.15.refs_8_.refs_3_.refs_10_.refs_14_), channel_id=1, source_target_pairs={{0,2},{2,0},{4,6},{6,4},{8,10},{10,8},{12,14},{14,12},{16,18},{18,... | collective-permute-start | bytes 5505032 | tf_op jit(solution)/shard_map/ppermute | solution.py:459
  206.8 8.1 %copy-start.12 = (bf16[128,7168]{1,0:T(8,128)(2,1)S(1)}, bf16[128,7168]{1,0:T(8,128)(2,1)}, u32[]{:S(2)}) copy-start(bf16[128,7168]{1,0:T(8,128)(2,1)} %copy-done.11) | copy-start | bytes 5505028
  206.8 33.4 %collective-permute-start.19 = (bf16[64,11264]{1,0:T(8,128)(2,1)S(1)}, bf16[64,11264]{1,0:T(8,128)(2,1)}, u32[]{:S(2)}, u32[]{:S(2)}) collective-permute-start(bf16[64,11264]{1,0:T(8,128)(2,1)S(1)} %pad_maximum_fusion), channel_id=1, source_target_pairs={{0,4},{2,6},{4,0},{6,2},{8,12},{10,14},{12,8},{14,10},{16,20},{18,... | collective-permute-start | bytes 4325384 | tf_op jit(solution)/shard_map/ppermute | solution.py:545
  211.1 48.9 %collective-permute-start.18 = (bf16[3584,256]{1,0:T(8,128)(2,1)}, bf16[3584,256]{1,0:T(8,128)(2,1)}, u32[]{:S(2)}, u32[]{:S(2)}) collective-permute-start(bf16[3584,256]{1,0:T(8,128)(2,1)} %get-tuple-element.124), channel_id=1, source_target_pairs={{8,0},{10,2},{12,4},{14,6},{16,24},{18,26},{20,28},{22,30},{9,1},{... | collective-permute-start | bytes 5505032 | tf_op jit(solution)/shard_map/ppermute | solution.py:443
  212.4 47.5 %collective-permute-start.21 = (f32[1024,256]{1,0:T(8,128)}, f32[1024,256]{1,0:T(8,128)}, u32[]{:S(2)}, u32[]{:S(2)}) collective-permute-start(f32[1024,256]{1,0:T(8,128)} %broadcast_select_fusion.8), channel_id=1, source_target_pairs={{0,1},{1,0},{2,3},{3,2},{4,5},{5,4},{6,7},{7,6},{8,9},{9,8},{10,11... | collective-permute-start | bytes 3145736 | tf_op jit(solution)/shard_map/ppermute | solution.py:546
  213.6 85.7 %collective-permute-start.28 = (bf16[3584,256]{1,0:T(8,128)(2,1)}, bf16[3584,256]{1,0:T(8,128)(2,1)}, u32[]{:S(2)}, u32[]{:S(2)}) collective-permute-start(bf16[3584,256]{1,0:T(8,128)(2,1)} %get-tuple-element.123), channel_id=1, source_target_pairs={{8,0},{10,2},{12,4},{14,6},{16,24},{18,26},{20,28},{22,30},{9,1},{... | collective-permute-start | bytes 5505032 | tf_op jit(solution)/shard_map/ppermute | solution.py:443
  224.8 5.0 %copy-start.13 = (bf16[128,7168]{1,0:T(8,128)(2,1)}, bf16[128,7168]{1,0:T(8,128)(2,1)S(1)}, u32[]{:S(2)}) copy-start(bf16[128,7168]{1,0:T(8,128)(2,1)S(1)} %collective-permute-done.20.refs_10_.refs_5_.refs_14_.refs_18_) | copy-start | bytes 5505028
  237.1 25.9 %collective-permute-start.22 = (f32[1024,256]{1,0:T(8,128)}, f32[1024,256]{1,0:T(8,128)}, u32[]{:S(2)}, u32[]{:S(2)}) collective-permute-start(f32[1024,256]{1,0:T(8,128)} %get-tuple-element.133), channel_id=1, source_target_pairs={{0,1},{1,0},{2,3},{3,2},{4,5},{5,4},{6,7},{7,6},{8,9},{9,8},{10,11... | collective-permute-start | bytes 3145736 | tf_op jit(solution)/shard_map/ppermute | solution.py:561
  245.0 1.5 copy-start.4
  246.5 1.5 copy-start.8
  263.0 2.5 collective-permute-start.23
  264.2 2.3 copy-start.22
  264.2 20.3 %collective-permute-start.26 = (bf16[512,256]{1,0:T(8,128)(2,1)S(1)}, bf16[512,256]{1,0:T(8,128)(2,1)S(1)}, u32[]{:S(2)}, u32[]{:S(2)}) collective-permute-start(bf16[512,256]{1,0:T(8,128)(2,1)S(1)} %get-tuple-element.108), channel_id=1, source_target_pairs={{0,2},{2,0},{4,6},{6,4},{8,10},{10,8},{12,14},{14,12},{16,18},{18,... | collective-permute-start | bytes 786440 | tf_op jit(solution)/shard_map/ppermute | solution.py:459
  266.5 1.5 copy-start.5
  268.0 1.2 copy-start.23
  270.5 14.0 %copy-start.17 = (f32[1024,256]{1,0:T(8,128)S(1)}, f32[1024,256]{1,0:T(8,128)}, u32[]{:S(2)}) copy-start(f32[1024,256]{1,0:T(8,128)} %copy-done.16) | copy-start | bytes 3145732
  280.6 3.9 %copy-start.15 = (f32[1024,256]{1,0:T(8,128)S(1)}, f32[1024,256]{1,0:T(8,128)}, u32[]{:S(2)}) copy-start(f32[1024,256]{1,0:T(8,128)} %copy-done.14) | copy-start | bytes 3145732
  280.7 38.5 %collective-permute-start.24 = (bf16[512,256]{1,0:T(8,128)(2,1)S(1)}, bf16[512,256]{1,0:T(8,128)(2,1)S(1)}, u32[]{:S(2)}, u32[]{:S(2)}) collective-permute-start(bf16[512,256]{1,0:T(8,128)(2,1)S(1)} %get-tuple-element.142), channel_id=1, source_target_pairs={{0,6},{2,4},{4,2},{6,0},{8,14},{10,12},{12,10},{14,8},{16,22},{18,... | collective-permute-start | bytes 786440 | tf_op jit(solution)/shard_map/ppermute | solution.py:596
  282.0 25.2 %collective-permute-start.29 = (bf16[1024,256]{1,0:T(8,128)(2,1)S(1)}, bf16[1024,256]{1,0:T(8,128)(2,1)S(1)}, u32[]{:S(2)}, u32[]{:S(2)}) collective-permute-start(bf16[1024,256]{1,0:T(8,128)(2,1)S(1)} %get-tuple-element.117), channel_id=1, source_target_pairs={{0,1},{1,0},{2,3},{3,2},{4,5},{5,4},{6,7},{7,6},{8,9},{9,8},{10,11... | collective-permute-start | bytes 1572872 | tf_op jit(solution)/shard_map/ppermute | solution.py:609
  284.5 11.3 %copy-start.27 = (f32[64,9216]{1,0:T(8,128)S(1)}, f32[64,9216]{1,0:T(8,128)}, u32[]{:S(2)}) copy-start(f32[64,9216]{1,0:T(8,128)} %convert_add_fusion) | copy-start | bytes 7077892
  295.3 17.6 %collective-permute-start.32 = (bf16[1024,256]{1,0:T(8,128)(2,1)S(1)}, bf16[1024,256]{1,0:T(8,128)(2,1)S(1)}, u32[]{:S(2)}, u32[]{:S(2)}) collective-permute-start(bf16[1024,256]{1,0:T(8,128)(2,1)S(1)} %get-tuple-element.119), channel_id=1, source_target_pairs={{0,1},{1,0},{2,3},{3,2},{4,5},{5,4},{6,7},{7,6},{8,9},{9,8},{10,11... | collective-permute-start | bytes 1572872 | tf_op jit(solution)/shard_map/ppermute | solution.py:609
  299.3 21.5 %collective-permute-start.36 = (bf16[16,9216]{1,0:T(8,128)(2,1)S(1)}, bf16[16,9216]{1,0:T(8,128)(2,1)S(1)}, u32[]{:S(2)}, u32[]{:S(2)}) collective-permute-start(bf16[16,9216]{1,0:T(8,128)(2,1)S(1)} %get-tuple-element.128), channel_id=1, source_target_pairs={{0,24},{2,26},{4,28},{6,30},{8,16},{10,18},{12,20},{14,22},{16,8},... | collective-permute-start | bytes 884744 | tf_op jit(solution)/shard_map/ppermute | solution.py:467
  302.2 26.8 %collective-permute-start.35 = (bf16[16,9216]{1,0:T(8,128)(2,1)S(1)}, bf16[16,9216]{1,0:T(8,128)(2,1)S(1)}, u32[]{:S(2)}, u32[]{:S(2)}) collective-permute-start(bf16[16,9216]{1,0:T(8,128)(2,1)S(1)} %get-tuple-element.129), channel_id=1, source_target_pairs={{0,16},{2,18},{4,20},{6,22},{8,24},{10,26},{12,28},{14,30},{16,0},... | collective-permute-start | bytes 884744 | tf_op jit(solution)/shard_map/ppermute | solution.py:467
  307.2 22.7 %collective-permute-start.34 = (bf16[16,9216]{1,0:T(8,128)(2,1)S(1)}, bf16[16,9216]{1,0:T(8,128)(2,1)S(1)}, u32[]{:S(2)}, u32[]{:S(2)}) collective-permute-start(bf16[16,9216]{1,0:T(8,128)(2,1)S(1)} %get-tuple-element.127), channel_id=1, source_target_pairs={{0,8},{2,10},{4,12},{6,14},{8,0},{10,2},{12,4},{14,6},{16,24},{18,... | collective-permute-start | bytes 884744 | tf_op jit(solution)/shard_map/ppermute | solution.py:467
  312.9 19.4 %collective-permute-start.25 = (bf16[512,256]{1,0:T(8,128)(2,1)S(1)}, bf16[512,256]{1,0:T(8,128)(2,1)S(1)}, u32[]{:S(2)}, u32[]{:S(2)}) collective-permute-start(bf16[512,256]{1,0:T(8,128)(2,1)S(1)} %get-tuple-element.141), channel_id=1, source_target_pairs={{0,4},{2,6},{4,0},{6,2},{8,12},{10,14},{12,8},{14,10},{16,20},{18,... | collective-permute-start | bytes 786440 | tf_op jit(solution)/shard_map/ppermute | solution.py:596
  319.2 13.1 %collective-permute-start.27 = (bf16[512,256]{1,0:T(8,128)(2,1)S(1)}, bf16[512,256]{1,0:T(8,128)(2,1)S(1)}, u32[]{:S(2)}, u32[]{:S(2)}) collective-permute-start(bf16[512,256]{1,0:T(8,128)(2,1)S(1)} %get-tuple-element.140), channel_id=1, source_target_pairs={{0,2},{2,0},{4,6},{6,4},{8,10},{10,8},{12,14},{14,12},{16,18},{18,... | collective-permute-start | bytes 786440 | tf_op jit(solution)/shard_map/ppermute | solution.py:596
  320.8 11.5 %collective-permute-start.30 = (bf16[512,256]{1,0:T(8,128)(2,1)S(1)}, bf16[512,256]{1,0:T(8,128)(2,1)S(1)}, u32[]{:S(2)}, u32[]{:S(2)}) collective-permute-start(bf16[512,256]{1,0:T(8,128)(2,1)S(1)} %get-tuple-element.138), channel_id=1, source_target_pairs={{0,6},{2,4},{4,2},{6,0},{8,14},{10,12},{12,10},{14,8},{16,22},{18,... | collective-permute-start | bytes 786440 | tf_op jit(solution)/shard_map/ppermute | solution.py:596
  329.0 7.4 %collective-permute-start.31 = (bf16[512,256]{1,0:T(8,128)(2,1)S(1)}, bf16[512,256]{1,0:T(8,128)(2,1)S(1)}, u32[]{:S(2)}, u32[]{:S(2)}) collective-permute-start(bf16[512,256]{1,0:T(8,128)(2,1)S(1)} %get-tuple-element.137), channel_id=1, source_target_pairs={{0,4},{2,6},{4,0},{6,2},{8,12},{10,14},{12,8},{14,10},{16,20},{18,... | collective-permute-start | bytes 786440 | tf_op jit(solution)/shard_map/ppermute | solution.py:596
  329.9 6.5 %collective-permute-start.33 = (bf16[512,256]{1,0:T(8,128)(2,1)S(1)}, bf16[512,256]{1,0:T(8,128)(2,1)S(1)}, u32[]{:S(2)}, u32[]{:S(2)}) collective-permute-start(bf16[512,256]{1,0:T(8,128)(2,1)S(1)} %get-tuple-element.136), channel_id=1, source_target_pairs={{0,2},{2,0},{4,6},{6,4},{8,10},{10,8},{12,14},{14,12},{16,18},{18,... | collective-permute-start | bytes 786440 | tf_op jit(solution)/shard_map/ppermute | solution.py:596
  (3 other events, 3.2 us)

commit v6 on v5

--- a/solution.py
+++ b/solution.py
@@ -609,7 +609,7 @@
         held["w", h] = lax.ppermute(held["w", h], "tensor", pair_swap)
         if h:
             held.gate(("third sum", h), "mine")
-            for k in (1, 2, 3):
+            for k in (3, 2, 1):
                 send_sums(k)
     for h in (1, 0):
         give_out(0, h, held["total", h])

time: 342 us -> 342 us (level)
  no operation moved by 1% of the time
where the time goes in v6:
time: 342 us; the launch traced here: 340 us
  waiting for transfers between devices  112 us (33%)
  Pallas kernels  95.3 us (28%)
  starting transfers between devices  66.4 us (19%)
  local copies, waits for them, and re-layouts  36.9 us (11%)
  other arithmetic  28.5 us (8%)
    pallas_call x12, Pallas kernels, product(): pl.pallas_call(kernel, out_shape=shapes if several else shape, in_specs=i...  77.9 us
    ppermute x8, waiting for transfers between devices, send_weight(): held[name, s] = lax.ppermute(sent, 'dp', line_pairs(sources, sign))  76.7 us
    unnamed x62, local copies, waits for them, and re-layouts  20.8 us
    ppermute x8, starting transfers between devices, send_weight(): held[name, s] = lax.ppermute(sent, 'dp', line_pairs(sources, sign))  20.1 us
    ppermute x7, starting transfers between devices, over_core(): held[result or name] = lax.ppermute(held[name], 'dp', core_swap)  17.4 us
    ppermute x4, waiting for transfers between devices, send_hidden(): held['x', i] = lax.ppermute(held['x', i], 'dp', x_swap)  16.3 us
    select_n x5, other arithmetic, send_weight(): sent = jnp.where(jnp.logical_and(early, z == last), other, sent)  13.9 us
    ppermute x3, starting transfers between devices, send_sums(): held['got', k] = lax.ppermute(sent, 'dp', pairs)  7.92 us
  transfers between devices with their start and end apart: 37, of which 16 were waited for; matrix products, arithmetic and copies ran while one was open for 13% of the time, Pallas kernels for 27%

profile of v6, /device:TPU:1, one launch (start us, length us, event | category | flops | bytes accessed | tf_op | source)
XLA Modules:
  0.0 340.0 jit_solution(2632605312094362893)
XLA Ops:
  0.8 3.0 slice.88
  5.0 6.6 %collective-permute-start.1 = (bf16[3584,256]{1,0:T(8,128)(2,1)}, bf16[3584,256]{1,0:T(8,128)(2,1)}, u32[]{:S(2)}, u32[]{:S(2)}) collective-permute-start(bf16[3584,256]{1,0:T(8,128)(2,1)} %slice.88), channel_id=1, source_target_pairs={{0,8},{2,10},{4,12},{6,14},{8,16},{10,18},{12,20},{14,22},{16,24},... | collective-permute-start | bytes 5505032 | tf_op jit(solution)/shard_map/ppermute | solution.py:451
  11.6 4.3 %fusion.15 = (bf16[128,7168]{1,0:T(8,128)(2,1)}, bf16[128,7168]{1,0:T(8,128)(2,1)}) fusion(bf16[512,7168]{1,0:T(8,128)(2,1)} %refs_7_.5), kind=kLoop, calls=%fused_computation.58 | loop fusion | bytes 7340032 | tf_op jit(solution)/shard_map/slice | solution.py:456
  15.9 1.4 collective-permute-start.2
  17.3 2.0 copy-done.25
  19.3 5.8 %shard_map.76.own = f32[512,640]{1,0:T(8,128)S(1)} custom-call(bf16[512,7168]{1,0:T(8,128)(2,1)S(1)} %copy-done, bf16[256,7168]{1,0:T(8,128)(2,1)S(1)} %copy-done.25, bf16[512,2048]{1,0:T(8,128)(2,1)S(1)} %copy-done.18, bf16[256,2048]{1,0:T(8,128)(2,1)S(1)} %copy-done.26), custom_call_target="tpu_custom_call" | custom-call | flops 24159192 | bytes 141557 | tf_op jit(solution)/shard_map/pallas_call | solution.py:280
  25.2 1.3 collective-permute-start.7
  26.5 22.5 %collective-permute-done.refs_3_.refs_1_ = bf16[3584,256]{1,0:T(8,128)(2,1)S(1)} collective-permute-done((bf16[3584,256]{1,0:T(8,128)(2,1)}, bf16[3584,256]{1,0:T(8,128)(2,1)S(1)}, u32[]{:S(2)}, u32[]{:S(2)}) %collective-permute-start) | collective-permute-done | bytes 1835040 | tf_op jit(solution)/shard_map/ppermute | solution.py:451
  50.0 7.5 %collective-permute-done.2.refs_7_.refs_2_.refs_11_ = bf16[128,7168]{1,0:T(8,128)(2,1)} collective-permute-done((bf16[128,7168]{1,0:T(8,128)(2,1)}, bf16[128,7168]{1,0:T(8,128)(2,1)}, u32[]{:S(2)}, u32[]{:S(2)}) %collective-permute-start.2) | collective-permute-done | bytes 1835040 | tf_op jit(solution)/shard_map/ppermute | solution.py:454
  57.5 3.6 %broadcast_select_fusion.2 = (bf16[3584,256]{1,0:T(8,128)(2,1)}, bf16[3584,256]{1,0:T(8,128)(2,1)}) fusion(bf16[3584,256]{1,0:T(8,128)(2,1)} %collective-permute-done.1.refs_4_.refs_2_, pred[]{:T(512)S(6)} %and.100, bf16[7168,256]{1,0:T(8,128)(2,1)} %refs_1_.5, bf16[3584,256]{1,0:T(8,128)(2,1)S(1)} %collective-permute-done.refs_3_.refs_1_, pred[]{:T(512)S(6)} %and.99), kind=kLoop, calls=%fused_computation.6 | loop fusion | flops 1835008 | bytes 9175042 | tf_op jit(solution)/shard_map/jit(_where)/select_n | solution.py:449
  62.4 5.2 %collective-permute-start.4 = (bf16[3584,256]{1,0:T(8,128)(2,1)}, bf16[3584,256]{1,0:T(8,128)(2,1)}, u32[]{:S(2)}, u32[]{:S(2)}) collective-permute-start(bf16[3584,256]{1,0:T(8,128)(2,1)} %get-tuple-element.125), channel_id=1, source_target_pairs={{0,8},{2,10},{4,12},{6,14},{8,16},{10,18},{12,20},{14,22},{16,24},... | collective-permute-start | bytes 5505032 | tf_op jit(solution)/shard_map/ppermute | solution.py:451
  68.9 3.1 copy-done.1
  72.0 1.6 copy-done.19
  73.6 7.9 %shard_map.77 = (bf16[512,256]{1,0:T(8,128)(2,1)S(1)}, f32[128,9216]{1,0:T(8,128)S(1)}, f32[128,9216]{1,0:T(8,128)S(1)}) custom-call(f32[512,640]{1,0:T(8,128)S(1)} %shard_map.76.own, f32[512,640]{1,0:T(8,128)} %collective-permute-done.7.other, bf16[256,256]{1,0:T(8,128)(2,1)S(1)} %fusion.5.order, bf16[512,7168]{1,0:T(8,128)(2,1)S(1)} %copy-done.1, ...), custom_call_target="tpu_custom_call" | custom-call | flops 24159192 | bytes 188743 | tf_op jit(solution)/shard_map/pallas_call | solution.py:360
  81.5 2.2 copy-done.20
  83.7 2.3 collective-permute-start.12
  86.0 1.4 slice.92
  87.4 16.3 %collective-permute-done.3.refs_1_.refs_7_ = bf16[3584,256]{1,0:T(8,128)(2,1)} collective-permute-done((bf16[3584,256]{1,0:T(8,128)(2,1)}, bf16[3584,256]{1,0:T(8,128)(2,1)}, u32[]{:S(2)}, u32[]{:S(2)}) %collective-permute-start.3) | collective-permute-done | bytes 1835040 | tf_op jit(solution)/shard_map/ppermute | solution.py:451
  103.7 2.1 collective-permute-start.11
  105.8 2.0 collective-permute-done.5.refs_8_.refs_3_.refs_12_
  107.8 1.4 broadcast_select_fusion.4
  109.2 1.5 collective-permute-start.8
  110.8 2.9 broadcast_select_fusion.1
  115.4 1.3 slice.93
  116.7 6.2 %shard_map.78.refs_15_ = f32[1024,256]{1,0:T(8,128)S(1)} custom-call(s32[1]{0:T(128)} %constant.117.clone.1.refs_0_, bf16[7168,256]{1,0:T(8,128)(2,1)S(1)} %copy-done.9, bf16[512,7168]{1,0:T(8,128)(2,1)S(1)} %bitcast.27, bf16[512,7168]{1,0:T(8,128)(2,1)} %collective-permute-done.6.refs_3_.refs_8_.refs_12_), custom_call_target="tpu_custom_call" | custom-call | flops 37580964 | bytes 183500 | tf_op jit(solution)/shard_map/pallas_call | solution.py:225
  123.0 3.3 collective-permute-start.16
  126.3 24.3 %collective-permute-done.8.refs_5_ = bf16[3584,256]{1,0:T(8,128)(2,1)S(1)} collective-permute-done((bf16[3584,256]{1,0:T(8,128)(2,1)}, bf16[3584,256]{1,0:T(8,128)(2,1)S(1)}, u32[]{:S(2)}, u32[]{:S(2)}) %collective-permute-start.8) | collective-permute-done | bytes 1835040 | tf_op jit(solution)/shard_map/ppermute | solution.py:451
  150.6 3.3 collective-permute-done.10.refs_7_.refs_2_.refs_9_.refs_13_
  153.9 2.9 broadcast_select_fusion.3
  158.1 3.0 broadcast_select_fusion
  161.1 2.0 collective-permute-start.14
  163.5 4.1 %collective-permute-start.17 = (bf16[128,7168]{1,0:T(8,128)(2,1)}, bf16[128,7168]{1,0:T(8,128)(2,1)}, u32[]{:S(2)}, u32[]{:S(2)}) collective-permute-start(bf16[128,7168]{1,0:T(8,128)(2,1)} %collective-permute-done.10.refs_7_.refs_2_.refs_9_.refs_13_), channel_id=1, source_target_pairs={{0,2},{2,0},{4,6},{6,4},{8,10},{10,8},{12,14},{14,12},{16,18},{18,... | collective-permute-start | bytes 5505032 | tf_op jit(solution)/shard_map/ppermute | solution.py:459
  167.8 4.3 %add.139 = f32[128,9216]{1,0:T(8,128)S(1)} add(f32[128,9216]{1,0:T(8,128)} %copy-done.20, f32[128,9216]{1,0:T(8,128)} %collective-permute-done.12) | non-fusion elementwise | flops 1179648 | bytes 14155776 | tf_op jit(solution)/shard_map/add | solution.py:534
  174.3 8.6 %shard_map.79.refs_14_ = f32[1024,256]{1,0:T(8,128)S(1)} custom-call(s32[2]{0:T(128)S(1)} %pad_add_fusion.1.refs_0_, bf16[3584,256]{1,0:T(8,128)(2,1)} %collective-permute-done.3.refs_1_.refs_7_, bf16[3584,256]{1,0:T(8,128)(2,1)} %collective-permute-done.4.refs_2_.refs_8_, bf16[3584,256]{1,0:T(8,128)(2,1)S(1)} %collective-permute-done.refs_3_.refs_1_, ...), custom_call_target="tpu_custom_call" | custom-call | flops 37580964 | bytes 183500 | tf_op jit(solution)/shard_map/pallas_call | solution.py:225
  185.2 12.6 %collective-permute-done.13.refs_1_.refs_9_.refs_5_ = bf16[3584,256]{1,0:T(8,128)(2,1)} collective-permute-done((bf16[3584,256]{1,0:T(8,128)(2,1)}, bf16[3584,256]{1,0:T(8,128)(2,1)}, u32[]{:S(2)}, u32[]{:S(2)}) %collective-permute-start.13) | collective-permute-done | bytes 1835040 | tf_op jit(solution)/shard_map/ppermute | solution.py:451
  197.8 3.5 %collective-permute-done.15.refs_8_.refs_3_.refs_10_.refs_14_ = bf16[128,7168]{1,0:T(8,128)(2,1)} collective-permute-done((bf16[128,7168]{1,0:T(8,128)(2,1)}, bf16[128,7168]{1,0:T(8,128)(2,1)}, u32[]{:S(2)}, u32[]{:S(2)}) %collective-permute-start.15) | collective-permute-done | bytes 1835040 | tf_op jit(solution)/shard_map/ppermute | solution.py:454
  201.3 4.5 %collective-permute-start.20 = (bf16[128,7168]{1,0:T(8,128)(2,1)}, bf16[128,7168]{1,0:T(8,128)(2,1)S(1)}, u32[]{:S(2)}, u32[]{:S(2)}) collective-permute-start(bf16[128,7168]{1,0:T(8,128)(2,1)} %collective-permute-done.15.refs_8_.refs_3_.refs_10_.refs_14_), channel_id=1, source_target_pairs={{0,2},{2,0},{4,6},{6,4},{8,10},{10,8},{12,14},{14,12},{16,18},{18,... | collective-permute-start | bytes 5505032 | tf_op jit(solution)/shard_map/ppermute | solution.py:459
  207.3 3.8 %slice_select_fusion = (bf16[3584,256]{1,0:T(8,128)(2,1)}, bf16[3584,256]{1,0:T(8,128)(2,1)}) fusion(bf16[7168,256]{1,0:T(8,128)(2,1)S(1)} %copy-done.10, pred[]{:T(512)S(6)} %and.98, bf16[3584,256]{1,0:T(8,128)(2,1)} %collective-permute-done.13.refs_1_.refs_9_.refs_5_, bf16[3584,256]{1,0:T(8,128)(2,1)} %collective-permute-done.14.refs_2_.refs_10_.refs_6_, ...), kind=kLoop, calls=%fused_computation.2 | loop fusion | flops 3670016 | bytes 12845058 | tf_op jit(solution)/shard_map/jit(_where)/select_n | solution.py:441
  214.9 4.3 %shard_map.82 = f32[512,256]{1,0:T(8,128)S(1)} custom-call(s32[1]{0:T(128)} %constant.117.clone.1.refs_0_, bf16[7168,256]{1,0:T(8,128)(2,1)S(1)} %copy-done.10, bf16[128,7168]{1,0:T(8,128)(2,1)} %collective-permute-done.2.refs_7_.refs_2_.refs_11_, bf16[128,7168]{1,0:T(8,128)(2,1)} %collective-permute-done.5.refs_8_.refs_3_.refs_12_, ...), custom_call_target="tpu_custom_call" | custom-call | flops 18790480 | bytes 110100 | tf_op jit(solution)/shard_map/pallas_call | solution.py:225
  219.2 5.4 %shard_map.80 = f32[512,256]{1,0:T(8,128)S(1)} custom-call(s32[2]{0:T(128)S(1)} %pad_add_fusion.1.refs_0_, bf16[3584,256]{1,0:T(8,128)(2,1)} %collective-permute-done.3.refs_1_.refs_7_, bf16[3584,256]{1,0:T(8,128)(2,1)} %collective-permute-done.4.refs_2_.refs_8_, bf16[3584,256]{1,0:T(8,128)(2,1)S(1)} %collective-permute-done.refs_3_.refs_1_, ...), custom_call_target="tpu_custom_call" | custom-call | flops 18790480 | bytes 110100 | tf_op jit(solution)/shard_map/pallas_call | solution.py:225
  224.8 5.0 %shard_map.83 = f32[512,256]{1,0:T(8,128)S(1)} custom-call(s32[1]{0:T(128)} %constant.117.clone.1.refs_0_, bf16[7168,256]{1,0:T(8,128)(2,1)S(1)} %copy-done.10, bf16[128,7168]{1,0:T(8,128)(2,1)} %collective-permute-done.10.refs_7_.refs_2_.refs_9_.refs_13_, bf16[128,7168]{1,0:T(8,128)(2,1)} %collective-permute-done.15.refs_8_.refs_3_.refs_10_.refs_14_, ...), custom_call_target="tpu_custom_call" | custom-call | flops 18790480 | bytes 110100 | tf_op jit(solution)/shard_map/pallas_call | solution.py:225
  229.8 5.4 %shard_map.81 = f32[512,256]{1,0:T(8,128)S(1)} custom-call(s32[2]{0:T(128)S(1)} %pad_add_fusion.1.refs_0_, bf16[3584,256]{1,0:T(8,128)(2,1)} %collective-permute-done.3.refs_1_.refs_7_, bf16[3584,256]{1,0:T(8,128)(2,1)} %collective-permute-done.4.refs_2_.refs_8_, bf16[3584,256]{1,0:T(8,128)(2,1)S(1)} %collective-permute-done.refs_3_.refs_1_, ...), custom_call_target="tpu_custom_call" | custom-call | flops 18790480 | bytes 110100 | tf_op jit(solution)/shard_map/pallas_call | solution.py:225
  235.3 1.8 pad_maximum_fusion.2
  237.1 2.5 collective-permute-start.22
  240.2 3.0 convert_add_fusion
  245.0 1.5 copy-done.4
  246.5 1.5 copy-done.8
  248.0 5.5 %shard_map.84.refs_13_ = f32[1024,256]{1,0:T(8,128)S(1)} custom-call(s32[1]{0:T(128)} %bitcast.9.refs_0_, bf16[3584,256]{1,0:T(8,128)(2,1)} %collective-permute-done.13.refs_1_.refs_9_.refs_5_, bf16[3584,256]{1,0:T(8,128)(2,1)} %collective-permute-done.14.refs_2_.refs_10_.refs_6_, bf16[3584,256]{1,0:T(8,128)(2,1)S(1)} %collective-permute-done.refs_3_.refs_1_, ...), custom_call_target="tpu_custom_call" | custom-call | flops 18790480 | bytes 91750 | tf_op jit(solution)/shard_map/pallas_call | solution.py:225
  253.5 5.4 %shard_map.85.refs_19_ = f32[1024,256]{1,0:T(8,128)S(1)} custom-call(s32[1]{0:T(128)} %bitcast.9.refs_0_, bf16[3584,256]{1,0:T(8,128)(2,1)} %collective-permute-done.13.refs_1_.refs_9_.refs_5_, bf16[3584,256]{1,0:T(8,128)(2,1)} %collective-permute-done.14.refs_2_.refs_10_.refs_6_, bf16[3584,256]{1,0:T(8,128)(2,1)S(1)} %collective-permute-done.refs_3_.refs_1_, ...), custom_call_target="tpu_custom_call" | custom-call | flops 18790480 | bytes 91750 | tf_op jit(solution)/shard_map/pallas_call | solution.py:225
  260.0 3.0 collective-permute-done.22.refs_22_
  266.5 1.5 copy-done.5
  270.5 10.1 %shard_map.86 = (bf16[1024,256]{1,0:T(8,128)(2,1)S(1)}, bf16[1024,256]{1,0:T(8,128)(2,1)S(1)}, f32[1024,256]{1,0:T(8,128)S(1)}) custom-call(s32[3]{0:T(128)S(1)} %pad_add_fusion.refs_0_, bf16[3584,256]{1,0:T(8,128)(2,1)S(1)} %collective-permute-done.refs_3_.refs_1_, bf16[3584,256]{1,0:T(8,128)(2,1)} %collective-permute-done.1.refs_4_.refs_2_, ...), custom_call_target="tpu_custom_call" | custom-call | flops 37580964 | bytes 183500 | tf_op jit(solution)/shard_map/pallas_call | solution.py:225
  280.7 1.3 collective-permute-start.24
  282.0 2.5 collective-permute-start.29
  284.5 10.7 %shard_map.87 = (bf16[1024,256]{1,0:T(8,128)(2,1)S(1)}, bf16[1024,256]{1,0:T(8,128)(2,1)S(1)}, f32[1024,256]{1,0:T(8,128)S(1)}) custom-call(s32[3]{0:T(128)S(1)} %pad_add_fusion.refs_0_, bf16[3584,256]{1,0:T(8,128)(2,1)S(1)} %collective-permute-done.refs_3_.refs_1_, bf16[3584,256]{1,0:T(8,128)(2,1)} %collective-permute-done.1.refs_4_.refs_2_, ...), custom_call_target="tpu_custom_call" | custom-call | flops 37580964 | bytes 183500 | tf_op jit(solution)/shard_map/pallas_call | solution.py:225
  296.0 3.3 collective-permute-done.28.refs_3_.refs_4_
  299.3 2.9 collective-permute-start.36
  302.2 4.9 %collective-permute-start.35 = (bf16[16,9216]{1,0:T(8,128)(2,1)S(1)}, bf16[16,9216]{1,0:T(8,128)(2,1)S(1)}, u32[]{:S(2)}, u32[]{:S(2)}) collective-permute-start(bf16[16,9216]{1,0:T(8,128)(2,1)S(1)} %get-tuple-element.129), channel_id=1, source_target_pairs={{0,16},{2,18},{4,20},{6,22},{8,24},{10,26},{12,28},{14,30},{16,0},... | collective-permute-start | bytes 884744 | tf_op jit(solution)/shard_map/ppermute | solution.py:467
  307.3 5.6 %shard_map.88 = bf16[1024,256]{1,0:T(8,128)(2,1)S(1)} custom-call(s32[1]{0:T(128)} %bitcast.13.refs_0_, bf16[3584,256]{1,0:T(8,128)(2,1)} %collective-permute-done.3.refs_1_.refs_7_, bf16[3584,256]{1,0:T(8,128)(2,1)} %collective-permute-done.4.refs_2_.refs_8_, bf16[3584,256]{1,0:T(8,128)(2,1)} %collective-permute-done.28.refs_3_.refs_4_, ...), custom_call_target="tpu_custom_call" | custom-call | flops 18790480 | bytes 91750 | tf_op jit(solution)/shard_map/pallas_call | solution.py:225
  313.5 5.7 %shard_map.89 = bf16[1024,256]{1,0:T(8,128)(2,1)S(1)} custom-call(s32[1]{0:T(128)} %bitcast.13.refs_0_, bf16[3584,256]{1,0:T(8,128)(2,1)} %collective-permute-done.3.refs_1_.refs_7_, bf16[3584,256]{1,0:T(8,128)(2,1)} %collective-permute-done.4.refs_2_.refs_8_, bf16[3584,256]{1,0:T(8,128)(2,1)} %collective-permute-done.28.refs_3_.refs_4_, ...), custom_call_target="tpu_custom_call" | custom-call | flops 18790480 | bytes 91750 | tf_op jit(solution)/shard_map/pallas_call | solution.py:225
  319.2 1.6 collective-permute-start.27
  321.8 7.2 %collective-permute-done.35 = bf16[16,9216]{1,0:T(8,128)(2,1)S(1)} collective-permute-done((bf16[16,9216]{1,0:T(8,128)(2,1)S(1)}, bf16[16,9216]{1,0:T(8,128)(2,1)S(1)}, u32[]{:S(2)}, u32[]{:S(2)}) %collective-permute-start.35) | collective-permute-done | bytes 294944 | tf_op jit(solution)/shard_map/ppermute | solution.py:467
  332.3 4.1 %collective-permute-done.31.refs_5_ = bf16[512,256]{1,0:T(8,128)(2,1)S(1)} collective-permute-done((bf16[512,256]{1,0:T(8,128)(2,1)S(1)}, bf16[512,256]{1,0:T(8,128)(2,1)S(1)}, u32[]{:S(2)}, u32[]{:S(2)}) %collective-permute-start.31) | collective-permute-done | bytes 262176 | tf_op jit(solution)/shard_map/ppermute | solution.py:596
  336.4 3.6 %shard_map.90 = bf16[512,2048]{1,0:T(8,128)(2,1)} custom-call(s32[8]{0:T(128)S(1)} %stack.35.code, bf16[512,256]{1,0:T(8,128)(2,1)S(1)} %collective-permute-done.24.refs_0_, bf16[512,256]{1,0:T(8,128)(2,1)S(1)} %collective-permute-done.25.refs_1_, bf16[512,256]{1,0:T(8,128)(2,1)S(1)} %collective-permute-done.27.refs_2_, ...), custom_call_target="tpu_custom_call" | custom-call | tf_op jit(solution)/shard_map/pallas_call | solution.py:393
  (128 shorter events, 33.4 us)
Async XLA Ops:
  0.6 107.2 %collective-permute-start.6 = (bf16[512,7168]{1,0:T(8,128)(2,1)}, bf16[512,7168]{1,0:T(8,128)(2,1)}, u32[]{:S(2)}, u32[]{:S(2)}) collective-permute-start(bf16[512,7168]{1,0:T(8,128)(2,1)} %refs_7_.5), channel_id=1, source_target_pairs={{0,2},{2,0},{4,6},{6,4},{8,10},{10,8},{12,14},{14,12},{16,18},{18,... | collective-permute-start | bytes 22020104 | tf_op jit(solution)/shard_map/ppermute | solution.py:505
  0.8 16.5 %copy-start.18 = (bf16[512,2048]{1,0:T(8,128)(2,1)S(1)}, bf16[512,2048]{1,0:T(8,128)(2,1)}, u32[]{:S(2)}) copy-start(bf16[512,2048]{1,0:T(8,128)(2,1)} %cotangent.3) | copy-start | bytes 6291460
  0.8 16.5 %copy-start.26 = (bf16[256,2048]{1,0:T(8,128)(2,1)S(1)}, bf16[256,2048]{1,0:T(8,128)(2,1)}, u32[]{:S(2)}) copy-start(bf16[256,2048]{1,0:T(8,128)(2,1)} %adapter_out.1) | copy-start | bytes 3145732
  3.8 45.3 %collective-permute-start = (bf16[3584,256]{1,0:T(8,128)(2,1)}, bf16[3584,256]{1,0:T(8,128)(2,1)S(1)}, u32[]{:S(2)}, u32[]{:S(2)}) collective-permute-start(bf16[3584,256]{1,0:T(8,128)(2,1)} %slice.88), channel_id=1, source_target_pairs={{8,0},{10,2},{12,4},{14,6},{16,8},{18,10},{20,12},{22,14},{24,16},... | collective-permute-start | bytes 5505032 | tf_op jit(solution)/shard_map/ppermute | solution.py:451
  5.0 45.0 %collective-permute-start.1 = (bf16[3584,256]{1,0:T(8,128)(2,1)}, bf16[3584,256]{1,0:T(8,128)(2,1)}, u32[]{:S(2)}, u32[]{:S(2)}) collective-permute-start(bf16[3584,256]{1,0:T(8,128)(2,1)} %slice.88), channel_id=1, source_target_pairs={{0,8},{2,10},{4,12},{6,14},{8,16},{10,18},{12,20},{14,22},{16,24},... | collective-permute-start | bytes 5505032 | tf_op jit(solution)/shard_map/ppermute | solution.py:451
  11.6 5.7 %copy-start = (bf16[512,7168]{1,0:T(8,128)(2,1)S(1)}, bf16[512,7168]{1,0:T(8,128)(2,1)}, u32[]{:S(2)}) copy-start(bf16[512,7168]{1,0:T(8,128)(2,1)} %refs_7_.5) | copy-start | bytes 22020100
  15.9 41.6 %collective-permute-start.2 = (bf16[128,7168]{1,0:T(8,128)(2,1)}, bf16[128,7168]{1,0:T(8,128)(2,1)}, u32[]{:S(2)}, u32[]{:S(2)}) collective-permute-start(bf16[128,7168]{1,0:T(8,128)(2,1)} %get-tuple-element.122), channel_id=1, source_target_pairs={{0,4},{2,6},{4,0},{6,2},{8,12},{10,14},{12,8},{14,10},{16,20},{18,... | collective-permute-start | bytes 5505032 | tf_op jit(solution)/shard_map/ppermute | solution.py:454
  17.3 2.0 copy-start.25
  25.2 43.7 %collective-permute-start.7 = (f32[512,640]{1,0:T(8,128)S(1)}, f32[512,640]{1,0:T(8,128)}, u32[]{:S(2)}, u32[]{:S(2)}) collective-permute-start(f32[512,640]{1,0:T(8,128)S(1)} %shard_map.76.own), channel_id=1, source_target_pairs={{0,1},{1,0},{2,3},{3,2},{4,5},{5,4},{6,7},{7,6},{8,9},{9,8},{10,11... | collective-permute-start | bytes 3932168 | tf_op jit(solution)/shard_map/ppermute | solution.py:507
  61.2 42.6 %collective-permute-start.3 = (bf16[3584,256]{1,0:T(8,128)(2,1)}, bf16[3584,256]{1,0:T(8,128)(2,1)}, u32[]{:S(2)}, u32[]{:S(2)}) collective-permute-start(bf16[3584,256]{1,0:T(8,128)(2,1)} %get-tuple-element.126), channel_id=1, source_target_pairs={{8,0},{10,2},{12,4},{14,6},{16,8},{18,10},{20,12},{22,14},{24,16},... | collective-permute-start | bytes 5505032 | tf_op jit(solution)/shard_map/ppermute | solution.py:451
  62.4 43.3 %collective-permute-start.4 = (bf16[3584,256]{1,0:T(8,128)(2,1)}, bf16[3584,256]{1,0:T(8,128)(2,1)}, u32[]{:S(2)}, u32[]{:S(2)}) collective-permute-start(bf16[3584,256]{1,0:T(8,128)(2,1)} %get-tuple-element.125), channel_id=1, source_target_pairs={{0,8},{2,10},{4,12},{6,14},{8,16},{10,18},{12,20},{14,22},{16,24},... | collective-permute-start | bytes 5505032 | tf_op jit(solution)/shard_map/ppermute | solution.py:451
  67.7 40.1 %collective-permute-start.5 = (bf16[128,7168]{1,0:T(8,128)(2,1)}, bf16[128,7168]{1,0:T(8,128)(2,1)}, u32[]{:S(2)}, u32[]{:S(2)}) collective-permute-start(bf16[128,7168]{1,0:T(8,128)(2,1)} %get-tuple-element.65), channel_id=1, source_target_pairs={{0,4},{2,6},{4,0},{6,2},{8,12},{10,14},{12,8},{14,10},{16,20},{18,... | collective-permute-start | bytes 5505032 | tf_op jit(solution)/shard_map/ppermute | solution.py:454
  68.9 3.1 copy-start.1
  72.0 1.6 copy-start.19
  81.5 2.2 copy-start.20
  83.7 42.6 %collective-permute-start.12 = (f32[128,9216]{1,0:T(8,128)S(1)}, f32[128,9216]{1,0:T(8,128)}, u32[]{:S(2)}, u32[]{:S(2)}) collective-permute-start(f32[128,9216]{1,0:T(8,128)S(1)} %get-tuple-element.75), channel_id=1, source_target_pairs={{0,2},{2,0},{4,6},{6,4},{8,10},{10,8},{12,14},{14,12},{16,18},{18,... | collective-permute-start | bytes 14155784 | tf_op jit(solution)/shard_map/ppermute | solution.py:459
  103.7 19.2 %collective-permute-start.11 = (bf16[128,7168]{1,0:T(8,128)(2,1)}, bf16[128,7168]{1,0:T(8,128)(2,1)S(1)}, u32[]{:S(2)}, u32[]{:S(2)}) collective-permute-start(bf16[128,7168]{1,0:T(8,128)(2,1)} %collective-permute-done.2.refs_7_.refs_2_.refs_11_), channel_id=1, source_target_pairs={{0,2},{2,0},{4,6},{6,4},{8,10},{10,8},{12,14},{14,12},{16,18},{18,... | collective-permute-start | bytes 5505032 | tf_op jit(solution)/shard_map/ppermute | solution.py:459
  107.8 8.9 %slice-start = ((s8[7340032]{0:T(1024)(128)(4,1)}), s8[4194304]{0:T(1024)(128)(4,1)S(1)}, s32[]{:S(2)}) async-start(s8[7340032]{0:T(1024)(128)(4,1)} %bitcast.26), calls=%async_computation | async-start | bytes 8388608
  109.2 7.5 %slice-start.1 = ((s8[7340032]{0:T(1024)(128)(4,1)}), s8[3145728]{0:T(1024)(128)(4,1)S(1)}, s32[]{:S(2)}) async-start(s8[7340032]{0:T(1024)(128)(4,1)} %bitcast.26), calls=%async_computation.1 | async-start | bytes 6291456
  109.2 41.3 %collective-permute-start.8 = (bf16[3584,256]{1,0:T(8,128)(2,1)}, bf16[3584,256]{1,0:T(8,128)(2,1)S(1)}, u32[]{:S(2)}, u32[]{:S(2)}) collective-permute-start(bf16[3584,256]{1,0:T(8,128)(2,1)} %broadcast_select_fusion.4), channel_id=1, source_target_pairs={{8,0},{10,2},{12,4},{14,6},{16,8},{18,10},{20,12},{22,14},{9,1},{1... | collective-permute-start | bytes 5505032 | tf_op jit(solution)/shard_map/ppermute | solution.py:451
  113.7 3.0 copy-start.9
  113.7 36.9 %collective-permute-start.9 = (bf16[3584,256]{1,0:T(8,128)(2,1)}, bf16[3584,256]{1,0:T(8,128)(2,1)S(1)}, u32[]{:S(2)}, u32[]{:S(2)}) collective-permute-start(bf16[3584,256]{1,0:T(8,128)(2,1)} %broadcast_select_fusion.1), channel_id=1, source_target_pairs={{8,16},{10,18},{12,20},{14,22},{16,24},{18,26},{20,28},{22,30},{9,... | collective-permute-start | bytes 5505032 | tf_op jit(solution)/shard_map/ppermute | solution.py:451
  114.6 39.3 %collective-permute-start.10 = (bf16[128,7168]{1,0:T(8,128)(2,1)}, bf16[128,7168]{1,0:T(8,128)(2,1)}, u32[]{:S(2)}, u32[]{:S(2)}) collective-permute-start(bf16[128,7168]{1,0:T(8,128)(2,1)} %slice.92), channel_id=1, source_target_pairs={{0,4},{2,6},{4,0},{6,2},{8,12},{10,14},{12,8},{14,10},{16,20},{18,... | collective-permute-start | bytes 5505032 | tf_op jit(solution)/shard_map/ppermute | solution.py:454
  123.0 33.8 %copy-start.11 = (bf16[128,7168]{1,0:T(8,128)(2,1)}, bf16[128,7168]{1,0:T(8,128)(2,1)S(1)}, u32[]{:S(2)}) copy-start(bf16[128,7168]{1,0:T(8,128)(2,1)S(1)} %collective-permute-done.11.refs_9_.refs_4_.refs_11_.refs_15_) | copy-start | bytes 5505028
  123.0 62.2 %collective-permute-start.16 = (bf16[128,7168]{1,0:T(8,128)(2,1)}, bf16[128,7168]{1,0:T(8,128)(2,1)}, u32[]{:S(2)}, u32[]{:S(2)}) collective-permute-start(bf16[128,7168]{1,0:T(8,128)(2,1)} %collective-permute-done.5.refs_8_.refs_3_.refs_12_), channel_id=1, source_target_pairs={{0,2},{2,0},{4,6},{6,4},{8,10},{10,8},{12,14},{14,12},{16,18},{18,... | collective-permute-start | bytes 5505032 | tf_op jit(solution)/shard_map/ppermute | solution.py:459
  150.6 6.2 %copy-start.2 = (bf16[3584,256]{1,0:T(8,128)(2,1)}, bf16[3584,256]{1,0:T(8,128)(2,1)S(1)}, u32[]{:S(2)}) copy-start(bf16[3584,256]{1,0:T(8,128)(2,1)S(1)} %collective-permute-done.8.refs_5_) | copy-start | bytes 5505028
  150.6 7.5 %copy-start.6 = (bf16[3584,256]{1,0:T(8,128)(2,1)}, bf16[3584,256]{1,0:T(8,128)(2,1)S(1)}, u32[]{:S(2)}) copy-start(bf16[3584,256]{1,0:T(8,128)(2,1)S(1)} %collective-permute-done.9.refs_6_) | copy-start | bytes 5505028
  156.8 41.0 %collective-permute-start.13 = (bf16[3584,256]{1,0:T(8,128)(2,1)}, bf16[3584,256]{1,0:T(8,128)(2,1)}, u32[]{:S(2)}, u32[]{:S(2)}) collective-permute-start(bf16[3584,256]{1,0:T(8,128)(2,1)} %broadcast_select_fusion.3), channel_id=1, source_target_pairs={{8,0},{10,2},{12,4},{14,6},{16,8},{18,10},{20,12},{22,14},{9,1},{1... | collective-permute-start | bytes 5505032 | tf_op jit(solution)/shard_map/ppermute | solution.py:451
  161.1 36.7 %collective-permute-start.14 = (bf16[3584,256]{1,0:T(8,128)(2,1)}, bf16[3584,256]{1,0:T(8,128)(2,1)}, u32[]{:S(2)}, u32[]{:S(2)}) collective-permute-start(bf16[3584,256]{1,0:T(8,128)(2,1)} %broadcast_select_fusion), channel_id=1, source_target_pairs={{8,16},{10,18},{12,20},{14,22},{16,24},{18,26},{20,28},{22,30},{9,... | collective-permute-start | bytes 5505032 | tf_op jit(solution)/shard_map/ppermute | solution.py:451
  163.0 38.3 %collective-permute-start.15 = (bf16[128,7168]{1,0:T(8,128)(2,1)}, bf16[128,7168]{1,0:T(8,128)(2,1)}, u32[]{:S(2)}, u32[]{:S(2)}) collective-permute-start(bf16[128,7168]{1,0:T(8,128)(2,1)} %slice.93), channel_id=1, source_target_pairs={{0,4},{2,6},{4,0},{6,2},{8,12},{10,14},{12,8},{14,10},{16,20},{18,... | collective-permute-start | bytes 5505032 | tf_op jit(solution)/shard_map/ppermute | solution.py:454
  163.5 37.9 %collective-permute-start.17 = (bf16[128,7168]{1,0:T(8,128)(2,1)}, bf16[128,7168]{1,0:T(8,128)(2,1)}, u32[]{:S(2)}, u32[]{:S(2)}) collective-permute-start(bf16[128,7168]{1,0:T(8,128)(2,1)} %collective-permute-done.10.refs_7_.refs_2_.refs_9_.refs_13_), channel_id=1, source_target_pairs={{0,2},{2,0},{4,6},{6,4},{8,10},{10,8},{12,14},{14,12},{16,18},{18,... | collective-permute-start | bytes 5505032 | tf_op jit(solution)/shard_map/ppermute | solution.py:459
  172.3 1.5 copy-start.3
  172.3 2.0 copy-start.7
  183.0 2.2 copy-start.16
  183.0 24.3 %copy-start.10 = (bf16[7168,256]{1,0:T(8,128)(2,1)S(1)}, bf16[7168,256]{1,0:T(8,128)(2,1)}, u32[]{:S(2)}) copy-start(bf16[7168,256]{1,0:T(8,128)(2,1)} %refs_1_.5) | copy-start | bytes 11010052
  201.3 23.4 %collective-permute-start.20 = (bf16[128,7168]{1,0:T(8,128)(2,1)}, bf16[128,7168]{1,0:T(8,128)(2,1)S(1)}, u32[]{:S(2)}, u32[]{:S(2)}) collective-permute-start(bf16[128,7168]{1,0:T(8,128)(2,1)} %collective-permute-done.15.refs_8_.refs_3_.refs_10_.refs_14_), channel_id=1, source_target_pairs={{0,2},{2,0},{4,6},{6,4},{8,10},{10,8},{12,14},{14,12},{16,18},{18,... | collective-permute-start | bytes 5505032 | tf_op jit(solution)/shard_map/ppermute | solution.py:459
  206.8 8.1 %copy-start.12 = (bf16[128,7168]{1,0:T(8,128)(2,1)S(1)}, bf16[128,7168]{1,0:T(8,128)(2,1)}, u32[]{:S(2)}) copy-start(bf16[128,7168]{1,0:T(8,128)(2,1)} %copy-done.11) | copy-start | bytes 5505028
  206.8 33.4 %collective-permute-start.19 = (bf16[64,11264]{1,0:T(8,128)(2,1)S(1)}, bf16[64,11264]{1,0:T(8,128)(2,1)}, u32[]{:S(2)}, u32[]{:S(2)}) collective-permute-start(bf16[64,11264]{1,0:T(8,128)(2,1)S(1)} %pad_maximum_fusion), channel_id=1, source_target_pairs={{0,4},{2,6},{4,0},{6,2},{8,12},{10,14},{12,8},{14,10},{16,20},{18,... | collective-permute-start | bytes 4325384 | tf_op jit(solution)/shard_map/ppermute | solution.py:545
  211.1 48.9 %collective-permute-start.18 = (bf16[3584,256]{1,0:T(8,128)(2,1)}, bf16[3584,256]{1,0:T(8,128)(2,1)}, u32[]{:S(2)}, u32[]{:S(2)}) collective-permute-start(bf16[3584,256]{1,0:T(8,128)(2,1)} %get-tuple-element.124), channel_id=1, source_target_pairs={{8,0},{10,2},{12,4},{14,6},{16,24},{18,26},{20,28},{22,30},{9,1},{... | collective-permute-start | bytes 5505032 | tf_op jit(solution)/shard_map/ppermute | solution.py:443
  212.4 47.5 %collective-permute-start.21 = (f32[1024,256]{1,0:T(8,128)}, f32[1024,256]{1,0:T(8,128)}, u32[]{:S(2)}, u32[]{:S(2)}) collective-permute-start(f32[1024,256]{1,0:T(8,128)} %broadcast_select_fusion.8), channel_id=1, source_target_pairs={{0,1},{1,0},{2,3},{3,2},{4,5},{5,4},{6,7},{7,6},{8,9},{9,8},{10,11... | collective-permute-start | bytes 3145736 | tf_op jit(solution)/shard_map/ppermute | solution.py:546
  213.6 85.7 %collective-permute-start.28 = (bf16[3584,256]{1,0:T(8,128)(2,1)}, bf16[3584,256]{1,0:T(8,128)(2,1)}, u32[]{:S(2)}, u32[]{:S(2)}) collective-permute-start(bf16[3584,256]{1,0:T(8,128)(2,1)} %get-tuple-element.123), channel_id=1, source_target_pairs={{8,0},{10,2},{12,4},{14,6},{16,24},{18,26},{20,28},{22,30},{9,1},{... | collective-permute-start | bytes 5505032 | tf_op jit(solution)/shard_map/ppermute | solution.py:443
  224.8 5.0 %copy-start.13 = (bf16[128,7168]{1,0:T(8,128)(2,1)}, bf16[128,7168]{1,0:T(8,128)(2,1)S(1)}, u32[]{:S(2)}) copy-start(bf16[128,7168]{1,0:T(8,128)(2,1)S(1)} %collective-permute-done.20.refs_10_.refs_5_.refs_14_.refs_18_) | copy-start | bytes 5505028
  237.1 25.9 %collective-permute-start.22 = (f32[1024,256]{1,0:T(8,128)}, f32[1024,256]{1,0:T(8,128)}, u32[]{:S(2)}, u32[]{:S(2)}) collective-permute-start(f32[1024,256]{1,0:T(8,128)} %get-tuple-element.133), channel_id=1, source_target_pairs={{0,1},{1,0},{2,3},{3,2},{4,5},{5,4},{6,7},{7,6},{8,9},{9,8},{10,11... | collective-permute-start | bytes 3145736 | tf_op jit(solution)/shard_map/ppermute | solution.py:561
  245.0 1.5 copy-start.4
  246.5 1.5 copy-start.8
  263.0 2.5 collective-permute-start.23
  264.2 2.3 copy-start.22
  264.2 20.3 %collective-permute-start.26 = (bf16[512,256]{1,0:T(8,128)(2,1)S(1)}, bf16[512,256]{1,0:T(8,128)(2,1)S(1)}, u32[]{:S(2)}, u32[]{:S(2)}) collective-permute-start(bf16[512,256]{1,0:T(8,128)(2,1)S(1)} %get-tuple-element.108), channel_id=1, source_target_pairs={{0,2},{2,0},{4,6},{6,4},{8,10},{10,8},{12,14},{14,12},{16,18},{18,... | collective-permute-start | bytes 786440 | tf_op jit(solution)/shard_map/ppermute | solution.py:459
  266.5 1.5 copy-start.5
  268.0 1.2 copy-start.23
  270.5 14.0 %copy-start.17 = (f32[1024,256]{1,0:T(8,128)S(1)}, f32[1024,256]{1,0:T(8,128)}, u32[]{:S(2)}) copy-start(f32[1024,256]{1,0:T(8,128)} %copy-done.16) | copy-start | bytes 3145732
  280.6 3.9 %copy-start.15 = (f32[1024,256]{1,0:T(8,128)S(1)}, f32[1024,256]{1,0:T(8,128)}, u32[]{:S(2)}) copy-start(f32[1024,256]{1,0:T(8,128)} %copy-done.14) | copy-start | bytes 3145732
  280.7 38.5 %collective-permute-start.24 = (bf16[512,256]{1,0:T(8,128)(2,1)S(1)}, bf16[512,256]{1,0:T(8,128)(2,1)S(1)}, u32[]{:S(2)}, u32[]{:S(2)}) collective-permute-start(bf16[512,256]{1,0:T(8,128)(2,1)S(1)} %get-tuple-element.142), channel_id=1, source_target_pairs={{0,6},{2,4},{4,2},{6,0},{8,14},{10,12},{12,10},{14,8},{16,22},{18,... | collective-permute-start | bytes 786440 | tf_op jit(solution)/shard_map/ppermute | solution.py:596
  282.0 25.2 %collective-permute-start.29 = (bf16[1024,256]{1,0:T(8,128)(2,1)S(1)}, bf16[1024,256]{1,0:T(8,128)(2,1)S(1)}, u32[]{:S(2)}, u32[]{:S(2)}) collective-permute-start(bf16[1024,256]{1,0:T(8,128)(2,1)S(1)} %get-tuple-element.117), channel_id=1, source_target_pairs={{0,1},{1,0},{2,3},{3,2},{4,5},{5,4},{6,7},{7,6},{8,9},{9,8},{10,11... | collective-permute-start | bytes 1572872 | tf_op jit(solution)/shard_map/ppermute | solution.py:609
  284.5 11.3 %copy-start.27 = (f32[64,9216]{1,0:T(8,128)S(1)}, f32[64,9216]{1,0:T(8,128)}, u32[]{:S(2)}) copy-start(f32[64,9216]{1,0:T(8,128)} %convert_add_fusion) | copy-start | bytes 7077892
  295.3 17.6 %collective-permute-start.32 = (bf16[1024,256]{1,0:T(8,128)(2,1)S(1)}, bf16[1024,256]{1,0:T(8,128)(2,1)S(1)}, u32[]{:S(2)}, u32[]{:S(2)}) collective-permute-start(bf16[1024,256]{1,0:T(8,128)(2,1)S(1)} %get-tuple-element.119), channel_id=1, source_target_pairs={{0,1},{1,0},{2,3},{3,2},{4,5},{5,4},{6,7},{7,6},{8,9},{9,8},{10,11... | collective-permute-start | bytes 1572872 | tf_op jit(solution)/shard_map/ppermute | solution.py:609
  299.3 21.5 %collective-permute-start.36 = (bf16[16,9216]{1,0:T(8,128)(2,1)S(1)}, bf16[16,9216]{1,0:T(8,128)(2,1)S(1)}, u32[]{:S(2)}, u32[]{:S(2)}) collective-permute-start(bf16[16,9216]{1,0:T(8,128)(2,1)S(1)} %get-tuple-element.128), channel_id=1, source_target_pairs={{0,24},{2,26},{4,28},{6,30},{8,16},{10,18},{12,20},{14,22},{16,8},... | collective-permute-start | bytes 884744 | tf_op jit(solution)/shard_map/ppermute | solution.py:467
  302.2 26.8 %collective-permute-start.35 = (bf16[16,9216]{1,0:T(8,128)(2,1)S(1)}, bf16[16,9216]{1,0:T(8,128)(2,1)S(1)}, u32[]{:S(2)}, u32[]{:S(2)}) collective-permute-start(bf16[16,9216]{1,0:T(8,128)(2,1)S(1)} %get-tuple-element.129), channel_id=1, source_target_pairs={{0,16},{2,18},{4,20},{6,22},{8,24},{10,26},{12,28},{14,30},{16,0},... | collective-permute-start | bytes 884744 | tf_op jit(solution)/shard_map/ppermute | solution.py:467
  307.2 22.7 %collective-permute-start.34 = (bf16[16,9216]{1,0:T(8,128)(2,1)S(1)}, bf16[16,9216]{1,0:T(8,128)(2,1)S(1)}, u32[]{:S(2)}, u32[]{:S(2)}) collective-permute-start(bf16[16,9216]{1,0:T(8,128)(2,1)S(1)} %get-tuple-element.127), channel_id=1, source_target_pairs={{0,8},{2,10},{4,12},{6,14},{8,0},{10,2},{12,4},{14,6},{16,24},{18,... | collective-permute-start | bytes 884744 | tf_op jit(solution)/shard_map/ppermute | solution.py:467
  312.9 19.4 %collective-permute-start.25 = (bf16[512,256]{1,0:T(8,128)(2,1)S(1)}, bf16[512,256]{1,0:T(8,128)(2,1)S(1)}, u32[]{:S(2)}, u32[]{:S(2)}) collective-permute-start(bf16[512,256]{1,0:T(8,128)(2,1)S(1)} %get-tuple-element.141), channel_id=1, source_target_pairs={{0,4},{2,6},{4,0},{6,2},{8,12},{10,14},{12,8},{14,10},{16,20},{18,... | collective-permute-start | bytes 786440 | tf_op jit(solution)/shard_map/ppermute | solution.py:596
  319.2 13.1 %collective-permute-start.27 = (bf16[512,256]{1,0:T(8,128)(2,1)S(1)}, bf16[512,256]{1,0:T(8,128)(2,1)S(1)}, u32[]{:S(2)}, u32[]{:S(2)}) collective-permute-start(bf16[512,256]{1,0:T(8,128)(2,1)S(1)} %get-tuple-element.140), channel_id=1, source_target_pairs={{0,2},{2,0},{4,6},{6,4},{8,10},{10,8},{12,14},{14,12},{16,18},{18,... | collective-permute-start | bytes 786440 | tf_op jit(solution)/shard_map/ppermute | solution.py:596
  320.8 11.5 %collective-permute-start.30 = (bf16[512,256]{1,0:T(8,128)(2,1)S(1)}, bf16[512,256]{1,0:T(8,128)(2,1)S(1)}, u32[]{:S(2)}, u32[]{:S(2)}) collective-permute-start(bf16[512,256]{1,0:T(8,128)(2,1)S(1)} %get-tuple-element.138), channel_id=1, source_target_pairs={{0,6},{2,4},{4,2},{6,0},{8,14},{10,12},{12,10},{14,8},{16,22},{18,... | collective-permute-start | bytes 786440 | tf_op jit(solution)/shard_map/ppermute | solution.py:596
  329.0 7.4 %collective-permute-start.31 = (bf16[512,256]{1,0:T(8,128)(2,1)S(1)}, bf16[512,256]{1,0:T(8,128)(2,1)S(1)}, u32[]{:S(2)}, u32[]{:S(2)}) collective-permute-start(bf16[512,256]{1,0:T(8,128)(2,1)S(1)} %get-tuple-element.137), channel_id=1, source_target_pairs={{0,4},{2,6},{4,0},{6,2},{8,12},{10,14},{12,8},{14,10},{16,20},{18,... | collective-permute-start | bytes 786440 | tf_op jit(solution)/shard_map/ppermute | solution.py:596
  329.9 6.5 %collective-permute-start.33 = (bf16[512,256]{1,0:T(8,128)(2,1)S(1)}, bf16[512,256]{1,0:T(8,128)(2,1)S(1)}, u32[]{:S(2)}, u32[]{:S(2)}) collective-permute-start(bf16[512,256]{1,0:T(8,128)(2,1)S(1)} %get-tuple-element.136), channel_id=1, source_target_pairs={{0,2},{2,0},{4,6},{6,4},{8,10},{10,8},{12,14},{14,12},{16,18},{18,... | collective-permute-start | bytes 786440 | tf_op jit(solution)/shard_map/ppermute | solution.py:596
  (3 other events, 3.2 us)
